TPU v7x, 128 devices: a whole 4x4x4 slice. The times are simulated.
128 devices in a mesh: row: 8 (over x, y_lo), col: 16 (over z, y_hi, core).
Axes of the slice: x: 4, y: 4 (y_hi: 2, y_lo: 2; y = y_hi * 2 + y_lo), z: 4, core: 2. Of those that a mesh axis runs over, the one named last changes fastest.
Arguments:
- right_side: float32 [1024, 128], P('row'), may hold values from -6 to 6
- factor_window: float32 [1024, 1024], P('row', 'col'), may hold values from -0.125 to 0.125
- diag_inverse: float32 [1024, 128], P('row'), as said below
- phase_cov: bfloat16 [1024, 65536], P('col', 'row'), may hold values from -0.1875 to 0.1875
Outputs:
- basis: float32 [128, 512, 128], P('row', 'col')
- solved: float32 [1024, 128], P('col')
Inputs may be any that keep to these rules, and one draw needn't show every extreme that they name: `diag_inverse`: each block of 128 rows is a lower triangular matrix with a diagonal between 0.5 and 2.
All inputs are finite; a program needn't handle non-finite values.
Results may differ from a plain program's by a relative error of at most 0.0043.
Values sent between devices are 32-bit elements; how exact they have to be, the bound alone decides.
No kernel may reach another device: no remote copies, remote signals or barrier semaphores. Data moves between devices by JAX's collectives and lax.ppermute only.
A program may use at most 64 MiB of HBM per device.

v0:
```python
import jax
import jax.numpy as jnp
from jax import lax
from jax.sharding import PartitionSpec as P

TILE_ROWS = 512


def from_root(block, axis, owner):
    block = jnp.where(lax.axis_index(axis) == owner, block, jnp.zeros_like(block))
    return lax.psum(block, axis)


def tile_basis(lower, tile):
    return jax.scipy.linalg.solve_triangular(lower, tile.T, lower=True).T


def finish_tiles(gram, tiles):
    lower = jnp.linalg.cholesky(gram)
    return jax.vmap(tile_basis)(lower, tiles)


def local(right_side, factor_window, diag_inverse, phase_cov):
    row_count = lax.axis_size("row")
    col_count = lax.axis_size("col")
    col_index = lax.axis_index("col")
    block_rows = right_side.shape[0]
    rank_width = right_side.shape[1]
    col_width = factor_window.shape[1]
    col_ratio = col_count // row_count
    row_offset = col_index % col_ratio * col_width
    owner_block = col_index // col_ratio
    partial_value = jnp.zeros((block_rows, rank_width), jnp.float32)
    own_solved = jnp.zeros((col_width, rank_width), jnp.float32)
    for block_index in range(row_count):
        summed = lax.psum(partial_value, "col")
        remaining = right_side - summed
        solved_full = jnp.dot(
            diag_inverse,
            remaining,
            precision=lax.Precision.HIGHEST,
            preferred_element_type=jnp.float32,
        )
        received = from_root(solved_full, "row", block_index)
        column_piece = lax.dynamic_slice_in_dim(received, row_offset, col_width, 0)
        owns_block = owner_block == block_index
        own_solved = jnp.where(owns_block, column_piece, own_solved)
        partial_value = lax.cond(
            owns_block,
            lambda running: running
            + jnp.dot(
                factor_window,
                column_piece,
                precision=lax.Precision.HIGHEST,
                preferred_element_type=jnp.float32,
            ),
            lambda running: running,
            partial_value,
        )
    solved_low = own_solved.astype(jnp.bfloat16)
    tile_count = phase_cov.shape[1] // TILE_ROWS
    cov_tiles = phase_cov.reshape(col_width, tile_count, TILE_ROWS)
    shares = lax.psum_scatter(
        jnp.einsum("kts,kr->str", cov_tiles, solved_low, preferred_element_type=jnp.float32),
        "col",
        scatter_dimension=0,
        tiled=True,
    )
    shares = jnp.transpose(shares, (1, 0, 2))
    gram_part = jnp.einsum("tsr,tsq->trq", shares, shares, precision=lax.Precision.HIGHEST)
    gram = lax.psum(gram_part, "col")
    basis = finish_tiles(gram, shares)
    return (basis, own_solved)


def solution(mesh):
    in_specs = (P("row", None), P("row", "col"), P("row", None), P("col", "row"))
    out_specs = (P("row", "col", None), P("col", None))
    return jax.shard_map(local, mesh=mesh, in_specs=in_specs, out_specs=out_specs, check_vma=False)
```

profile of v0, /device:TPU:1, one launch (start us, length us, event | category | flops | bytes accessed | tf_op | source)
XLA Modules:
  0.0 2093.8 jit_solution(3622350053202336708)
XLA Ops:
  7.3 0.8 copy-done
  8.0 1.7 convolution_select_fusion.7
  9.7 0.0 all-reduce.19.cloned.1.call-start
  9.8 71.9 %all-reduce.17.cloned.1.call-done = f32[128,128]{1,0:T(8,128)} async-done(((f32[128,128]{1,0:T(8,128)}), f32[128,128]{1,0:T(8,128)}) %all-reduce.17.cloned.1.call-update) | async-done | bytes 65552 | tf_op jit(solution)/shard_map/psum | solution.py:11
  81.6 0.8 constant_dynamic-slice_fusion.6
  82.5 1.0 conditional.7
  82.5 1.0 fusion.24
  83.5 0.6 copy-done.1
  84.2 0.0 all-reduce.21.cloned.1.call-start
  84.2 130.9 %all-reduce.19.cloned.1.call-done = f32[128,128]{1,0:T(8,128)} async-done(((f32[128,128]{1,0:T(8,128)}), f32[128,128]{1,0:T(8,128)}) %all-reduce.19.cloned.1.call-update) | async-done | bytes 65552 | tf_op jit(solution)/shard_map/psum | solution.py:36
  215.1 1.7 fusion.6
  216.8 0.0 all-reduce.23.cloned.1.call-start
  216.9 67.5 %all-reduce.21.cloned.1.call-done = f32[128,128]{1,0:T(8,128)} async-done(((f32[128,128]{1,0:T(8,128)}), f32[128,128]{1,0:T(8,128)}) %all-reduce.21.cloned.1.call-update) | async-done | bytes 65552 | tf_op jit(solution)/shard_map/psum | solution.py:11
  284.3 0.8 constant_dynamic-slice_fusion.5
  285.1 0.0 all-reduce.25.cloned.1.call-start
  285.2 132.5 %all-reduce.23.cloned.1.call-done = f32[128,128]{1,0:T(8,128)} async-done(((f32[128,128]{1,0:T(8,128)}), f32[128,128]{1,0:T(8,128)}) %all-reduce.23.cloned.1.call-update) | async-done | bytes 65552 | tf_op jit(solution)/shard_map/psum | solution.py:36
  417.7 1.7 fusion.5
  419.4 0.0 all-reduce.27.cloned.1.call-start
  419.4 67.3 %all-reduce.25.cloned.1.call-done = f32[128,128]{1,0:T(8,128)} async-done(((f32[128,128]{1,0:T(8,128)}), f32[128,128]{1,0:T(8,128)}) %all-reduce.25.cloned.1.call-update) | async-done | bytes 65552 | tf_op jit(solution)/shard_map/psum | solution.py:11
  486.8 0.8 constant_dynamic-slice_fusion.4
  487.5 0.0 all-reduce.29.cloned.1.call-start
  487.6 132.5 %all-reduce.27.cloned.1.call-done = f32[128,128]{1,0:T(8,128)} async-done(((f32[128,128]{1,0:T(8,128)}), f32[128,128]{1,0:T(8,128)}) %all-reduce.27.cloned.1.call-update) | async-done | bytes 65552 | tf_op jit(solution)/shard_map/psum | solution.py:36
  620.1 1.7 fusion.4
  621.8 0.0 all-reduce.31.cloned.1.call-start
  621.9 67.5 %all-reduce.29.cloned.1.call-done = f32[128,128]{1,0:T(8,128)} async-done(((f32[128,128]{1,0:T(8,128)}), f32[128,128]{1,0:T(8,128)}) %all-reduce.29.cloned.1.call-update) | async-done | bytes 65552 | tf_op jit(solution)/shard_map/psum | solution.py:11
  689.3 0.8 constant_dynamic-slice_fusion.3
  690.1 0.0 all-reduce.33.cloned.1.call-start
  690.2 132.6 %all-reduce.31.cloned.1.call-done = f32[128,128]{1,0:T(8,128)} async-done(((f32[128,128]{1,0:T(8,128)}), f32[128,128]{1,0:T(8,128)}) %all-reduce.31.cloned.1.call-update) | async-done | bytes 65552 | tf_op jit(solution)/shard_map/psum | solution.py:36
  822.8 1.7 fusion.3
  824.5 0.0 all-reduce.35.cloned.1.call-start
  824.5 67.5 %all-reduce.33.cloned.1.call-done = f32[128,128]{1,0:T(8,128)} async-done(((f32[128,128]{1,0:T(8,128)}), f32[128,128]{1,0:T(8,128)}) %all-reduce.33.cloned.1.call-update) | async-done | bytes 65552 | tf_op jit(solution)/shard_map/psum | solution.py:11
  892.0 0.8 constant_dynamic-slice_fusion.2
  892.8 0.0 all-reduce.37.cloned.1.call-start
  892.9 132.5 %all-reduce.35.cloned.1.call-done = f32[128,128]{1,0:T(8,128)} async-done(((f32[128,128]{1,0:T(8,128)}), f32[128,128]{1,0:T(8,128)}) %all-reduce.35.cloned.1.call-update) | async-done | bytes 65552 | tf_op jit(solution)/shard_map/psum | solution.py:36
  1025.3 1.7 fusion.2
  1027.0 0.0 all-reduce.39.cloned.1.call-start
  1027.1 67.5 %all-reduce.37.cloned.1.call-done = f32[128,128]{1,0:T(8,128)} async-done(((f32[128,128]{1,0:T(8,128)}), f32[128,128]{1,0:T(8,128)}) %all-reduce.37.cloned.1.call-update) | async-done | bytes 65552 | tf_op jit(solution)/shard_map/psum | solution.py:11
  1094.6 0.8 constant_dynamic-slice_fusion.1
  1095.4 0.0 all-reduce.41.cloned.1.call-start
  1095.4 132.5 %all-reduce.39.cloned.1.call-done = f32[128,128]{1,0:T(8,128)} async-done(((f32[128,128]{1,0:T(8,128)}), f32[128,128]{1,0:T(8,128)}) %all-reduce.39.cloned.1.call-update) | async-done | bytes 65552 | tf_op jit(solution)/shard_map/psum | solution.py:36
  1227.9 1.7 fusion.1
  1229.6 0.0 all-reduce.43.cloned.1.call-start
  1229.7 67.5 %all-reduce.41.cloned.1.call-done = f32[128,128]{1,0:T(8,128)} async-done(((f32[128,128]{1,0:T(8,128)}), f32[128,128]{1,0:T(8,128)}) %all-reduce.41.cloned.1.call-update) | async-done | bytes 65552 | tf_op jit(solution)/shard_map/psum | solution.py:11
  1297.1 0.8 constant_dynamic-slice_fusion
  1297.9 0.0 all-reduce.45.cloned.1.call-start
  1298.0 132.5 %all-reduce.43.cloned.1.call-done = f32[128,128]{1,0:T(8,128)} async-done(((f32[128,128]{1,0:T(8,128)}), f32[128,128]{1,0:T(8,128)}) %all-reduce.43.cloned.1.call-update) | async-done | bytes 65552 | tf_op jit(solution)/shard_map/psum | solution.py:36
  1430.4 1.7 fusion
  1432.1 0.0 reduce-scatter.2.cloned.1.call-start
  1432.2 67.9 %all-reduce.45.cloned.1.call-done = f32[128,128]{1,0:T(8,128)} async-done(((f32[128,128]{1,0:T(8,128)}), f32[128,128]{1,0:T(8,128)}) %all-reduce.45.cloned.1.call-update) | async-done | bytes 65552 | tf_op jit(solution)/shard_map/psum | solution.py:11
  1500.1 0.9 select_select_fusion
  1501.0 2.7 convolution_bitcast_fusion
  1503.7 5.5 copy.67
  1509.2 0.2 all-reduce.47.cloned.1.call-start
  1509.4 83.6 %reduce-scatter.2.cloned.1.call-done = f32[32,16,128]{2,1,0:T(8,128)} async-done(((f32[512,16,128]{2,1,0:T(8,128)}), f32[32,16,128]{2,1,0:T(8,128)}) %reduce-scatter.2.cloned.1.call-update) | async-done | bytes 262160 | tf_op jit(solution)/shard_map/reduce_scatter | solution.py:63
  1593.1 3.8 fusion.13
  1597.0 140.5 %all-reduce.47.cloned.1.call-done = f32[16,128,128]{1,2,0:T(8,128)} async-done(((f32[16,128,128]{1,2,0:T(8,128)}), f32[16,128,128]{1,2,0:T(8,128)}) %all-reduce.47.cloned.1.call-update) | async-done | bytes 1048592 | tf_op jit(solution)/shard_map/psum | solution.py:71
  1737.4 1.6 copy.71
  1739.0 1.3 fusion.11
  1740.3 187.5 %custom-call.8 = f32[16,128,128]{2,1,0:T(8,128)S(1)} custom-call(f32[16,128,128]{2,1,0:T(8,128)S(1)} %fusion.11), custom_call_target="Cholesky" | custom-call | tf_op jit(solution)/shard_map/jit(cholesky)/cholesky | solution.py:19
  1927.9 0.1 select_reduce_fusion
  1928.0 0.1 compare_reduce_fusion
  1928.1 0.2 select_bitcast_fusion
  1928.3 157.2 %custom-call.9 = f32[16,1,128,128]{2,3,1,0:T(8,128)S(1)} custom-call(f32[16,1,128,128]{3,2,1,0:T(8,128)S(1)} %select_bitcast_fusion), custom_call_target="InvertDiagBlocksLowerTriangular" | custom-call | tf_op jit(solution)/shard_map/vmap(jit(_solve_triangular))/triangular_solve | solution.py:15
  2085.5 1.8 fusion.9
  (38 shorter events, 0.4 us)
Async XLA Ops:
  7.2 0.8 copy-start
  7.2 1423.3 %copy-start.2 = (f32[128,128]{1,0:T(8,128)S(1)}, f32[128,128]{1,0:T(8,128)}, u32[]{:S(2)}) copy-start(f32[128,128]{1,0:T(8,128)} %param.18) | copy-start | bytes 196612
  7.2 1493.8 %copy-start.3 = (bf16[64,8192]{1,0:T(8,128)(2,1)S(1)}, bf16[64,8192]{1,0:T(8,128)(2,1)}, u32[]{:S(2)}) copy-start(bf16[64,8192]{1,0:T(8,128)(2,1)} %param.21) | copy-start | bytes 3145732
  7.2 74.4 %all-reduce.17.cloned.1.call-start = ((), (), s32[]{:S(2)}) async-start(), calls=%async_computation.1 | async-start | bytes 131072 | tf_op jit(solution)/shard_map/psum | solution.py:11
  9.7 205.4 %all-reduce.19.cloned.1.call-start = ((), (), s32[]{:S(2)}) async-start(), calls=%async_computation.2 | async-start | bytes 131072 | tf_op jit(solution)/shard_map/psum | solution.py:36
  81.6 1418.5 %copy-start.6 = (f32[128,128]{1,0:T(8,128)S(1)}, f32[128,128]{1,0:T(8,128)}, u32[]{:S(2)}) copy-start(f32[128,128]{1,0:T(8,128)} %all-reduce.17.cloned.1.call-done) | copy-start | bytes 196612
  83.5 0.6 copy-start.1
  84.2 200.2 %all-reduce.21.cloned.1.call-start = ((), (), s32[]{:S(2)}) async-start(), calls=%async_computation.3 | async-start | bytes 131072 | tf_op jit(solution)/shard_map/psum | solution.py:11
  216.8 200.8 %all-reduce.23.cloned.1.call-start = ((), (), s32[]{:S(2)}) async-start(), calls=%async_computation.4 | async-start | bytes 131072 | tf_op jit(solution)/shard_map/psum | solution.py:36
  285.1 201.6 %all-reduce.25.cloned.1.call-start = ((), (), s32[]{:S(2)}) async-start(), calls=%async_computation.5 | async-start | bytes 131072 | tf_op jit(solution)/shard_map/psum | solution.py:11
  419.4 200.7 %all-reduce.27.cloned.1.call-start = ((), (), s32[]{:S(2)}) async-start(), calls=%async_computation.6 | async-start | bytes 131072 | tf_op jit(solution)/shard_map/psum | solution.py:36
  487.5 201.8 %all-reduce.29.cloned.1.call-start = ((), (), s32[]{:S(2)}) async-start(), calls=%async_computation.7 | async-start | bytes 131072 | tf_op jit(solution)/shard_map/psum | solution.py:11
  621.8 201.0 %all-reduce.31.cloned.1.call-start = ((), (), s32[]{:S(2)}) async-start(), calls=%async_computation.8 | async-start | bytes 131072 | tf_op jit(solution)/shard_map/psum | solution.py:36
  690.1 201.9 %all-reduce.33.cloned.1.call-start = ((), (), s32[]{:S(2)}) async-start(), calls=%async_computation.9 | async-start | bytes 131072 | tf_op jit(solution)/shard_map/psum | solution.py:11
  824.5 200.8 %all-reduce.35.cloned.1.call-start = ((), (), s32[]{:S(2)}) async-start(), calls=%async_computation.10 | async-start | bytes 131072 | tf_op jit(solution)/shard_map/psum | solution.py:36
  892.8 201.8 %all-reduce.37.cloned.1.call-start = ((), (), s32[]{:S(2)}) async-start(), calls=%async_computation.11 | async-start | bytes 131072 | tf_op jit(solution)/shard_map/psum | solution.py:11
  1027.0 200.8 %all-reduce.39.cloned.1.call-start = ((), (), s32[]{:S(2)}) async-start(), calls=%async_computation.12 | async-start | bytes 131072 | tf_op jit(solution)/shard_map/psum | solution.py:36
  1095.4 201.8 %all-reduce.41.cloned.1.call-start = ((), (), s32[]{:S(2)}) async-start(), calls=%async_computation.13 | async-start | bytes 131072 | tf_op jit(solution)/shard_map/psum | solution.py:11
  1229.6 200.8 %all-reduce.43.cloned.1.call-start = ((), (), s32[]{:S(2)}) async-start(), calls=%async_computation.14 | async-start | bytes 131072 | tf_op jit(solution)/shard_map/psum | solution.py:36
  1297.9 202.2 %all-reduce.45.cloned.1.call-start = ((), (), s32[]{:S(2)}) async-start(), calls=%async_computation.15 | async-start | bytes 131072 | tf_op jit(solution)/shard_map/psum | solution.py:11
  1432.1 160.9 %reduce-scatter.2.cloned.1.call-start = ((), (), s32[]{:S(2)}) async-start(), calls=%async_computation.16 | async-start | bytes 4456448 | tf_op jit(solution)/shard_map/reduce_scatter | solution.py:63
  1501.0 8.2 copy-start.5
  1509.2 228.2 %all-reduce.47.cloned.1.call-start = ((), (), s32[]{:S(2)}) async-start(), calls=%async_computation.17 | async-start | bytes 2097152 | tf_op jit(solution)/shard_map/psum | solution.py:71
  1597.0 488.5 %copy-start.4 = (f32[32,16,128]{2,1,0:T(8,128)S(1)}, f32[32,16,128]{2,1,0:T(8,128)}, u32[]{:S(2)}) copy-start(f32[32,16,128]{2,1,0:T(8,128)} %reduce-scatter.2.cloned.1.call-done) | copy-start | bytes 786436
Sparse Core Ops, SparseCore 0:
  11.1 70.5 all-reduce.16
  84.8 130.2 all-reduce.18
  217.6 66.7 all-reduce.20
  287.4 130.2 all-reduce.22
  420.0 66.7 all-reduce.24
  489.8 130.2 all-reduce.26
  622.5 66.7 all-reduce.28
  692.5 130.2 all-reduce.30
  825.2 66.7 all-reduce.32
  895.1 130.2 all-reduce.34
  1027.8 66.7 all-reduce.36
  1097.6 130.2 all-reduce.38
  1230.3 66.7 all-reduce.40
  1300.2 130.2 all-reduce.42
  1433.3 66.7 all-reduce.44
  1509.3 83.6 reduce-scatter.1
  1597.0 140.3 all-reduce.46
where the time goes:
time: 2100 us; the launch traced here: 2090 us
  waiting for transfers between devices  1690 us (80%)
  other arithmetic  347 us (17%)
  matrix products  22.9 us (1%)
    psum x7, waiting for transfers between devices, local(): summed = lax.psum(partial_value, 'col')  926 us
    psum x8, waiting for transfers between devices, from_root(): return lax.psum(block, axis)  544 us
    another operation x4, other arithmetic, finish_tiles(): lower = jnp.linalg.cholesky(gram)  188 us
    another operation x3, other arithmetic, tile_basis(): return jax.scipy.linalg.solve_triangular(lower, tile.T, lower=True).T  157 us
    psum x1, waiting for transfers between devices, local(): gram = lax.psum(gram_part, 'col')  140 us
    reduce_scatter x1, waiting for transfers between devices, local(): lax.psum_scatter(jnp.einsum('kts,kr->str', cov_tiles, solved_low, preferr...  83.6 us
  transfers between devices with their start and end apart: 17, of which 17 were waited for; matrix products, arithmetic and copies ran while one was open for 0% of the time, Pallas kernels for 0%

commit v1 on v0

v1 whole, which is shorter than its diff:
```python
import functools

import jax
import jax.numpy as jnp
from jax import lax
from jax.experimental import pallas as pl
from jax.experimental.pallas import tpu as pltpu
from jax.sharding import PartitionSpec as P

TILE_ROWS = 512
PANEL = 32
HIGHEST = lax.Precision.HIGHEST
VMEM_BYTES = 48 * 1024 * 1024


def contract(a, b, da, db):
    return lax.dot_general(a, b, (((da,), (db,)), ((), ())), precision=HIGHEST, preferred_element_type=jnp.float32)


def split(a):
    high = a.astype(jnp.bfloat16)
    return high, (a - high.astype(jnp.float32)).astype(jnp.bfloat16)


def dot3(a, b):
    dot = functools.partial(jnp.dot, preferred_element_type=jnp.float32)
    return dot(a[0], b[0]) + (dot(a[0], b[1]) + dot(a[1], b[0]))


def prepare(col_ref, right_ref, factor_ref, diag_ref, out_ref, scratch):
    diag = diag_ref[...]
    half = factor_ref.shape[1]
    chunk = out_ref.shape[0] - half
    out_ref[:half] = contract(factor_ref[...], diag, 0, 1)
    scratch[...] = contract(right_ref[...], diag, 0, 1)
    out_ref[half:] = scratch[pl.ds(pl.multiple_of(col_ref[0] * chunk, chunk), chunk), :]


def factor_and_invert(work, size):
    rows = lax.broadcasted_iota(jnp.int32, (PANEL, 1), 0)
    for start in range(0, size, PANEL):
        panel = work[start : start + PANEL, :]
        for k in range(PANEL):
            column = panel[:, start + k : start + k + 1]
            scale = lax.rsqrt(column[k : k + 1, :])
            row = panel[k : k + 1, :] * scale
            below = jnp.where(rows > k, column * scale, 0.0)
            panel = jnp.where(rows == k, row, panel - below * row)
        work[start : start + PANEL, :] = panel
        rest = start + PANEL
        if rest < size:
            work[rest:, :] -= contract(panel[:, rest:size], panel, 0, 0)


def finish(col_ref, pieces_ref, phase_ref, basis_ref, solved_ref, solved_t, work):
    blocks = solved_t.shape[0]
    size = solved_t.shape[1]
    quarter = size // 4
    current = []
    for i in range(blocks):
        parts = [pieces_ref[core, i * blocks + j, quarter:, :] for j in range(blocks) for core in range(2)]
        current.append(jnp.concatenate(parts, axis=0))
    for j in range(blocks):
        solved_t[j] = current[j]
        if j + 1 == blocks:
            break
        solved_pair = split(current[j])
        for i in range(j + 1, blocks):
            own, other = i * blocks + j, (blocks - 1 - i) * blocks + blocks - 1 - j
            factor = jnp.concatenate([pieces_ref[core, at, :quarter, :] for core in range(2) for at in (own, other)], axis=0)
            current[i] = current[i] - dot3(solved_pair, split(factor))
    col = col_ref[0]
    half = solved_ref.shape[0]
    work[:, :size] = solved_t[col // 2].T
    solved_ref[...] = work[pl.ds(pl.multiple_of(col % 2 * half, half), half), :size]
    low = jnp.concatenate([part.astype(jnp.bfloat16) for part in current], axis=1)
    phase = phase_ref[...].astype(jnp.bfloat16)
    weighted_t = jnp.dot(low, phase, preferred_element_type=jnp.float32)
    weighted = weighted_t.T
    work[:, :size] = contract(weighted_t, weighted_t, 1, 1)
    row_at = lax.broadcasted_iota(jnp.int32, (size, size), 0)
    col_at = lax.broadcasted_iota(jnp.int32, (size, size), 1)
    work[:, size:] = jnp.where(row_at == col_at, 1.0, 0.0)
    factor_and_invert(work, size)
    basis_ref[...] = contract(weighted, work[:, size:], 1, 1)


def local(right_side, factor_window, diag_inverse, phase_cov):
    row_count = lax.axis_size("row")
    col_count = lax.axis_size("col")
    row_index = lax.axis_index("row")
    col_index = lax.axis_index("col")
    block_rows = right_side.shape[0]
    rank_width = right_side.shape[1]
    col_width = factor_window.shape[1]
    chunk = rank_width // col_count
    vmem = pl.BlockSpec(memory_space=pltpu.VMEM)
    smem = pl.BlockSpec(memory_space=pltpu.SMEM)
    params = pltpu.CompilerParams(vmem_limit_bytes=VMEM_BYTES)
    col_scalar = col_index.astype(jnp.int32).reshape(1)
    piece = pl.pallas_call(
        prepare,
        out_shape=jax.ShapeDtypeStruct((col_width + chunk, block_rows), jnp.float32),
        in_specs=[smem, vmem, vmem, vmem],
        out_specs=vmem,
        scratch_shapes=[pltpu.VMEM((rank_width, block_rows), jnp.float32)],
        compiler_params=params,
    )(col_scalar, right_side, factor_window, diag_inverse)
    quarter = col_width // 2
    device = lambda row, col: row * col_count + col
    fold = [
        (device(row, 2 * j + core), device(row_count - 1 - row, 2 * (row_count - 1 - j) + core))
        for row in range(row_count)
        for j in range(row)
        for core in range(2)
    ]
    folded = lax.ppermute(piece[quarter:col_width], ("row", "col"), fold)
    kept = jnp.where(col_index // 2 < row_index, piece[:quarter], folded)
    message = jnp.concatenate([kept, piece[col_width:]], axis=0)
    chips = row_count * col_count // 2
    cores = [[2 * chip + core for chip in range(chips)] for core in range(2)]
    half_pieces = lax.all_to_all(
        jnp.broadcast_to(message[None], (chips,) + message.shape), ("row", "col"), 0, 0, axis_index_groups=cores, tiled=True
    )
    pairs = [[2 * j, 2 * j + 1] for j in range(col_count // 2)]
    pieces = lax.all_gather(half_pieces, "col", axis_index_groups=pairs)
    tile_count = phase_cov.shape[1] // TILE_ROWS
    cut = jnp.transpose(phase_cov.reshape(col_width, tile_count, TILE_ROWS), (1, 0, 2)).astype(jnp.float32)
    phase = lax.all_to_all(cut, "col", 0, 0, tiled=True).reshape(col_count * col_width, TILE_ROWS)
    basis, solved = pl.pallas_call(
        finish,
        out_shape=[
            jax.ShapeDtypeStruct((TILE_ROWS, rank_width), jnp.float32),
            jax.ShapeDtypeStruct((col_width, rank_width), jnp.float32),
        ],
        in_specs=[smem, vmem, vmem],
        out_specs=[vmem, vmem],
        scratch_shapes=[
            pltpu.VMEM((row_count, rank_width, block_rows), jnp.float32),
            pltpu.VMEM((rank_width, 2 * rank_width), jnp.float32),
        ],
        compiler_params=params,
    )(col_scalar, pieces, phase)
    basis = basis.reshape(col_count, TILE_ROWS // col_count, rank_width)
    return (lax.all_to_all(basis, "col", 0, 0, tiled=True), solved)


def solution(mesh):
    in_specs = (P("row", None), P("row", "col"), P("row", None), P("col", "row"))
    out_specs = (P("row", "col", None), P("col", None))
    return jax.shard_map(local, mesh=mesh, in_specs=in_specs, out_specs=out_specs, check_vma=False)
```

time: 2100 us -> 121 us (0.06)
  waiting for transfers between devices: 1690 us -> 0.02 us
  other arithmetic: 347 us -> 0.15 us
  blocking collectives: 0 us -> 85.5 us
  matrix products: 22.9 us -> 0 us
    psum x16 -> x0, waiting for transfers between devices: 1610 us -> none  [the longest x7 926 us: local(): summed = lax.psum(partial_value, 'col')]
    another operation x7 -> x0, other arithmetic: 345 us -> none  [the longest x4 188 us: finish_tiles(): lower = jnp.linalg.cholesky(gram)]
    all_to_all x0 -> x3, blocking collectives: none -> 85.5 us  [the longest x1 39.2 us: local(): lax.all_to_all(jnp.broadcast_to(message[None], (chips,) + message.shape),...]
    reduce_scatter x1 -> x0, waiting for transfers between devices: 83.6 us -> none  [local(): lax.psum_scatter(jnp.einsum('kts,kr->str', cov_tiles, solved_low, preferr...]
    dot_general x11 -> x0, matrix products: 21.1 us -> none  [the longest x8 13.5 us: local(): jnp.dot(diag_inverse, remaining, precision=lax.Precision.HIGHEST, preferr...]
  transfers between devices with their start and end apart: 17 -> 2, of which waited for: 17 -> 0; matrix products, arithmetic and copies ran while one was open for 0% -> 0% of each run, Pallas kernels for 0% -> 0%
where the time goes in v1:
time: 121 us; the launch traced here: 120 us
  blocking collectives  85.5 us (71%)
  Pallas kernels  14.2 us (12%)
  between operations  14.2 us (12%)
  local copies, waits for them, and re-layouts  5.3 us (4%)
    all_to_all x1, blocking collectives, local(): lax.all_to_all(jnp.broadcast_to(message[None], (chips,) + message.shape),...  39.2 us
    all_to_all x1, blocking collectives, local(): lax.all_to_all(cut, 'col', 0, 0, tiled=True)  34 us
    pallas_call x1, Pallas kernels, local(): pl.pallas_call(finish, out_shape=[jax.ShapeDtypeStruct((TILE_ROWS, rank_w...  13.8 us
    all_to_all x1, blocking collectives, local(): return (lax.all_to_all(basis, 'col', 0, 0, tiled=True), solved)  12.3 us
    unnamed x10, local copies, waits for them, and re-layouts  4.97 us
  transfers between devices with their start and end apart: 2, of which 0 were waited for; matrix products, arithmetic and copies ran while one was open for 0% of the time, Pallas kernels for 0%

profile of v1, /device:TPU:1, one launch (start us, length us, event | category | flops | bytes accessed | tf_op | source)
XLA Modules:
  0.0 120.1 jit_solution(14438107305364039630)
XLA Ops:
  7.2 0.0 all-gather.3.cloned.1.call-start
  7.2 0.8 copy.8.factor_ref
  8.1 0.0 copy-start.1
  8.1 0.8 copy-done.1
  8.9 0.0 copy-start.2
  8.9 0.8 copy-done.2
  9.8 0.4 shard_map.59
  10.2 0.7 collective-permute-start
  10.9 0.0 collective-permute-done
  10.9 0.1 broadcast_in_dim.2
  11.0 0.0 copy-start.3
  11.0 39.2 %all_to_all.15 = f32[64,40,128]{2,1,0:T(8,128)} all-to-all(f32[64,40,128]{2,1,0:T(8,128)S(1)} %broadcast_in_dim.2), channel_id=1, replica_groups={{0,2,4,6,8,10,12,14,16,18,20,22,24,26,28,30,32,34,36,38,40,42,44,46,48,..., dimensions={0} | all-to-all | bytes 2621440 | tf_op jit(solution)/shard_map/all_to_all | solution.py:122
  50.2 0.0 all-gather.3.cloned.1.call-update
  50.3 0.0 copy-done.3
  50.3 0.1 convert_element_type.13
  50.4 0.2 copy.12
  50.7 34.0 %all_to_all.16 = f32[16,64,512]{2,1,0:T(8,128)S(1)} all-to-all(f32[16,64,512]{2,1,0:T(8,128)S(1)} %bitcast.14), channel_id=1, replica_groups=mesh['row'=8,'col'=16] {'col'}, dimensions={0} | all-to-all | bytes 4194304 | tf_op jit(solution)/shard_map/all_to_all | solution.py:129
  84.7 0.0 all-gather.3.cloned.1.call-done
  84.7 0.0 copy-start
  84.7 1.7 %copy-done = f32[128,40,128]{2,1,0:T(8,128)S(1)} copy-done((f32[128,40,128]{2,1,0:T(8,128)S(1)}, f32[128,40,128]{2,1,0:T(8,128)}, u32[]{:S(2)}) %copy-start) | copy-done | bytes 2621464
  86.4 13.8 %shard_map.60 = (f32[512,128]{1,0:T(8,128)S(1)}, f32[64,128]{1,0:T(8,128)}) custom-call(s32[1]{0:T(128)} %bitcast.col_ref, f32[2,64,40,128]{3,2,1,0:T(8,128)S(1)} %bitcast.12, f32[1024,512]{1,0:T(8,128)S(1)} %bitcast.11), custom_call_target="tpu_custom_call" | custom-call | tf_op jit(solution)/shard_map/pallas_call | solution.py:130
  100.2 12.3 %all_to_all.17 = f32[16,32,128]{2,1,0:T(8,128)S(1)} all-to-all(f32[16,32,128]{2,1,0:T(8,128)S(1)} %bitcast.13), channel_id=1, replica_groups=mesh['row'=8,'col'=16] {'col'}, dimensions={0} | all-to-all | bytes 524288 | tf_op jit(solution)/shard_map/all_to_all | solution.py:145
  112.5 0.7 copy.14
  (4 shorter events, 0.0 us)
Async XLA Ops:
  7.2 77.5 %all-gather.3.cloned.1.call-start = ((), (), s32[]{:S(2)}) async-start(), calls=%async_computation.3 | async-start | bytes 3932160 | tf_op jit(solution)/shard_map/all_gather | solution.py:126
  8.1 0.8 copy-start.1
  8.9 0.8 copy-start.2
  10.2 0.7 collective-permute-start
  11.0 39.3 %copy-start.3 = (bf16[64,8192]{1,0:T(8,128)(2,1)S(1)}, bf16[64,8192]{1,0:T(8,128)(2,1)}, u32[]{:S(2)}) copy-start(bf16[64,8192]{1,0:T(8,128)(2,1)} %param.7) | copy-start | bytes 3145732
  84.7 1.7 %copy-start = (f32[128,40,128]{2,1,0:T(8,128)S(1)}, f32[128,40,128]{2,1,0:T(8,128)}, u32[]{:S(2)}) copy-start(f32[128,40,128]{2,1,0:T(8,128)} %all-gather.3.cloned.1.call-done) | copy-start | bytes 7864324
Sparse Core Ops, SparseCore 0:
  50.4 12.9 all-gather.2

commit v2 on v1

--- a/solution.py
+++ b/solution.py
@@ -52,30 +52,42 @@
             work[rest:, :] -= contract(panel[:, rest:size], panel, 0, 0)
 
 
-def finish(col_ref, pieces_ref, phase_ref, basis_ref, solved_ref, solved_t, work):
-    blocks = solved_t.shape[0]
-    size = solved_t.shape[1]
+def block_solve(place_ref, own_ref, other_ref, low_ref, solved_ref, solved_t, work):
+    turns, planes, rows, size = own_ref.shape
+    blocks = turns * 2
     quarter = size // 4
+    col, turn = place_ref[0], place_ref[1]
+    core = col % 2
+
+    def piece(block_row, block_col, half, start, stop):
+        slot = (turn - block_row // 2 + turns) % turns
+        at = block_row % 2 * blocks + block_col
+        own, other = own_ref[slot, at, start:stop, :], other_ref[slot, at, start:stop, :]
+        return jnp.where(core == half, own, other)
+
     current = []
     for i in range(blocks):
-        parts = [pieces_ref[core, i * blocks + j, quarter:, :] for j in range(blocks) for core in range(2)]
+        parts = [piece(i, j, half, quarter, rows) for j in range(blocks) for half in range(2)]
         current.append(jnp.concatenate(parts, axis=0))
     for j in range(blocks):
         solved_t[j] = current[j]
+        low_ref[:, j * size : (j + 1) * size] = current[j].astype(jnp.bfloat16)
         if j + 1 == blocks:
             break
         solved_pair = split(current[j])
         for i in range(j + 1, blocks):
-            own, other = i * blocks + j, (blocks - 1 - i) * blocks + blocks - 1 - j
-            factor = jnp.concatenate([pieces_ref[core, at, :quarter, :] for core in range(2) for at in (own, other)], axis=0)
-            current[i] = current[i] - dot3(solved_pair, split(factor))
-    col = col_ref[0]
-    half = solved_ref.shape[0]
-    work[:, :size] = solved_t[col // 2].T
-    solved_ref[...] = work[pl.ds(pl.multiple_of(col % 2 * half, half), half), :size]
-    low = jnp.concatenate([part.astype(jnp.bfloat16) for part in current], axis=1)
+            places = ((i, j), (blocks - 1 - i, blocks - 1 - j))
+            parts = [piece(*at, half, 0, quarter) for half in range(2) for at in places]
+            current[i] = current[i] - dot3(solved_pair, split(jnp.concatenate(parts, axis=0)))
+    half_rows = solved_ref.shape[0]
+    work[...] = solved_t[col // 2].T
+    solved_ref[...] = work[pl.ds(pl.multiple_of(core * half_rows, half_rows), half_rows), :]
+
+
+def tile_basis(low_ref, phase_ref, basis_ref, work):
+    size = low_ref.shape[0]
     phase = phase_ref[...].astype(jnp.bfloat16)
-    weighted_t = jnp.dot(low, phase, preferred_element_type=jnp.float32)
+    weighted_t = jnp.dot(low_ref[...], phase, preferred_element_type=jnp.float32)
     weighted = weighted_t.T
     work[:, :size] = contract(weighted_t, weighted_t, 1, 1)
     row_at = lax.broadcasted_iota(jnp.int32, (size, size), 0)
@@ -94,10 +106,12 @@
     rank_width = right_side.shape[1]
     col_width = factor_window.shape[1]
     chunk = rank_width // col_count
+    turns = row_count // 2
+    blocks = col_count // 2
     vmem = pl.BlockSpec(memory_space=pltpu.VMEM)
     smem = pl.BlockSpec(memory_space=pltpu.SMEM)
     params = pltpu.CompilerParams(vmem_limit_bytes=VMEM_BYTES)
-    col_scalar = col_index.astype(jnp.int32).reshape(1)
+    place = jnp.stack([col_index, row_index // 2]).astype(jnp.int32)
     piece = pl.pallas_call(
         prepare,
         out_shape=jax.ShapeDtypeStruct((col_width + chunk, block_rows), jnp.float32),
@@ -105,11 +119,14 @@
         out_specs=vmem,
         scratch_shapes=[pltpu.VMEM((rank_width, block_rows), jnp.float32)],
         compiler_params=params,
-    )(col_scalar, right_side, factor_window, diag_inverse)
+    )(place, right_side, factor_window, diag_inverse)
     quarter = col_width // 2
-    device = lambda row, col: row * col_count + col
+
+    def device(row, col):
+        return row * col_count + col
+
     fold = [
-        (device(row, 2 * j + core), device(row_count - 1 - row, 2 * (row_count - 1 - j) + core))
+        (device(row, 2 * j + core), device(row_count - 1 - row, 2 * (blocks - 1 - j) + core))
         for row in range(row_count)
         for j in range(row)
         for core in range(2)
@@ -117,30 +134,47 @@
     folded = lax.ppermute(piece[quarter:col_width], ("row", "col"), fold)
     kept = jnp.where(col_index // 2 < row_index, piece[:quarter], folded)
     message = jnp.concatenate([kept, piece[col_width:]], axis=0)
-    chips = row_count * col_count // 2
-    cores = [[2 * chip + core for chip in range(chips)] for core in range(2)]
-    half_pieces = lax.all_to_all(
-        jnp.broadcast_to(message[None], (chips,) + message.shape), ("row", "col"), 0, 0, axis_index_groups=cores, tiled=True
-    )
-    pairs = [[2 * j, 2 * j + 1] for j in range(col_count // 2)]
-    pieces = lax.all_gather(half_pieces, "col", axis_index_groups=pairs)
+    planes = [
+        [device(2 * turn + low_bit, 2 * j + core) for low_bit in range(2) for j in range(blocks)]
+        for turn in range(turns)
+        for core in range(2)
+    ]
+    copies = jnp.broadcast_to(message[None], (2 * blocks,) + message.shape)
+    plane = lax.all_to_all(copies, ("row", "col"), 0, 0, axis_index_groups=planes, tiled=True)
     tile_count = phase_cov.shape[1] // TILE_ROWS
     cut = jnp.transpose(phase_cov.reshape(col_width, tile_count, TILE_ROWS), (1, 0, 2)).astype(jnp.float32)
+    plane, cut = lax.optimization_barrier((plane, cut))
     phase = lax.all_to_all(cut, "col", 0, 0, tiled=True).reshape(col_count * col_width, TILE_ROWS)
-    basis, solved = pl.pallas_call(
-        finish,
+    slots = [plane]
+    for step in range(1, turns):
+        turn_on = [(2 * turn + bit, 2 * ((turn + step) % turns) + bit) for turn in range(turns) for bit in range(2)]
+        slots.append(lax.ppermute(plane, "row", turn_on))
+    own = jnp.stack(slots)
+    other = lax.ppermute(own, "col", [(col, col ^ 1) for col in range(col_count)])
+    low, solved = pl.pallas_call(
+        block_solve,
         out_shape=[
-            jax.ShapeDtypeStruct((TILE_ROWS, rank_width), jnp.float32),
+            jax.ShapeDtypeStruct((rank_width, row_count * block_rows), jnp.bfloat16),
             jax.ShapeDtypeStruct((col_width, rank_width), jnp.float32),
         ],
         in_specs=[smem, vmem, vmem],
         out_specs=[vmem, vmem],
         scratch_shapes=[
             pltpu.VMEM((row_count, rank_width, block_rows), jnp.float32),
-            pltpu.VMEM((rank_width, 2 * rank_width), jnp.float32),
+            pltpu.VMEM((rank_width, block_rows), jnp.float32),
         ],
         compiler_params=params,
-    )(col_scalar, pieces, phase)
+        cost_estimate=pl.CostEstimate(flops=800_000_000, bytes_accessed=3_000_000, transcendentals=0),
+    )(place, own, other)
+    basis = pl.pallas_call(
+        tile_basis,
+        out_shape=jax.ShapeDtypeStruct((TILE_ROWS, rank_width), jnp.float32),
+        in_specs=[vmem, vmem],
+        out_specs=vmem,
+        scratch_shapes=[pltpu.VMEM((rank_width, 2 * rank_width), jnp.float32)],
+        compiler_params=params,
+        cost_estimate=pl.CostEstimate(flops=1_000_000_000, bytes_accessed=3_000_000, transcendentals=0),
+    )(low, phase)
     basis = basis.reshape(col_count, TILE_ROWS // col_count, rank_width)
     return (lax.all_to_all(basis, "col", 0, 0, tiled=True), solved)
 

time: 121 us -> 93 us (0.77)
  blocking collectives: 85.5 us -> 12.6 us
  waiting for transfers between devices: 0.02 us -> 29.3 us
  starting transfers between devices: 0.7 us -> 27.8 us
  between operations: 14.2 us -> 0.77 us
  Pallas kernels: 14.2 us -> 16.2 us
    all_to_all x2 -> x0, blocking collectives: 73.2 us -> none  [the longest x1 39.2 us: local(): lax.all_to_all(jnp.broadcast_to(message[None], (chips,) + message.shape),...]
    all_to_all x0 -> x2, starting transfers between devices: none -> 24.1 us  [the longest x1 17.6 us: local(): lax.all_to_all(copies, ('row', 'col'), 0, 0, axis_index_groups=planes, ti...]
    ppermute x0 -> x4, waiting for transfers between devices: none -> 19.9 us  [the longest x3 17.2 us: local(): slots.append(lax.ppermute(plane, 'row', turn_on))]
    all_to_all x0 -> x2, waiting for transfers between devices: none -> 9.39 us  [the longest x1 6.26 us: local(): lax.all_to_all(copies, ('row', 'col'), 0, 0, axis_index_groups=planes, ti...]
    ppermute x0 -> x4, starting transfers between devices: none -> 2.96 us  [the longest x3 2.39 us: local(): slots.append(lax.ppermute(plane, 'row', turn_on))]
    unnamed x10 -> x8, local copies, waits for them, and re-layouts: 4.97 us -> 3.23 us
    pallas_call x1 -> x2, Pallas kernels: 13.8 us -> 15.3 us  [the longest x1 12.8 us: local(): pl.pallas_call(tile_basis, out_shape=jax.ShapeDtypeStruct((TILE_ROWS, ran...]
    convert_element_type x1, local copies, waits for them, and re-layouts: 0.23 us -> 1.54 us  [local(): jnp.transpose(phase_cov.reshape(col_width, tile_count, TILE_ROWS), (1, 0,...]
  transfers between devices with their start and end apart: 2 -> 7, of which waited for: 0 -> 6; matrix products, arithmetic and copies ran while one was open for 0% -> 2% of each run, Pallas kernels for 0% -> 3%
where the time goes in v2:
time: 93 us; the launch traced here: 92.5 us
  waiting for transfers between devices  29.3 us (32%)
  starting transfers between devices  27.8 us (30%)
  Pallas kernels  16.2 us (17%)
  blocking collectives  12.6 us (14%)
  local copies, waits for them, and re-layouts  5.54 us (6%)
    all_to_all x1, starting transfers between devices, local(): lax.all_to_all(copies, ('row', 'col'), 0, 0, axis_index_groups=planes, ti...  17.6 us
    ppermute x3, waiting for transfers between devices, local(): slots.append(lax.ppermute(plane, 'row', turn_on))  17.2 us
    pallas_call x1, Pallas kernels, local(): pl.pallas_call(tile_basis, out_shape=jax.ShapeDtypeStruct((TILE_ROWS, ran...  12.8 us
    all_to_all x1, blocking collectives, local(): return (lax.all_to_all(basis, 'col', 0, 0, tiled=True), solved)  12.6 us
    all_to_all x1, starting transfers between devices, local(): lax.all_to_all(cut, 'col', 0, 0, tiled=True)  6.54 us
    all_to_all x1, waiting for transfers between devices, local(): lax.all_to_all(copies, ('row', 'col'), 0, 0, axis_index_groups=planes, ti...  6.26 us
    unnamed x8, local copies, waits for them, and re-layouts  3.23 us
    all_to_all x1, waiting for transfers between devices, local(): lax.all_to_all(cut, 'col', 0, 0, tiled=True)  3.12 us
  transfers between devices with their start and end apart: 7, of which 6 were waited for; matrix products, arithmetic and copies ran while one was open for 2% of the time, Pallas kernels for 3%

profile of v2, /device:TPU:1, one launch (start us, length us, event | category | flops | bytes accessed | tf_op | source)
XLA Modules:
  0.0 92.5 jit_solution(10198874893490595674)
XLA Ops:
  0.6 0.8 copy.6.factor_ref
  1.5 0.1 pad_add_fusion.col_ref.place_ref
  1.6 0.0 copy-start
  1.6 0.8 copy-done
  2.4 0.0 copy-start.1
  2.4 0.8 copy-done.1
  3.3 0.0 copy-start.2
  3.3 0.9 %shard_map.59 = f32[72,128]{1,0:T(8,128)S(1)} custom-call(s32[2]{0:T(128)S(1)} %pad_add_fusion.col_ref.place_ref, f32[128,128]{1,0:T(8,128)S(1)} %copy-done, f32[128,64]{1,0:T(8,128)S(1)} %copy.6.factor_ref, f32[128,128]{1,0:T(8,128)S(1)} %copy-done.1), custom_call_target="tpu_custom_call" | custom-call | tf_op jit(solution)/shard_map/pallas_call | solution.py:115
  4.2 0.7 collective-permute-start
  4.9 0.0 collective-permute-done
  5.0 0.8 broadcast_in_dim.2
  5.7 17.6 %all-to-all-start = ((f32[16,40,128]{2,1,0:T(8,128)}), f32[16,40,128]{2,1,0:T(8,128)S(1)}, u32[]{:S(2)}, u32[]{:S(2)}) async-start(f32[16,40,128]{2,1,0:T(8,128)} %broadcast_in_dim.2), calls=%async_computation | async-start | bytes 655360 | tf_op jit(solution)/shard_map/all_to_all | solution.py:143
  23.3 0.0 copy-done.2
  23.3 0.1 convert_element_type.13
  23.5 1.5 %copy.10 = f32[8,16,8,512]{3,2,0,1:T(8,128)} copy(f32[8,16,8,512]{3,2,1,0:T(8,128)S(1)} %bitcast.18) | data formatting | bytes 4194304 | tf_op jit(solution)/shard_map/convert_element_type | solution.py:145
  25.0 6.3 %all-to-all-done = f32[16,40,128]{2,1,0:T(8,128)S(1)} async-done(((f32[16,40,128]{2,1,0:T(8,128)}), f32[16,40,128]{2,1,0:T(8,128)S(1)}, u32[]{:S(2)}, u32[]{:S(2)}) %all-to-all-start) | async-done | bytes 327712 | tf_op jit(solution)/shard_map/all_to_all | solution.py:143
  31.3 6.5 %all-to-all-start.1 = ((f32[16,64,512]{2,1,0:T(8,128)}), f32[16,64,512]{2,1,0:T(8,128)S(1)}, u32[]{:S(2)}, u32[]{:S(2)}) async-start(f32[16,64,512]{2,1,0:T(8,128)} %bitcast.17), calls=%async_computation.1 | async-start | bytes 4194304 | tf_op jit(solution)/shard_map/all_to_all | solution.py:147
  37.8 1.5 %collective-permute-start.3 = (f32[16,40,128]{2,1,0:T(8,128)S(1)}, f32[16,40,128]{2,1,0:T(8,128)S(1)}, u32[]{:S(2)}, u32[]{:S(2)}) collective-permute-start(f32[16,40,128]{2,1,0:T(8,128)S(1)} %all-to-all-done), channel_id=1, source_target_pairs={{0,96},{16,112},{32,0},{48,16},{64,32},{80,48},{96,64},{112,80},{1... | collective-permute-start | bytes 983048 | tf_op jit(solution)/shard_map/ppermute | solution.py:151
  39.3 0.3 collective-permute-start.2
  39.6 0.6 collective-permute-start.1
  40.2 6.6 %collective-permute-done.3 = f32[16,40,128]{2,1,0:T(8,128)S(1)} collective-permute-done((f32[16,40,128]{2,1,0:T(8,128)S(1)}, f32[16,40,128]{2,1,0:T(8,128)S(1)}, u32[]{:S(2)}, u32[]{:S(2)}) %collective-permute-start.3) | collective-permute-done | bytes 327712 | tf_op jit(solution)/shard_map/ppermute | solution.py:151
  46.9 2.7 %collective-permute-done.2 = f32[16,40,128]{2,1,0:T(8,128)S(1)} collective-permute-done((f32[16,40,128]{2,1,0:T(8,128)S(1)}, f32[16,40,128]{2,1,0:T(8,128)S(1)}, u32[]{:S(2)}, u32[]{:S(2)}) %collective-permute-start.2) | collective-permute-done | bytes 327712 | tf_op jit(solution)/shard_map/ppermute | solution.py:151
  49.5 7.9 %collective-permute-done.1 = f32[16,40,128]{2,1,0:T(8,128)S(1)} collective-permute-done((f32[16,40,128]{2,1,0:T(8,128)S(1)}, f32[16,40,128]{2,1,0:T(8,128)S(1)}, u32[]{:S(2)}, u32[]{:S(2)}) %collective-permute-start.1) | collective-permute-done | bytes 327712 | tf_op jit(solution)/shard_map/ppermute | solution.py:151
  57.4 0.1 pad_maximum_fusion.own_ref
  57.5 0.6 collective-permute-start.4
  58.1 2.7 %collective-permute-done.4.other_ref = f32[4,16,40,128]{3,2,1,0:T(8,128)S(1)} collective-permute-done((f32[4,16,40,128]{3,2,1,0:T(8,128)S(1)}, f32[4,16,40,128]{3,2,1,0:T(8,128)S(1)}, u32[]{:S(2)}, u32[]{:S(2)}) %collective-permute-start.4) | collective-permute-done | bytes 1310752 | tf_op jit(solution)/shard_map/ppermute | solution.py:153
  60.8 2.5 %shard_map.60 = (bf16[128,1024]{1,0:T(8,128)(2,1)S(1)}, f32[64,128]{1,0:T(8,128)}) custom-call(s32[2]{0:T(128)S(1)} %pad_add_fusion.col_ref.place_ref, f32[4,16,40,128]{3,2,1,0:T(8,128)S(1)} %pad_maximum_fusion.own_ref, f32[4,16,40,128]{3,2,1,0:T(8,128)S(1)} %collective-permute-done.4.other_ref), custom_call_target="tpu_custom_call" | custom-call | flops 800000000 | bytes 3000000 | tf_op jit(solution)/shard_map/pallas_call | solution.py:154
  63.3 3.1 %all-to-all-done.1 = f32[16,64,512]{2,1,0:T(8,128)S(1)} async-done(((f32[16,64,512]{2,1,0:T(8,128)}), f32[16,64,512]{2,1,0:T(8,128)S(1)}, u32[]{:S(2)}, u32[]{:S(2)}) %all-to-all-start.1) | async-done | bytes 2097184 | tf_op jit(solution)/shard_map/all_to_all | solution.py:147
  66.4 12.8 %shard_map.61 = f32[512,128]{1,0:T(8,128)S(1)} custom-call(bf16[128,1024]{1,0:T(8,128)(2,1)S(1)} %get-tuple-element.7.low_ref, f32[1024,512]{1,0:T(8,128)S(1)} %bitcast.15), custom_call_target="tpu_custom_call" | custom-call | flops 1000000000 | bytes 3000000 | tf_op jit(solution)/shard_map/pallas_call | solution.py:169
  79.2 12.6 %all_to_all.15 = f32[16,32,128]{2,1,0:T(8,128)S(1)} all-to-all(f32[16,32,128]{2,1,0:T(8,128)S(1)} %bitcast.16), channel_id=1, replica_groups=mesh['row'=8,'col'=16] {'col'}, dimensions={0} | all-to-all | bytes 524288 | tf_op jit(solution)/shard_map/all_to_all | solution.py:179
  91.8 0.7 copy.12
  (4 shorter events, 0.0 us)
Async XLA Ops:
  1.6 0.8 copy-start
  2.4 0.8 copy-start.1
  3.3 20.1 %copy-start.2 = (bf16[64,8192]{1,0:T(8,128)(2,1)S(1)}, bf16[64,8192]{1,0:T(8,128)(2,1)}, u32[]{:S(2)}) copy-start(bf16[64,8192]{1,0:T(8,128)(2,1)} %param.7) | copy-start | bytes 3145732
  4.2 0.7 collective-permute-start
  5.7 25.6 %all-to-all-start = ((f32[16,40,128]{2,1,0:T(8,128)}), f32[16,40,128]{2,1,0:T(8,128)S(1)}, u32[]{:S(2)}, u32[]{:S(2)}) async-start(f32[16,40,128]{2,1,0:T(8,128)} %broadcast_in_dim.2), calls=%async_computation | async-start | bytes 655360 | tf_op jit(solution)/shard_map/all_to_all | solution.py:143
  31.3 35.1 %all-to-all-start.1 = ((f32[16,64,512]{2,1,0:T(8,128)}), f32[16,64,512]{2,1,0:T(8,128)S(1)}, u32[]{:S(2)}, u32[]{:S(2)}) async-start(f32[16,64,512]{2,1,0:T(8,128)} %bitcast.17), calls=%async_computation.1 | async-start | bytes 4194304 | tf_op jit(solution)/shard_map/all_to_all | solution.py:147
  37.8 9.0 %collective-permute-start.3 = (f32[16,40,128]{2,1,0:T(8,128)S(1)}, f32[16,40,128]{2,1,0:T(8,128)S(1)}, u32[]{:S(2)}, u32[]{:S(2)}) collective-permute-start(f32[16,40,128]{2,1,0:T(8,128)S(1)} %all-to-all-done), channel_id=1, source_target_pairs={{0,96},{16,112},{32,0},{48,16},{64,32},{80,48},{96,64},{112,80},{1... | collective-permute-start | bytes 983048 | tf_op jit(solution)/shard_map/ppermute | solution.py:151
  39.3 10.2 %collective-permute-start.2 = (f32[16,40,128]{2,1,0:T(8,128)S(1)}, f32[16,40,128]{2,1,0:T(8,128)S(1)}, u32[]{:S(2)}, u32[]{:S(2)}) collective-permute-start(f32[16,40,128]{2,1,0:T(8,128)S(1)} %all-to-all-done), channel_id=1, source_target_pairs={{0,64},{16,80},{32,96},{48,112},{64,0},{80,16},{96,32},{112,48},{1... | collective-permute-start | bytes 983048 | tf_op jit(solution)/shard_map/ppermute | solution.py:151
  39.6 17.8 %collective-permute-start.1 = (f32[16,40,128]{2,1,0:T(8,128)S(1)}, f32[16,40,128]{2,1,0:T(8,128)S(1)}, u32[]{:S(2)}, u32[]{:S(2)}) collective-permute-start(f32[16,40,128]{2,1,0:T(8,128)S(1)} %all-to-all-done), channel_id=1, source_target_pairs={{0,32},{16,48},{32,64},{48,80},{64,96},{80,112},{96,0},{112,16},{1... | collective-permute-start | bytes 983048 | tf_op jit(solution)/shard_map/ppermute | solution.py:151
  57.5 3.2 %collective-permute-start.4 = (f32[4,16,40,128]{3,2,1,0:T(8,128)S(1)}, f32[4,16,40,128]{3,2,1,0:T(8,128)S(1)}, u32[]{:S(2)}, u32[]{:S(2)}) collective-permute-start(f32[4,16,40,128]{3,2,1,0:T(8,128)S(1)} %pad_maximum_fusion.own_ref), channel_id=1, source_target_pairs={{0,1},{1,0},{2,3},{3,2},{4,5},{5,4},{6,7},{7,6},{8,9},{9,8},{10,11... | collective-permute-start | bytes 3932168 | tf_op jit(solution)/shard_map/ppermute | solution.py:153

commit v3 on v2

--- a/solution.py
+++ b/solution.py
@@ -29,9 +29,9 @@
 
 def prepare(col_ref, right_ref, factor_ref, diag_ref, out_ref, scratch):
     diag = diag_ref[...]
-    half = factor_ref.shape[1]
+    half = factor_ref.shape[0]
     chunk = out_ref.shape[0] - half
-    out_ref[:half] = contract(factor_ref[...], diag, 0, 1)
+    out_ref[:half] = contract(factor_ref[...], diag, 1, 1)
     scratch[...] = contract(right_ref[...], diag, 0, 1)
     out_ref[half:] = scratch[pl.ds(pl.multiple_of(col_ref[0] * chunk, chunk), chunk), :]
 
@@ -53,16 +53,18 @@
 
 
 def block_solve(place_ref, own_ref, other_ref, low_ref, solved_ref, solved_t, work):
-    turns, planes, rows, size = own_ref.shape
-    blocks = turns * 2
+    rows, size = own_ref.shape[1:]
+    blocks = solved_t.shape[0]
     quarter = size // 4
-    col, turn = place_ref[0], place_ref[1]
+    col, row = place_ref[0], place_ref[1]
     core = col % 2
+    turn, ring, level = row // 2, col // 2 % 2 * 2 + row % 2, col // 4
 
     def piece(block_row, block_col, half, start, stop):
-        slot = (turn - block_row // 2 + turns) % turns
-        at = block_row % 2 * blocks + block_col
-        own, other = own_ref[slot, at, start:stop, :], other_ref[slot, at, start:stop, :]
+        steps = [(block_row // 2, turn), (block_col % 2 * 2 + block_row % 2, ring), (block_col // 2, level)]
+        far = [jnp.bitwise_xor(here, there) for there, here in steps]
+        at = far[0] * 16 + far[1] * 4 + far[2]
+        own, other = own_ref[at, start:stop, :], other_ref[at, start:stop, :]
         return jnp.where(core == half, own, other)
 
     current = []
@@ -106,12 +108,11 @@
     rank_width = right_side.shape[1]
     col_width = factor_window.shape[1]
     chunk = rank_width // col_count
-    turns = row_count // 2
     blocks = col_count // 2
     vmem = pl.BlockSpec(memory_space=pltpu.VMEM)
     smem = pl.BlockSpec(memory_space=pltpu.SMEM)
     params = pltpu.CompilerParams(vmem_limit_bytes=VMEM_BYTES)
-    place = jnp.stack([col_index, row_index // 2]).astype(jnp.int32)
+    place = jnp.stack([col_index, row_index]).astype(jnp.int32)
     piece = pl.pallas_call(
         prepare,
         out_shape=jax.ShapeDtypeStruct((col_width + chunk, block_rows), jnp.float32),
@@ -119,7 +120,7 @@
         out_specs=vmem,
         scratch_shapes=[pltpu.VMEM((rank_width, block_rows), jnp.float32)],
         compiler_params=params,
-    )(place, right_side, factor_window, diag_inverse)
+    )(place, right_side, factor_window.T, diag_inverse)
     quarter = col_width // 2
 
     def device(row, col):
@@ -134,22 +135,18 @@
     folded = lax.ppermute(piece[quarter:col_width], ("row", "col"), fold)
     kept = jnp.where(col_index // 2 < row_index, piece[:quarter], folded)
     message = jnp.concatenate([kept, piece[col_width:]], axis=0)
-    planes = [
-        [device(2 * turn + low_bit, 2 * j + core) for low_bit in range(2) for j in range(blocks)]
-        for turn in range(turns)
-        for core in range(2)
-    ]
-    copies = jnp.broadcast_to(message[None], (2 * blocks,) + message.shape)
-    plane = lax.all_to_all(copies, ("row", "col"), 0, 0, axis_index_groups=planes, tiled=True)
     tile_count = phase_cov.shape[1] // TILE_ROWS
     cut = jnp.transpose(phase_cov.reshape(col_width, tile_count, TILE_ROWS), (1, 0, 2)).astype(jnp.float32)
-    plane, cut = lax.optimization_barrier((plane, cut))
     phase = lax.all_to_all(cut, "col", 0, 0, tiled=True).reshape(col_count * col_width, TILE_ROWS)
-    slots = [plane]
-    for step in range(1, turns):
-        turn_on = [(2 * turn + bit, 2 * ((turn + step) % turns) + bit) for turn in range(turns) for bit in range(2)]
-        slots.append(lax.ppermute(plane, "row", turn_on))
-    own = jnp.stack(slots)
+    by_level = [[(device(row, col), device(row, col ^ 4 * mask)) for row in range(row_count) for col in range(col_count)] for mask in range(1, 4)]
+    by_ring = [
+        [(device(row, col), device(row ^ mask % 2, col ^ mask // 2 * 2)) for row in range(row_count) for col in range(col_count)]
+        for mask in range(1, 4)
+    ]
+    by_turn = [[(device(row, col), device(row ^ 2 * mask, col)) for row in range(row_count) for col in range(col_count)] for mask in range(1, 4)]
+    own = message[None]
+    for routes in (by_level, by_ring, by_turn):
+        own = jnp.concatenate([own] + [lax.ppermute(own, ("row", "col"), route) for route in routes], axis=0)
     other = lax.ppermute(own, "col", [(col, col ^ 1) for col in range(col_count)])
     low, solved = pl.pallas_call(
         block_solve,

time: 93 us -> 99.6 us (1.071)
  starting transfers between devices: 27.8 us -> 33.4 us
  local copies, waits for them, and re-layouts: 5.54 us -> 11.1 us
  waiting for transfers between devices: 29.3 us -> 24.3 us
    ppermute x3 -> x9, starting transfers between devices: 2.39 us -> 21.9 us  [local(): lax.ppermute(own, ('row', 'col'), route)]
    all_to_all x1 -> x0, starting transfers between devices: 17.6 us -> none  [local(): lax.all_to_all(copies, ('row', 'col'), 0, 0, axis_index_groups=planes, ti...]
    all_to_all x1 -> x0, waiting for transfers between devices: 6.26 us -> none  [local(): lax.all_to_all(copies, ('row', 'col'), 0, 0, axis_index_groups=planes, ti...]
    unnamed x8 -> x20, local copies, waits for them, and re-layouts: 3.23 us -> 8.9 us
    all_to_all x1, starting transfers between devices: 6.54 us -> 10.4 us  [local(): lax.all_to_all(cut, 'col', 0, 0, tiled=True)]
    ppermute x3 -> x9, waiting for transfers between devices: 17.2 us -> 18 us  [local(): lax.ppermute(own, ('row', 'col'), route)]
  transfers between devices with their start and end apart: 7 -> 12, of which waited for: 6 -> 7; matrix products, arithmetic and copies ran while one was open for 2% -> 6% of each run, Pallas kernels for 3% -> 3%
where the time goes in v3:
time: 99.6 us; the launch traced here: 99.2 us
  starting transfers between devices  33.4 us (34%)
  waiting for transfers between devices  24.3 us (24%)
  Pallas kernels  16.2 us (16%)
  blocking collectives  12.5 us (13%)
  local copies, waits for them, and re-layouts  11.1 us (11%)
    ppermute x9, starting transfers between devices, local(): lax.ppermute(own, ('row', 'col'), route)  21.9 us
    ppermute x9, waiting for transfers between devices, local(): lax.ppermute(own, ('row', 'col'), route)  18 us
    pallas_call x1, Pallas kernels, local(): pl.pallas_call(tile_basis, out_shape=jax.ShapeDtypeStruct((TILE_ROWS, ran...  12.8 us
    all_to_all x1, blocking collectives, local(): return (lax.all_to_all(basis, 'col', 0, 0, tiled=True), solved)  12.5 us
    all_to_all x1, starting transfers between devices, local(): lax.all_to_all(cut, 'col', 0, 0, tiled=True)  10.4 us
    unnamed x20, local copies, waits for them, and re-layouts  8.9 us
    all_to_all x1, waiting for transfers between devices, local(): lax.all_to_all(cut, 'col', 0, 0, tiled=True)  3.63 us
    ppermute x1, waiting for transfers between devices, local(): lax.ppermute(own, 'col', [(col, col ^ 1) for col in range(col_count)])  2.66 us
  transfers between devices with their start and end apart: 12, of which 7 were waited for; matrix products, arithmetic and copies ran while one was open for 6% of the time, Pallas kernels for 3%

profile of v3, /device:TPU:1, one launch (start us, length us, event | category | flops | bytes accessed | tf_op | source)
XLA Modules:
  0.0 99.2 jit_solution(6805010704475826902)
XLA Ops:
  0.6 0.1 pad_add_fusion.col_ref.place_ref
  0.7 0.0 copy-start
  0.7 0.8 copy-done
  1.6 0.0 copy-start.1
  1.6 0.8 copy-done.1
  2.4 0.0 copy-start.2
  2.4 0.8 copy-done.2
  3.1 0.0 copy-start.5
  3.2 0.9 shard_map.59
  4.1 0.7 collective-permute-start
  4.8 0.0 collective-permute-done
  4.8 13.8 %collective-permute-start.3 = (f32[1,40,128]{2,1,0:T(8,128)S(1)}, f32[1,40,128]{2,1,0:T(8,128)S(1)}, u32[]{:S(2)}, u32[]{:S(2)}) collective-permute-start(f32[1,40,128]{2,1,0:T(8,128)S(1)} %maximum_bitcast_fusion), channel_id=1, source_target_pairs={{0,12},{1,13},{2,14},{3,15},{4,8},{5,9},{6,10},{7,11},{8,4},{9,5},... | collective-permute-start | bytes 61448 | tf_op jit(solution)/shard_map/ppermute | solution.py:149
  18.7 0.0 collective-permute-start.2
  18.7 0.7 collective-permute-start.1
  19.3 0.6 constant_dynamic-update-slice_fusion.6
  19.9 0.0 collective-permute-done.3
  19.9 2.9 %collective-permute-done.2 = f32[1,40,128]{2,1,0:T(8,128)S(1)} collective-permute-done((f32[1,40,128]{2,1,0:T(8,128)S(1)}, f32[1,40,128]{2,1,0:T(8,128)S(1)}, u32[]{:S(2)}, u32[]{:S(2)}) %collective-permute-start.2) | collective-permute-done | bytes 20512 | tf_op jit(solution)/shard_map/ppermute | solution.py:149
  22.8 0.0 collective-permute-done.1
  22.8 2.8 %collective-permute-start.6 = (f32[4,40,128]{2,1,0:T(8,128)S(1)}, f32[4,40,128]{2,1,0:T(8,128)S(1)}, u32[]{:S(2)}, u32[]{:S(2)}) collective-permute-start(f32[4,40,128]{2,1,0:T(8,128)S(1)} %pad_maximum_fusion), channel_id=1, source_target_pairs={{0,18},{1,19},{2,16},{3,17},{4,22},{5,23},{6,20},{7,21},{8,26},{9,... | collective-permute-start | bytes 245768 | tf_op jit(solution)/shard_map/ppermute | solution.py:149
  25.6 0.0 collective-permute-start.5
  25.6 0.7 collective-permute-start.4
  26.3 0.6 constant_dynamic-update-slice_fusion.5
  26.9 0.6 constant_dynamic-update-slice_fusion.4
  27.5 0.6 constant_dynamic-update-slice_fusion.3
  28.1 0.9 collective-permute-done.4
  29.0 0.6 constant_dynamic-update-slice_fusion.2
  29.6 0.8 collective-permute-done.5
  30.4 0.6 constant_dynamic-update-slice_fusion.1
  31.1 0.0 collective-permute-done.6
  31.1 0.7 constant_dynamic-update-slice_fusion
  31.7 0.0 collective-permute-start.7
  31.7 0.0 copy-done.5
  31.7 0.1 convert_element_type.13
  31.9 1.5 %copy.9 = f32[8,16,8,512]{3,2,0,1:T(8,128)} copy(f32[8,16,8,512]{3,2,1,0:T(8,128)S(1)} %bitcast.22) | data formatting | bytes 4194304 | tf_op jit(solution)/shard_map/convert_element_type | solution.py:139
  33.4 10.4 %all-to-all-start = ((f32[16,64,512]{2,1,0:T(8,128)}), f32[16,64,512]{2,1,0:T(8,128)S(1)}, u32[]{:S(2)}, u32[]{:S(2)}) async-start(f32[16,64,512]{2,1,0:T(8,128)} %bitcast.21), calls=%async_computation | async-start | bytes 4194304 | tf_op jit(solution)/shard_map/all_to_all | solution.py:140
  43.8 2.0 %collective-permute-start.8 = (f32[16,40,128]{2,1,0:T(8,128)}, f32[16,40,128]{2,1,0:T(8,128)S(1)}, u32[]{:S(2)}, u32[]{:S(2)}) collective-permute-start(f32[16,40,128]{2,1,0:T(8,128)} %get-tuple-element.6), channel_id=1, source_target_pairs={{0,64},{1,65},{2,66},{3,67},{4,68},{5,69},{6,70},{7,71},{8,72},{9,... | collective-permute-start | bytes 983048 | tf_op jit(solution)/shard_map/ppermute | solution.py:149
  45.8 1.8 %collective-permute-start.9 = (f32[16,40,128]{2,1,0:T(8,128)}, f32[16,40,128]{2,1,0:T(8,128)S(1)}, u32[]{:S(2)}, u32[]{:S(2)}) collective-permute-start(f32[16,40,128]{2,1,0:T(8,128)} %get-tuple-element.6), channel_id=1, source_target_pairs={{0,96},{1,97},{2,98},{3,99},{4,100},{5,101},{6,102},{7,103},{8,104... | collective-permute-start | bytes 983048 | tf_op jit(solution)/shard_map/ppermute | solution.py:149
  47.6 0.0 collective-permute-done.7
  47.6 1.0 %constant_dynamic-update-slice_fusion.9 = f32[64,40,128]{2,1,0:T(8,128)S(1)} fusion(f32[64,40,128]{2,1,0:T(8,128)S(1)} %get-tuple-element.7, f32[16,40,128]{2,1,0:T(8,128)} %collective-permute-done.7), kind=kLoop, calls=%fused_computation.11 | loop fusion | bytes 655360
  48.6 6.0 %collective-permute-done.8 = f32[16,40,128]{2,1,0:T(8,128)S(1)} collective-permute-done((f32[16,40,128]{2,1,0:T(8,128)}, f32[16,40,128]{2,1,0:T(8,128)S(1)}, u32[]{:S(2)}, u32[]{:S(2)}) %collective-permute-start.8) | collective-permute-done | bytes 327712 | tf_op jit(solution)/shard_map/ppermute | solution.py:149
  54.7 7.5 %collective-permute-done.9 = f32[16,40,128]{2,1,0:T(8,128)S(1)} collective-permute-done((f32[16,40,128]{2,1,0:T(8,128)}, f32[16,40,128]{2,1,0:T(8,128)S(1)}, u32[]{:S(2)}, u32[]{:S(2)}) %collective-permute-start.9) | collective-permute-done | bytes 327712 | tf_op jit(solution)/shard_map/ppermute | solution.py:149
  62.2 0.6 collective-permute-start.10
  62.8 2.7 %collective-permute-done.10.other_ref = f32[64,40,128]{2,1,0:T(8,128)S(1)} collective-permute-done((f32[64,40,128]{2,1,0:T(8,128)S(1)}, f32[64,40,128]{2,1,0:T(8,128)S(1)}, u32[]{:S(2)}, u32[]{:S(2)}) %collective-permute-start.10) | collective-permute-done | bytes 1310752 | tf_op jit(solution)/shard_map/ppermute | solution.py:150
  65.4 2.5 %shard_map.60 = (bf16[128,1024]{1,0:T(8,128)(2,1)S(1)}, f32[64,128]{1,0:T(8,128)}) custom-call(s32[2]{0:T(128)S(1)} %pad_add_fusion.col_ref.place_ref, f32[64,40,128]{2,1,0:T(8,128)S(1)} %constant_dynamic-update-slice_fusion.7.own_ref, f32[64,40,128]{2,1,0:T(8,128)S(1)} %collective-permute-done.10.other_ref), custom_call_target="tpu_custom_call" | custom-call | flops 800000000 | bytes 3000000 | tf_op jit(solution)/shard_map/pallas_call | solution.py:151
  67.9 0.0 copy-start.3
  67.9 0.7 copy-done.3
  68.6 3.6 %all-to-all-done = f32[16,64,512]{2,1,0:T(8,128)S(1)} async-done(((f32[16,64,512]{2,1,0:T(8,128)}), f32[16,64,512]{2,1,0:T(8,128)S(1)}, u32[]{:S(2)}, u32[]{:S(2)}) %all-to-all-start) | async-done | bytes 2097184 | tf_op jit(solution)/shard_map/all_to_all | solution.py:140
  72.3 0.0 copy-start.4
  72.3 0.9 copy-done.4
  73.2 12.8 %shard_map.61 = f32[512,128]{1,0:T(8,128)S(1)} custom-call(bf16[128,1024]{1,0:T(8,128)(2,1)S(1)} %copy-done.4, f32[1024,512]{1,0:T(8,128)S(1)} %bitcast.18), custom_call_target="tpu_custom_call" | custom-call | flops 1000000000 | bytes 3000000 | tf_op jit(solution)/shard_map/pallas_call | solution.py:166
  86.0 12.5 %all_to_all.10 = f32[16,32,128]{2,1,0:T(8,128)S(1)} all-to-all(f32[16,32,128]{2,1,0:T(8,128)S(1)} %bitcast.19), channel_id=1, replica_groups=mesh['row'=8,'col'=16] {'col'}, dimensions={0} | all-to-all | bytes 524288 | tf_op jit(solution)/shard_map/all_to_all | solution.py:176
  98.5 0.7 copy.26
  (7 shorter events, 0.1 us)
Async XLA Ops:
  0.7 0.8 copy-start
  1.6 0.8 copy-start.1
  2.4 0.8 copy-start.2
  3.1 28.6 %copy-start.5 = (bf16[64,8192]{1,0:T(8,128)(2,1)S(1)}, bf16[64,8192]{1,0:T(8,128)(2,1)}, u32[]{:S(2)}) copy-start(bf16[64,8192]{1,0:T(8,128)(2,1)} %param.7) | copy-start | bytes 3145732
  4.1 0.7 collective-permute-start
  4.8 15.1 %collective-permute-start.3 = (f32[1,40,128]{2,1,0:T(8,128)S(1)}, f32[1,40,128]{2,1,0:T(8,128)S(1)}, u32[]{:S(2)}, u32[]{:S(2)}) collective-permute-start(f32[1,40,128]{2,1,0:T(8,128)S(1)} %maximum_bitcast_fusion), channel_id=1, source_target_pairs={{0,12},{1,13},{2,14},{3,15},{4,8},{5,9},{6,10},{7,11},{8,4},{9,5},... | collective-permute-start | bytes 61448 | tf_op jit(solution)/shard_map/ppermute | solution.py:149
  18.7 4.1 %collective-permute-start.2 = (f32[1,40,128]{2,1,0:T(8,128)S(1)}, f32[1,40,128]{2,1,0:T(8,128)S(1)}, u32[]{:S(2)}, u32[]{:S(2)}) collective-permute-start(f32[1,40,128]{2,1,0:T(8,128)S(1)} %maximum_bitcast_fusion), channel_id=1, source_target_pairs={{0,8},{1,9},{2,10},{3,11},{4,12},{5,13},{6,14},{7,15},{8,0},{9,1},... | collective-permute-start | bytes 61448 | tf_op jit(solution)/shard_map/ppermute | solution.py:149
  18.7 4.1 %collective-permute-start.1 = (f32[1,40,128]{2,1,0:T(8,128)S(1)}, f32[1,40,128]{2,1,0:T(8,128)S(1)}, u32[]{:S(2)}, u32[]{:S(2)}) collective-permute-start(f32[1,40,128]{2,1,0:T(8,128)S(1)} %maximum_bitcast_fusion), channel_id=1, source_target_pairs={{0,4},{1,5},{2,6},{3,7},{4,0},{5,1},{6,2},{7,3},{8,12},{9,13},{10,... | collective-permute-start | bytes 61448 | tf_op jit(solution)/shard_map/ppermute | solution.py:149
  22.8 8.3 %collective-permute-start.6 = (f32[4,40,128]{2,1,0:T(8,128)S(1)}, f32[4,40,128]{2,1,0:T(8,128)S(1)}, u32[]{:S(2)}, u32[]{:S(2)}) collective-permute-start(f32[4,40,128]{2,1,0:T(8,128)S(1)} %pad_maximum_fusion), channel_id=1, source_target_pairs={{0,18},{1,19},{2,16},{3,17},{4,22},{5,23},{6,20},{7,21},{8,26},{9,... | collective-permute-start | bytes 245768 | tf_op jit(solution)/shard_map/ppermute | solution.py:149
  25.6 4.8 %collective-permute-start.5 = (f32[4,40,128]{2,1,0:T(8,128)S(1)}, f32[4,40,128]{2,1,0:T(8,128)S(1)}, u32[]{:S(2)}, u32[]{:S(2)}) collective-permute-start(f32[4,40,128]{2,1,0:T(8,128)S(1)} %pad_maximum_fusion), channel_id=1, source_target_pairs={{0,2},{1,3},{2,0},{3,1},{4,6},{5,7},{6,4},{7,5},{8,10},{9,11},{10,... | collective-permute-start | bytes 245768 | tf_op jit(solution)/shard_map/ppermute | solution.py:149
  25.6 3.4 %collective-permute-start.4 = (f32[4,40,128]{2,1,0:T(8,128)S(1)}, f32[4,40,128]{2,1,0:T(8,128)S(1)}, u32[]{:S(2)}, u32[]{:S(2)}) collective-permute-start(f32[4,40,128]{2,1,0:T(8,128)S(1)} %pad_maximum_fusion), channel_id=1, source_target_pairs={{0,16},{1,17},{2,18},{3,19},{4,20},{5,21},{6,22},{7,23},{8,24},{9,... | collective-permute-start | bytes 245768 | tf_op jit(solution)/shard_map/ppermute | solution.py:149
  31.7 15.9 %collective-permute-start.7 = (f32[16,40,128]{2,1,0:T(8,128)}, f32[16,40,128]{2,1,0:T(8,128)}, u32[]{:S(2)}, u32[]{:S(2)}) collective-permute-start(f32[16,40,128]{2,1,0:T(8,128)} %get-tuple-element.6), channel_id=1, source_target_pairs={{0,32},{1,33},{2,34},{3,35},{4,36},{5,37},{6,38},{7,39},{8,40},{9,... | collective-permute-start | bytes 983048 | tf_op jit(solution)/shard_map/ppermute | solution.py:149
  33.4 38.8 %all-to-all-start = ((f32[16,64,512]{2,1,0:T(8,128)}), f32[16,64,512]{2,1,0:T(8,128)S(1)}, u32[]{:S(2)}, u32[]{:S(2)}) async-start(f32[16,64,512]{2,1,0:T(8,128)} %bitcast.21), calls=%async_computation | async-start | bytes 4194304 | tf_op jit(solution)/shard_map/all_to_all | solution.py:140
  43.8 10.9 %collective-permute-start.8 = (f32[16,40,128]{2,1,0:T(8,128)}, f32[16,40,128]{2,1,0:T(8,128)S(1)}, u32[]{:S(2)}, u32[]{:S(2)}) collective-permute-start(f32[16,40,128]{2,1,0:T(8,128)} %get-tuple-element.6), channel_id=1, source_target_pairs={{0,64},{1,65},{2,66},{3,67},{4,68},{5,69},{6,70},{7,71},{8,72},{9,... | collective-permute-start | bytes 983048 | tf_op jit(solution)/shard_map/ppermute | solution.py:149
  45.8 16.3 %collective-permute-start.9 = (f32[16,40,128]{2,1,0:T(8,128)}, f32[16,40,128]{2,1,0:T(8,128)S(1)}, u32[]{:S(2)}, u32[]{:S(2)}) collective-permute-start(f32[16,40,128]{2,1,0:T(8,128)} %get-tuple-element.6), channel_id=1, source_target_pairs={{0,96},{1,97},{2,98},{3,99},{4,100},{5,101},{6,102},{7,103},{8,104... | collective-permute-start | bytes 983048 | tf_op jit(solution)/shard_map/ppermute | solution.py:149
  62.2 3.2 %collective-permute-start.10 = (f32[64,40,128]{2,1,0:T(8,128)S(1)}, f32[64,40,128]{2,1,0:T(8,128)S(1)}, u32[]{:S(2)}, u32[]{:S(2)}) collective-permute-start(f32[64,40,128]{2,1,0:T(8,128)S(1)} %constant_dynamic-update-slice_fusion.7.own_ref), channel_id=1, source_target_pairs={{0,1},{1,0},{2,3},{3,2},{4,5},{5,4},{6,7},{7,6},{8,9},{9,8},{10,11... | collective-permute-start | bytes 3932168 | tf_op jit(solution)/shard_map/ppermute | solution.py:150
  67.9 0.7 copy-start.3
  72.3 1.0 copy-start.4

commit v4 on v2

--- a/solution.py
+++ b/solution.py
@@ -9,6 +9,7 @@
 
 TILE_ROWS = 512
 PANEL = 32
+SUBLANES = 8
 HIGHEST = lax.Precision.HIGHEST
 VMEM_BYTES = 48 * 1024 * 1024
 
@@ -27,29 +28,72 @@
     return dot(a[0], b[0]) + (dot(a[0], b[1]) + dot(a[1], b[0]))
 
 
-def prepare(col_ref, right_ref, factor_ref, diag_ref, out_ref, scratch):
-    diag = diag_ref[...]
-    half = factor_ref.shape[1]
+def prepare(place_ref, right_hbm, factor_hbm, diag_hbm, out_ref, right, factor, diag, scratch, arrived):
+    sources = ((diag_hbm, diag), (factor_hbm, factor), (right_hbm, right))
+    copies = [pltpu.make_async_copy(source, target, arrived.at[i]) for i, (source, target) in enumerate(sources)]
+    for copy in copies:
+        copy.start()
+    for copy in copies:
+        copy.wait()
+    half = factor.shape[0]
     chunk = out_ref.shape[0] - half
-    out_ref[:half] = contract(factor_ref[...], diag, 0, 1)
-    scratch[...] = contract(right_ref[...], diag, 0, 1)
-    out_ref[half:] = scratch[pl.ds(pl.multiple_of(col_ref[0] * chunk, chunk), chunk), :]
+    out_ref[:half] = contract(factor[...], diag[...], 1, 1)
+    scratch[...] = contract(right[...], diag[...], 0, 1)
+    out_ref[half:] = scratch[pl.ds(pl.multiple_of(place_ref[0] * chunk, chunk), chunk), :]
 
 
 def factor_and_invert(work, size):
-    rows = lax.broadcasted_iota(jnp.int32, (PANEL, 1), 0)
+    shape = (SUBLANES, size)
+    lane = lax.broadcasted_iota(jnp.int32, shape, 1)
+    sublane = lax.broadcasted_iota(jnp.int32, shape, 0)
     for start in range(0, size, PANEL):
-        panel = work[start : start + PANEL, :]
-        for k in range(PANEL):
-            column = panel[:, start + k : start + k + 1]
-            scale = lax.rsqrt(column[k : k + 1, :])
-            row = panel[k : k + 1, :] * scale
-            below = jnp.where(rows > k, column * scale, 0.0)
-            panel = jnp.where(rows == k, row, panel - below * row)
-        work[start : start + PANEL, :] = panel
-        rest = start + PANEL
-        if rest < size:
-            work[rest:, :] -= contract(panel[:, rest:size], panel, 0, 0)
+        end = start + PANEL
+        groups = [work[at : at + SUBLANES, :] for at in range(start, end, SUBLANES)]
+        for g in range(len(groups)):
+            first = start + g * SUBLANES
+            inside = (lane >= first) & (lane < first + SUBLANES)
+            columns = [jnp.broadcast_to(groups[g][:, first + j : first + j + 1], shape) for j in range(SUBLANES)]
+            pivot = {(i, j): jnp.broadcast_to(columns[j][i : i + 1, :], shape) for j in range(SUBLANES) for i in range(j, SUBLANES)}
+            rows, scales = [], []
+            for i in range(SUBLANES):
+                row = jnp.broadcast_to(groups[g][i : i + 1, :], shape)
+                rows.append(jnp.where(inside, jnp.where(lane == first + i, 1.0, 0.0), row))
+            for j in range(SUBLANES):
+                scale = lax.rsqrt(pivot[j, j])
+                scales.append(scale)
+                rows[j] = rows[j] * scale
+                for i in range(j + 1, SUBLANES):
+                    pivot[i, j] = pivot[i, j] * scale
+                for i in range(j + 1, SUBLANES):
+                    for k in range(j + 1, i + 1):
+                        pivot[i, k] = pivot[i, k] - pivot[i, j] * pivot[k, j]
+                    rows[i] = rows[i] - pivot[i, j] * rows[j]
+            merged = rows[0]
+            for i in range(1, SUBLANES):
+                merged = jnp.where(sublane == i, rows[i], merged)
+            groups[g] = merged
+            for h in range(g + 1, len(groups)):
+                left = []
+                rest = jnp.where(inside, 0.0, groups[h])
+                for j in range(SUBLANES):
+                    column = jnp.broadcast_to(groups[h][:, first + j : first + j + 1], shape)
+                    for i in range(j):
+                        column = column - left[i] * pivot[j, i]
+                    left.append(column * scales[j])
+                    rest = rest - left[j] * rows[j]
+                groups[h] = rest
+        panel = jnp.concatenate(groups, axis=0)
+        work[start:end, :] = panel
+        if end < size:
+            row_lane = lax.broadcasted_iota(jnp.int32, (size - end, size), 1)
+            rest = jnp.where((row_lane >= start) & (row_lane < end), 0.0, work[end:, :])
+            panel_lane = lax.broadcasted_iota(jnp.int32, panel.shape, 1)
+            panel_row = lax.broadcasted_iota(jnp.int32, panel.shape, 0) + start
+            known = jnp.where((panel_lane <= panel_row) | (panel_lane >= end), panel, 0.0)
+            work[end:, :] = rest - contract(panel, known, 0, 0)[end:, :]
+    square = (size, size)
+    lower = lax.broadcasted_iota(jnp.int32, square, 1) <= lax.broadcasted_iota(jnp.int32, square, 0)
+    work[...] = jnp.where(lower, work[...], 0.0)
 
 
 def block_solve(place_ref, own_ref, other_ref, low_ref, solved_ref, solved_t, work):
@@ -89,12 +133,9 @@
     phase = phase_ref[...].astype(jnp.bfloat16)
     weighted_t = jnp.dot(low_ref[...], phase, preferred_element_type=jnp.float32)
     weighted = weighted_t.T
-    work[:, :size] = contract(weighted_t, weighted_t, 1, 1)
-    row_at = lax.broadcasted_iota(jnp.int32, (size, size), 0)
-    col_at = lax.broadcasted_iota(jnp.int32, (size, size), 1)
-    work[:, size:] = jnp.where(row_at == col_at, 1.0, 0.0)
+    work[...] = contract(weighted_t, weighted_t, 1, 1)
     factor_and_invert(work, size)
-    basis_ref[...] = contract(weighted, work[:, size:], 1, 1)
+    basis_ref[...] = contract(weighted, work[...], 1, 1)
 
 
 def local(right_side, factor_window, diag_inverse, phase_cov):
@@ -115,11 +156,17 @@
     piece = pl.pallas_call(
         prepare,
         out_shape=jax.ShapeDtypeStruct((col_width + chunk, block_rows), jnp.float32),
-        in_specs=[smem, vmem, vmem, vmem],
+        in_specs=[smem] + [pl.BlockSpec(memory_space=pltpu.HBM)] * 3,
         out_specs=vmem,
-        scratch_shapes=[pltpu.VMEM((rank_width, block_rows), jnp.float32)],
-        compiler_params=params,
-    )(place, right_side, factor_window, diag_inverse)
+        scratch_shapes=[
+            pltpu.VMEM(right_side.shape, jnp.float32),
+            pltpu.VMEM((col_width, block_rows), jnp.float32),
+            pltpu.VMEM(diag_inverse.shape, jnp.float32),
+            pltpu.VMEM((rank_width, block_rows), jnp.float32),
+            pltpu.SemaphoreType.DMA((3,)),
+        ],
+        compiler_params=pltpu.CompilerParams(vmem_limit_bytes=64 * 1024 * 1024 - 128 * 1024),
+    )(place, right_side, factor_window.T, diag_inverse)
     quarter = col_width // 2
 
     def device(row, col):
@@ -171,7 +218,7 @@
         out_shape=jax.ShapeDtypeStruct((TILE_ROWS, rank_width), jnp.float32),
         in_specs=[vmem, vmem],
         out_specs=vmem,
-        scratch_shapes=[pltpu.VMEM((rank_width, 2 * rank_width), jnp.float32)],
+        scratch_shapes=[pltpu.VMEM((rank_width, rank_width), jnp.float32)],
         compiler_params=params,
         cost_estimate=pl.CostEstimate(flops=1_000_000_000, bytes_accessed=3_000_000, transcendentals=0),
     )(low, phase)

time: 93 us -> 86.7 us (0.932)
  Pallas kernels: 16.2 us -> 10.4 us
  other arithmetic: 0.31 us -> 1.55 us
  local copies, waits for them, and re-layouts: 5.54 us -> 4.5 us
    pallas_call x1, Pallas kernels: 12.8 us -> 5.35 us  [local(): pl.pallas_call(tile_basis, out_shape=jax.ShapeDtypeStruct((TILE_ROWS, ran...]
    unnamed x8 -> x5, local copies, waits for them, and re-layouts: 3.23 us -> 0.71 us
    pallas_call x1, Pallas kernels: 0.95 us -> 2.57 us  [local(): pl.pallas_call(prepare, out_shape=jax.ShapeDtypeStruct((col_width + chunk...]
  transfers between devices with their start and end apart: 7 -> 7, of which waited for: 6 -> 6; matrix products, arithmetic and copies ran while one was open for 2% -> 3% of each run, Pallas kernels for 3% -> 3%
where the time goes in v4:
time: 86.7 us; the launch traced here: 86.2 us
  waiting for transfers between devices  29.3 us (34%)
  starting transfers between devices  27.1 us (31%)
  blocking collectives  12.6 us (15%)
  Pallas kernels  10.4 us (12%)
  local copies, waits for them, and re-layouts  4.5 us (5%)
  other arithmetic  1.55 us (2%)
    ppermute x3, waiting for transfers between devices, local(): slots.append(lax.ppermute(plane, 'row', turn_on))  17.2 us
    all_to_all x1, starting transfers between devices, local(): lax.all_to_all(copies, ('row', 'col'), 0, 0, axis_index_groups=planes, ti...  17 us
    all_to_all x1, blocking collectives, local(): return (lax.all_to_all(basis, 'col', 0, 0, tiled=True), solved)  12.6 us
    all_to_all x1, starting transfers between devices, local(): lax.all_to_all(cut, 'col', 0, 0, tiled=True)  6.54 us
    all_to_all x1, waiting for transfers between devices, local(): lax.all_to_all(copies, ('row', 'col'), 0, 0, axis_index_groups=planes, ti...  6.26 us
    pallas_call x1, Pallas kernels, local(): pl.pallas_call(tile_basis, out_shape=jax.ShapeDtypeStruct((TILE_ROWS, ran...  5.35 us
    all_to_all x1, waiting for transfers between devices, local(): lax.all_to_all(cut, 'col', 0, 0, tiled=True)  3.12 us
    ppermute x1, waiting for transfers between devices, local(): lax.ppermute(own, 'col', [(col, col ^ 1) for col in range(col_count)])  2.66 us
  transfers between devices with their start and end apart: 7, of which 6 were waited for; matrix products, arithmetic and copies ran while one was open for 3% of the time, Pallas kernels for 3%

profile of v4, /device:TPU:1, one launch (start us, length us, event | category | flops | bytes accessed | tf_op | source)
XLA Modules:
  0.0 86.2 jit_solution(9173441075266324067)
XLA Ops:
  0.6 0.6 pad_add_fusion.place_ref
  1.2 2.6 %shard_map.59 = f32[72,128]{1,0:T(8,128)} custom-call(s32[2]{0:T(128)} %pad_add_fusion.place_ref, f32[128,128]{1,0:T(8,128)} %right_hbm.1, f32[64,128]{1,0:T(8,128)} %bitcast.24, f32[128,128]{1,0:T(8,128)} %diag_hbm.1), custom_call_target="tpu_custom_call" | custom-call | tf_op jit(solution)/shard_map/pallas_call | solution.py:156
  3.8 0.0 copy-start.1
  3.8 0.8 slice.13
  4.6 0.7 collective-permute-start
  5.3 0.7 slice.14
  6.0 0.0 collective-permute-done
  6.0 0.7 slice_select_fusion
  6.7 0.7 broadcast_in_dim.2
  7.5 17.0 %all-to-all-start = ((f32[16,40,128]{2,1,0:T(8,128)}), f32[16,40,128]{2,1,0:T(8,128)S(1)}, u32[]{:S(2)}, u32[]{:S(2)}) async-start(f32[16,40,128]{2,1,0:T(8,128)} %broadcast_in_dim.2), calls=%async_computation | async-start | bytes 655360 | tf_op jit(solution)/shard_map/all_to_all | solution.py:190
  24.4 0.0 copy-done.1
  24.5 0.1 convert_element_type.13
  24.6 1.5 %copy.9 = f32[8,16,8,512]{3,2,0,1:T(8,128)} copy(f32[8,16,8,512]{3,2,1,0:T(8,128)S(1)} %bitcast.19) | data formatting | bytes 4194304 | tf_op jit(solution)/shard_map/convert_element_type | solution.py:192
  26.1 6.3 %all-to-all-done = f32[16,40,128]{2,1,0:T(8,128)S(1)} async-done(((f32[16,40,128]{2,1,0:T(8,128)}), f32[16,40,128]{2,1,0:T(8,128)S(1)}, u32[]{:S(2)}, u32[]{:S(2)}) %all-to-all-start) | async-done | bytes 327712 | tf_op jit(solution)/shard_map/all_to_all | solution.py:190
  32.4 6.5 %all-to-all-start.1 = ((f32[16,64,512]{2,1,0:T(8,128)}), f32[16,64,512]{2,1,0:T(8,128)S(1)}, u32[]{:S(2)}, u32[]{:S(2)}) async-start(f32[16,64,512]{2,1,0:T(8,128)} %bitcast.18), calls=%async_computation.1 | async-start | bytes 4194304 | tf_op jit(solution)/shard_map/all_to_all | solution.py:194
  38.9 1.4 %collective-permute-start.3 = (f32[16,40,128]{2,1,0:T(8,128)S(1)}, f32[16,40,128]{2,1,0:T(8,128)S(1)}, u32[]{:S(2)}, u32[]{:S(2)}) collective-permute-start(f32[16,40,128]{2,1,0:T(8,128)S(1)} %all-to-all-done), channel_id=1, source_target_pairs={{0,96},{16,112},{32,0},{48,16},{64,32},{80,48},{96,64},{112,80},{1... | collective-permute-start | bytes 983048 | tf_op jit(solution)/shard_map/ppermute | solution.py:198
  40.4 0.3 collective-permute-start.2
  40.7 0.6 collective-permute-start.1
  41.3 6.6 %collective-permute-done.3 = f32[16,40,128]{2,1,0:T(8,128)S(1)} collective-permute-done((f32[16,40,128]{2,1,0:T(8,128)S(1)}, f32[16,40,128]{2,1,0:T(8,128)S(1)}, u32[]{:S(2)}, u32[]{:S(2)}) %collective-permute-start.3) | collective-permute-done | bytes 327712 | tf_op jit(solution)/shard_map/ppermute | solution.py:198
  48.0 2.7 %collective-permute-done.2 = f32[16,40,128]{2,1,0:T(8,128)S(1)} collective-permute-done((f32[16,40,128]{2,1,0:T(8,128)S(1)}, f32[16,40,128]{2,1,0:T(8,128)S(1)}, u32[]{:S(2)}, u32[]{:S(2)}) %collective-permute-start.2) | collective-permute-done | bytes 327712 | tf_op jit(solution)/shard_map/ppermute | solution.py:198
  50.6 7.9 %collective-permute-done.1 = f32[16,40,128]{2,1,0:T(8,128)S(1)} collective-permute-done((f32[16,40,128]{2,1,0:T(8,128)S(1)}, f32[16,40,128]{2,1,0:T(8,128)S(1)}, u32[]{:S(2)}, u32[]{:S(2)}) %collective-permute-start.1) | collective-permute-done | bytes 327712 | tf_op jit(solution)/shard_map/ppermute | solution.py:198
  58.6 0.0 copy-start
  58.6 0.1 pad_maximum_fusion.own_ref
  58.7 0.6 collective-permute-start.4
  59.2 2.7 %collective-permute-done.4.other_ref = f32[4,16,40,128]{3,2,1,0:T(8,128)S(1)} collective-permute-done((f32[4,16,40,128]{3,2,1,0:T(8,128)S(1)}, f32[4,16,40,128]{3,2,1,0:T(8,128)S(1)}, u32[]{:S(2)}, u32[]{:S(2)}) %collective-permute-start.4) | collective-permute-done | bytes 1310752 | tf_op jit(solution)/shard_map/ppermute | solution.py:200
  61.9 0.0 copy-done
  61.9 2.5 %shard_map.60 = (bf16[128,1024]{1,0:T(8,128)(2,1)S(1)}, f32[64,128]{1,0:T(8,128)}) custom-call(s32[2]{0:T(128)S(1)} %copy-done, f32[4,16,40,128]{3,2,1,0:T(8,128)S(1)} %pad_maximum_fusion.own_ref, f32[4,16,40,128]{3,2,1,0:T(8,128)S(1)} %collective-permute-done.4.other_ref), custom_call_target="tpu_custom_call" | custom-call | flops 800000000 | bytes 3000000 | tf_op jit(solution)/shard_map/pallas_call | solution.py:201
  64.4 3.1 %all-to-all-done.1 = f32[16,64,512]{2,1,0:T(8,128)S(1)} async-done(((f32[16,64,512]{2,1,0:T(8,128)}), f32[16,64,512]{2,1,0:T(8,128)S(1)}, u32[]{:S(2)}, u32[]{:S(2)}) %all-to-all-start.1) | async-done | bytes 2097184 | tf_op jit(solution)/shard_map/all_to_all | solution.py:194
  67.5 5.4 %shard_map.61 = f32[512,128]{1,0:T(8,128)S(1)} custom-call(bf16[128,1024]{1,0:T(8,128)(2,1)S(1)} %get-tuple-element.7.low_ref, f32[1024,512]{1,0:T(8,128)S(1)} %bitcast.16), custom_call_target="tpu_custom_call" | custom-call | flops 1000000000 | bytes 3000000 | tf_op jit(solution)/shard_map/pallas_call | solution.py:216
  72.9 12.6 %all_to_all.15 = f32[16,32,128]{2,1,0:T(8,128)S(1)} all-to-all(f32[16,32,128]{2,1,0:T(8,128)S(1)} %bitcast.17), channel_id=1, replica_groups=mesh['row'=8,'col'=16] {'col'}, dimensions={0} | all-to-all | bytes 524288 | tf_op jit(solution)/shard_map/all_to_all | solution.py:226
  85.5 0.7 copy.11
  (1 shorter events, 0.0 us)
Async XLA Ops:
  3.8 20.6 %copy-start.1 = (bf16[64,8192]{1,0:T(8,128)(2,1)S(1)}, bf16[64,8192]{1,0:T(8,128)(2,1)}, u32[]{:S(2)}) copy-start(bf16[64,8192]{1,0:T(8,128)(2,1)} %param.7) | copy-start | bytes 3145732
  4.6 1.4 %collective-permute-start = (f32[32,128]{1,0:T(8,128)S(1)}, f32[32,128]{1,0:T(8,128)S(1)}, u32[]{:S(2)}, u32[]{:S(2)}) collective-permute-start(f32[32,128]{1,0:T(8,128)S(1)} %slice.13), channel_id=1, source_target_pairs={{16,110},{17,111},{32,94},{33,95},{34,92},{35,93},{48,78},{49,79},... | collective-permute-start | bytes 49160 | tf_op jit(solution)/shard_map/ppermute | solution.py:181
  7.5 24.9 %all-to-all-start = ((f32[16,40,128]{2,1,0:T(8,128)}), f32[16,40,128]{2,1,0:T(8,128)S(1)}, u32[]{:S(2)}, u32[]{:S(2)}) async-start(f32[16,40,128]{2,1,0:T(8,128)} %broadcast_in_dim.2), calls=%async_computation | async-start | bytes 655360 | tf_op jit(solution)/shard_map/all_to_all | solution.py:190
  32.4 35.1 %all-to-all-start.1 = ((f32[16,64,512]{2,1,0:T(8,128)}), f32[16,64,512]{2,1,0:T(8,128)S(1)}, u32[]{:S(2)}, u32[]{:S(2)}) async-start(f32[16,64,512]{2,1,0:T(8,128)} %bitcast.18), calls=%async_computation.1 | async-start | bytes 4194304 | tf_op jit(solution)/shard_map/all_to_all | solution.py:194
  38.9 9.0 %collective-permute-start.3 = (f32[16,40,128]{2,1,0:T(8,128)S(1)}, f32[16,40,128]{2,1,0:T(8,128)S(1)}, u32[]{:S(2)}, u32[]{:S(2)}) collective-permute-start(f32[16,40,128]{2,1,0:T(8,128)S(1)} %all-to-all-done), channel_id=1, source_target_pairs={{0,96},{16,112},{32,0},{48,16},{64,32},{80,48},{96,64},{112,80},{1... | collective-permute-start | bytes 983048 | tf_op jit(solution)/shard_map/ppermute | solution.py:198
  40.4 10.2 %collective-permute-start.2 = (f32[16,40,128]{2,1,0:T(8,128)S(1)}, f32[16,40,128]{2,1,0:T(8,128)S(1)}, u32[]{:S(2)}, u32[]{:S(2)}) collective-permute-start(f32[16,40,128]{2,1,0:T(8,128)S(1)} %all-to-all-done), channel_id=1, source_target_pairs={{0,64},{16,80},{32,96},{48,112},{64,0},{80,16},{96,32},{112,48},{1... | collective-permute-start | bytes 983048 | tf_op jit(solution)/shard_map/ppermute | solution.py:198
  40.7 17.8 %collective-permute-start.1 = (f32[16,40,128]{2,1,0:T(8,128)S(1)}, f32[16,40,128]{2,1,0:T(8,128)S(1)}, u32[]{:S(2)}, u32[]{:S(2)}) collective-permute-start(f32[16,40,128]{2,1,0:T(8,128)S(1)} %all-to-all-done), channel_id=1, source_target_pairs={{0,32},{16,48},{32,64},{48,80},{64,96},{80,112},{96,0},{112,16},{1... | collective-permute-start | bytes 983048 | tf_op jit(solution)/shard_map/ppermute | solution.py:198
  58.6 3.3 %copy-start = (s32[2]{0:T(128)S(1)}, s32[2]{0:T(128)}, u32[]{:S(2)}) copy-start(s32[2]{0:T(128)} %pad_add_fusion.place_ref) | copy-start | bytes 28
  58.7 3.2 %collective-permute-start.4 = (f32[4,16,40,128]{3,2,1,0:T(8,128)S(1)}, f32[4,16,40,128]{3,2,1,0:T(8,128)S(1)}, u32[]{:S(2)}, u32[]{:S(2)}) collective-permute-start(f32[4,16,40,128]{3,2,1,0:T(8,128)S(1)} %pad_maximum_fusion.own_ref), channel_id=1, source_target_pairs={{0,1},{1,0},{2,3},{3,2},{4,5},{5,4},{6,7},{7,6},{8,9},{9,8},{10,11... | collective-permute-start | bytes 3932168 | tf_op jit(solution)/shard_map/ppermute | solution.py:200

commit v5 on v4

--- a/solution.py
+++ b/solution.py
@@ -28,18 +28,30 @@
     return dot(a[0], b[0]) + (dot(a[0], b[1]) + dot(a[1], b[0]))
 
 
-def prepare(place_ref, right_hbm, factor_hbm, diag_hbm, out_ref, right, factor, diag, scratch, arrived):
+def prepare(right_hbm, factor_hbm, diag_hbm, message_ref, send_ref, right, factor, diag, scratch, arrived):
     sources = ((diag_hbm, diag), (factor_hbm, factor), (right_hbm, right))
     copies = [pltpu.make_async_copy(source, target, arrived.at[i]) for i, (source, target) in enumerate(sources)]
     for copy in copies:
         copy.start()
     for copy in copies:
         copy.wait()
-    half = factor.shape[0]
-    chunk = out_ref.shape[0] - half
-    out_ref[:half] = contract(factor[...], diag[...], 1, 1)
+    quarter = send_ref.shape[0]
+    chunk = message_ref.shape[0] - quarter
+    scaled = contract(factor[...], diag[...], 1, 1)
+    message_ref[:quarter] = scaled[:quarter]
+    send_ref[...] = scaled[quarter:]
     scratch[...] = contract(right[...], diag[...], 0, 1)
-    out_ref[half:] = scratch[pl.ds(pl.multiple_of(place_ref[0] * chunk, chunk), chunk), :]
+    message_ref[quarter:] = scratch[pl.ds(pl.multiple_of(lax.axis_index("col") * chunk, chunk), chunk), :]
+
+
+def spread(message_ref, folded_ref, out_ref):
+    quarter = folded_ref.shape[0]
+    keeps = lax.axis_index("col") // 2 < lax.axis_index("row")
+    top = jnp.where(keeps, message_ref[:quarter], folded_ref[...])
+    bottom = message_ref[quarter:]
+    for at in range(out_ref.shape[0]):
+        out_ref[at, :quarter] = top
+        out_ref[at, quarter:] = bottom
 
 
 def factor_and_invert(work, size):
@@ -96,16 +108,17 @@
     work[...] = jnp.where(lower, work[...], 0.0)
 
 
-def block_solve(place_ref, own_ref, other_ref, low_ref, solved_ref, solved_t, work):
+def block_solve(own_ref, other_ref, low_ref, solved_ref, solved_t, work):
     turns, planes, rows, size = own_ref.shape
     blocks = turns * 2
     quarter = size // 4
-    col, turn = place_ref[0], place_ref[1]
+    col, row = lax.axis_index("col"), lax.axis_index("row")
+    turn, low_bit = row // 2, row % 2
     core = col % 2
 
     def piece(block_row, block_col, half, start, stop):
         slot = (turn - block_row // 2 + turns) % turns
-        at = block_row % 2 * blocks + block_col
+        at = jnp.bitwise_xor(block_row % 2, low_bit) * blocks + block_col
         own, other = own_ref[slot, at, start:stop, :], other_ref[slot, at, start:stop, :]
         return jnp.where(core == half, own, other)
 
@@ -141,8 +154,6 @@
 def local(right_side, factor_window, diag_inverse, phase_cov):
     row_count = lax.axis_size("row")
     col_count = lax.axis_size("col")
-    row_index = lax.axis_index("row")
-    col_index = lax.axis_index("col")
     block_rows = right_side.shape[0]
     rank_width = right_side.shape[1]
     col_width = factor_window.shape[1]
@@ -150,14 +161,16 @@
     turns = row_count // 2
     blocks = col_count // 2
     vmem = pl.BlockSpec(memory_space=pltpu.VMEM)
-    smem = pl.BlockSpec(memory_space=pltpu.SMEM)
     params = pltpu.CompilerParams(vmem_limit_bytes=VMEM_BYTES)
-    place = jnp.stack([col_index, row_index // 2]).astype(jnp.int32)
-    piece = pl.pallas_call(
+    quarter = col_width // 2
+    message, send = pl.pallas_call(
         prepare,
-        out_shape=jax.ShapeDtypeStruct((col_width + chunk, block_rows), jnp.float32),
-        in_specs=[smem] + [pl.BlockSpec(memory_space=pltpu.HBM)] * 3,
-        out_specs=vmem,
+        out_shape=[
+            jax.ShapeDtypeStruct((quarter + chunk, block_rows), jnp.float32),
+            jax.ShapeDtypeStruct((quarter, block_rows), jnp.float32),
+        ],
+        in_specs=[pl.BlockSpec(memory_space=pltpu.HBM)] * 3,
+        out_specs=[vmem, vmem],
         scratch_shapes=[
             pltpu.VMEM(right_side.shape, jnp.float32),
             pltpu.VMEM((col_width, block_rows), jnp.float32),
@@ -166,8 +179,7 @@
             pltpu.SemaphoreType.DMA((3,)),
         ],
         compiler_params=pltpu.CompilerParams(vmem_limit_bytes=64 * 1024 * 1024 - 128 * 1024),
-    )(place, right_side, factor_window.T, diag_inverse)
-    quarter = col_width // 2
+    )(right_side, factor_window.T, diag_inverse)
 
     def device(row, col):
         return row * col_count + col
@@ -178,20 +190,22 @@
         for j in range(row)
         for core in range(2)
     ]
-    folded = lax.ppermute(piece[quarter:col_width], ("row", "col"), fold)
-    kept = jnp.where(col_index // 2 < row_index, piece[:quarter], folded)
-    message = jnp.concatenate([kept, piece[col_width:]], axis=0)
-    planes = [
-        [device(2 * turn + low_bit, 2 * j + core) for low_bit in range(2) for j in range(blocks)]
-        for turn in range(turns)
-        for core in range(2)
-    ]
-    copies = jnp.broadcast_to(message[None], (2 * blocks,) + message.shape)
-    plane = lax.all_to_all(copies, ("row", "col"), 0, 0, axis_index_groups=planes, tiled=True)
+    folded = lax.ppermute(send, ("row", "col"), fold)
+    copies = pl.pallas_call(
+        spread,
+        out_shape=jax.ShapeDtypeStruct((blocks,) + message.shape, jnp.float32),
+        in_specs=[vmem, vmem],
+        out_specs=vmem,
+        compiler_params=params,
+    )(message, folded)
+    levels = [[2 * j + core for j in range(blocks)] for core in range(2)]
+    plane = lax.all_to_all(copies, "col", 0, 0, axis_index_groups=levels, tiled=True)
     tile_count = phase_cov.shape[1] // TILE_ROWS
     cut = jnp.transpose(phase_cov.reshape(col_width, tile_count, TILE_ROWS), (1, 0, 2)).astype(jnp.float32)
     plane, cut = lax.optimization_barrier((plane, cut))
     phase = lax.all_to_all(cut, "col", 0, 0, tiled=True).reshape(col_count * col_width, TILE_ROWS)
+    beside = lax.ppermute(plane, "row", [(row, row ^ 1) for row in range(row_count)])
+    plane = jnp.concatenate([plane, beside], axis=0)
     slots = [plane]
     for step in range(1, turns):
         turn_on = [(2 * turn + bit, 2 * ((turn + step) % turns) + bit) for turn in range(turns) for bit in range(2)]
@@ -204,7 +218,7 @@
             jax.ShapeDtypeStruct((rank_width, row_count * block_rows), jnp.bfloat16),
             jax.ShapeDtypeStruct((col_width, rank_width), jnp.float32),
         ],
-        in_specs=[smem, vmem, vmem],
+        in_specs=[vmem, vmem],
         out_specs=[vmem, vmem],
         scratch_shapes=[
             pltpu.VMEM((row_count, rank_width, block_rows), jnp.float32),
@@ -212,7 +226,7 @@
         ],
         compiler_params=params,
         cost_estimate=pl.CostEstimate(flops=800_000_000, bytes_accessed=3_000_000, transcendentals=0),
-    )(place, own, other)
+    )(own, other)
     basis = pl.pallas_call(
         tile_basis,
         out_shape=jax.ShapeDtypeStruct((TILE_ROWS, rank_width), jnp.float32),

time: 86.7 us -> 84.8 us (0.978)
  starting transfers between devices: 27.1 us -> 29.1 us
  local copies, waits for them, and re-layouts: 4.5 us -> 2.99 us
  waiting for transfers between devices: 29.3 us -> 27.8 us
    all_to_all x1, waiting for transfers between devices: 6.26 us -> 4.38 us  [local(): lax.all_to_all(copies, 'col', 0, 0, axis_index_groups=levels, tiled=True)]
    ppermute x1 -> x2, starting transfers between devices: 0.65 us -> 2.27 us  [the longest x1 1.61 us: local(): lax.ppermute(plane, 'row', [(row, row ^ 1) for row in range(row_count)])]
    slice x2 -> x0, local copies, waits for them, and re-layouts: 1.5 us -> none  [the longest x1 0.81 us: local(): folded = lax.ppermute(piece[quarter:col_width], ('row', 'col'), fold)]
    all_to_all x1, waiting for transfers between devices: 3.12 us -> 4.43 us  [local(): lax.all_to_all(cut, 'col', 0, 0, tiled=True)]
    convert_element_type x1, other arithmetic: 0.14 us -> 1.36 us  [local(): jnp.transpose(phase_cov.reshape(col_width, tile_count, TILE_ROWS), (1, 0,...]
    pallas_call x1 -> x2, Pallas kernels: 2.57 us -> 2.58 us  [the longest x1 1.9 us: local(): pl.pallas_call(prepare, out_shape=[jax.ShapeDtypeStruct((quarter + chunk,...]
  transfers between devices with their start and end apart: 7 -> 8, of which waited for: 6 -> 6; matrix products, arithmetic and copies ran while one was open for 3% -> 4% of each run, Pallas kernels for 3% -> 2%
where the time goes in v5:
time: 84.8 us; the launch traced here: 84.4 us
  starting transfers between devices  29.1 us (34%)
  waiting for transfers between devices  27.8 us (33%)
  blocking collectives  12.5 us (15%)
  Pallas kernels  9.87 us (12%)
  local copies, waits for them, and re-layouts  2.99 us (4%)
  other arithmetic  1.45 us (2%)
    all_to_all x1, starting transfers between devices, local(): lax.all_to_all(copies, 'col', 0, 0, axis_index_groups=levels, tiled=True)  16.7 us
    ppermute x3, waiting for transfers between devices, local(): slots.append(lax.ppermute(plane, 'row', turn_on))  16.4 us
    all_to_all x1, blocking collectives, local(): return (lax.all_to_all(basis, 'col', 0, 0, tiled=True), solved)  12.5 us
    all_to_all x1, starting transfers between devices, local(): lax.all_to_all(cut, 'col', 0, 0, tiled=True)  7.05 us
    pallas_call x1, Pallas kernels, local(): pl.pallas_call(tile_basis, out_shape=jax.ShapeDtypeStruct((TILE_ROWS, ran...  5.35 us
    all_to_all x1, waiting for transfers between devices, local(): lax.all_to_all(cut, 'col', 0, 0, tiled=True)  4.43 us
    all_to_all x1, waiting for transfers between devices, local(): lax.all_to_all(copies, 'col', 0, 0, axis_index_groups=levels, tiled=True)  4.38 us
    ppermute x1, waiting for transfers between devices, local(): lax.ppermute(own, 'col', [(col, col ^ 1) for col in range(col_count)])  2.66 us
  transfers between devices with their start and end apart: 8, of which 6 were waited for; matrix products, arithmetic and copies ran while one was open for 4% of the time, Pallas kernels for 2%

profile of v5, /device:TPU:1, one launch (start us, length us, event | category | flops | bytes accessed | tf_op | source)
XLA Modules:
  0.0 84.4 jit_solution(12491956748119286663)
XLA Ops:
  0.6 1.9 %shard_map.59 = (f32[40,128]{1,0:T(8,128)}, f32[32,128]{1,0:T(8,128)}) custom-call(f32[128,128]{1,0:T(8,128)} %right_hbm.1, f32[64,128]{1,0:T(8,128)} %bitcast.22, f32[128,128]{1,0:T(8,128)} %diag_hbm.1), custom_call_target="tpu_custom_call" | custom-call | tf_op jit(solution)/shard_map/pallas_call | solution.py:166
  2.5 0.7 collective-permute-start
  3.2 0.0 collective-permute-done.folded_ref
  3.2 0.0 copy-start
  3.2 0.7 copy-done
  3.9 0.7 shard_map.60
  4.6 16.7 %all-to-all-start = ((f32[8,40,128]{2,1,0:T(8,128)}), f32[8,40,128]{2,1,0:T(8,128)S(1)}, u32[]{:S(2)}, u32[]{:S(2)}) async-start(f32[8,40,128]{2,1,0:T(8,128)} %shard_map.60), calls=%async_computation | async-start | bytes 327680 | tf_op jit(solution)/shard_map/all_to_all | solution.py:202
  21.4 1.4 %convert_element_type.13 = f32[64,8192]{1,0:T(8,128)S(1)} convert(bf16[64,8192]{1,0:T(8,128)(2,1)} %param.7) | non-fusion elementwise | flops 524288 | bytes 3145728 | tf_op jit(solution)/shard_map/convert_element_type | solution.py:204
  22.7 1.5 %copy.9 = f32[8,16,8,512]{3,2,0,1:T(8,128)} copy(f32[8,16,8,512]{3,2,1,0:T(8,128)S(1)} %bitcast.17) | data formatting | bytes 4194304 | tf_op jit(solution)/shard_map/convert_element_type | solution.py:204
  24.3 4.4 %all-to-all-done = f32[8,40,128]{2,1,0:T(8,128)S(1)} async-done(((f32[8,40,128]{2,1,0:T(8,128)}), f32[8,40,128]{2,1,0:T(8,128)S(1)}, u32[]{:S(2)}, u32[]{:S(2)}) %all-to-all-start) | async-done | bytes 163872 | tf_op jit(solution)/shard_map/all_to_all | solution.py:202
  28.6 1.6 %collective-permute-start.1 = (f32[8,40,128]{2,1,0:T(8,128)S(1)}, f32[8,40,128]{2,1,0:T(8,128)S(1)}, u32[]{:S(2)}, u32[]{:S(2)}) collective-permute-start(f32[8,40,128]{2,1,0:T(8,128)S(1)} %all-to-all-done), channel_id=1, source_target_pairs={{0,16},{16,0},{32,48},{48,32},{64,80},{80,64},{96,112},{112,96},{1... | collective-permute-start | bytes 491528 | tf_op jit(solution)/shard_map/ppermute | solution.py:207
  30.3 7.0 %all-to-all-start.1 = ((f32[16,64,512]{2,1,0:T(8,128)}), f32[16,64,512]{2,1,0:T(8,128)S(1)}, u32[]{:S(2)}, u32[]{:S(2)}) async-start(f32[16,64,512]{2,1,0:T(8,128)} %bitcast.16), calls=%async_computation.1 | async-start | bytes 4194304 | tf_op jit(solution)/shard_map/all_to_all | solution.py:206
  37.3 0.0 collective-permute-done.1
  37.3 0.7 collective-permute-start.4
  38.0 1.2 %collective-permute-start.3 = (f32[16,40,128]{2,1,0:T(8,128)S(1)}, f32[16,40,128]{2,1,0:T(8,128)S(1)}, u32[]{:S(2)}, u32[]{:S(2)}) collective-permute-start(f32[16,40,128]{2,1,0:T(8,128)S(1)} %constant_dynamic-update-slice_fusion), channel_id=1, source_target_pairs={{0,64},{16,80},{32,96},{48,112},{64,0},{80,16},{96,32},{112,48},{1... | collective-permute-start | bytes 983048 | tf_op jit(solution)/shard_map/ppermute | solution.py:212
  39.2 0.6 collective-permute-start.2
  39.8 6.7 %collective-permute-done.4 = f32[16,40,128]{2,1,0:T(8,128)S(1)} collective-permute-done((f32[16,40,128]{2,1,0:T(8,128)S(1)}, f32[16,40,128]{2,1,0:T(8,128)S(1)}, u32[]{:S(2)}, u32[]{:S(2)}) %collective-permute-start.4) | collective-permute-done | bytes 327712 | tf_op jit(solution)/shard_map/ppermute | solution.py:212
  46.5 0.2 collective-permute-done.3
  46.7 9.5 %collective-permute-done.2 = f32[16,40,128]{2,1,0:T(8,128)S(1)} collective-permute-done((f32[16,40,128]{2,1,0:T(8,128)S(1)}, f32[16,40,128]{2,1,0:T(8,128)S(1)}, u32[]{:S(2)}, u32[]{:S(2)}) %collective-permute-start.2) | collective-permute-done | bytes 327712 | tf_op jit(solution)/shard_map/ppermute | solution.py:212
  56.2 0.1 pad_maximum_fusion.own_ref
  56.3 0.6 collective-permute-start.5
  56.8 2.7 %collective-permute-done.5.other_ref = f32[4,16,40,128]{3,2,1,0:T(8,128)S(1)} collective-permute-done((f32[4,16,40,128]{3,2,1,0:T(8,128)S(1)}, f32[4,16,40,128]{3,2,1,0:T(8,128)S(1)}, u32[]{:S(2)}, u32[]{:S(2)}) %collective-permute-start.5) | collective-permute-done | bytes 1310752 | tf_op jit(solution)/shard_map/ppermute | solution.py:214
  59.5 1.9 %shard_map.61 = (bf16[128,1024]{1,0:T(8,128)(2,1)S(1)}, f32[64,128]{1,0:T(8,128)}) custom-call(f32[4,16,40,128]{3,2,1,0:T(8,128)S(1)} %pad_maximum_fusion.own_ref, f32[4,16,40,128]{3,2,1,0:T(8,128)S(1)} %collective-permute-done.5.other_ref), custom_call_target="tpu_custom_call" | custom-call | flops 800000000 | bytes 3000000 | tf_op jit(solution)/shard_map/pallas_call | solution.py:215
  61.4 4.4 %all-to-all-done.1 = f32[16,64,512]{2,1,0:T(8,128)S(1)} async-done(((f32[16,64,512]{2,1,0:T(8,128)}), f32[16,64,512]{2,1,0:T(8,128)S(1)}, u32[]{:S(2)}, u32[]{:S(2)}) %all-to-all-start.1) | async-done | bytes 2097184 | tf_op jit(solution)/shard_map/all_to_all | solution.py:206
  65.9 5.4 %shard_map.62 = f32[512,128]{1,0:T(8,128)S(1)} custom-call(bf16[128,1024]{1,0:T(8,128)(2,1)S(1)} %get-tuple-element.11.low_ref, f32[1024,512]{1,0:T(8,128)S(1)} %bitcast.14), custom_call_target="tpu_custom_call" | custom-call | flops 1000000000 | bytes 3000000 | tf_op jit(solution)/shard_map/pallas_call | solution.py:230
  71.2 12.5 %all_to_all.15 = f32[16,32,128]{2,1,0:T(8,128)S(1)} all-to-all(f32[16,32,128]{2,1,0:T(8,128)S(1)} %bitcast.15), channel_id=1, replica_groups=mesh['row'=8,'col'=16] {'col'}, dimensions={0} | all-to-all | bytes 524288 | tf_op jit(solution)/shard_map/all_to_all | solution.py:240
  83.7 0.7 copy.12
  (2 shorter events, 0.0 us)
Async XLA Ops:
  2.5 0.7 collective-permute-start
  3.2 0.7 copy-start
  4.6 24.0 %all-to-all-start = ((f32[8,40,128]{2,1,0:T(8,128)}), f32[8,40,128]{2,1,0:T(8,128)S(1)}, u32[]{:S(2)}, u32[]{:S(2)}) async-start(f32[8,40,128]{2,1,0:T(8,128)} %shard_map.60), calls=%async_computation | async-start | bytes 327680 | tf_op jit(solution)/shard_map/all_to_all | solution.py:202
  28.6 8.7 %collective-permute-start.1 = (f32[8,40,128]{2,1,0:T(8,128)S(1)}, f32[8,40,128]{2,1,0:T(8,128)S(1)}, u32[]{:S(2)}, u32[]{:S(2)}) collective-permute-start(f32[8,40,128]{2,1,0:T(8,128)S(1)} %all-to-all-done), channel_id=1, source_target_pairs={{0,16},{16,0},{32,48},{48,32},{64,80},{80,64},{96,112},{112,96},{1... | collective-permute-start | bytes 491528 | tf_op jit(solution)/shard_map/ppermute | solution.py:207
  30.3 35.6 %all-to-all-start.1 = ((f32[16,64,512]{2,1,0:T(8,128)}), f32[16,64,512]{2,1,0:T(8,128)S(1)}, u32[]{:S(2)}, u32[]{:S(2)}) async-start(f32[16,64,512]{2,1,0:T(8,128)} %bitcast.16), calls=%async_computation.1 | async-start | bytes 4194304 | tf_op jit(solution)/shard_map/all_to_all | solution.py:206
  37.3 9.2 %collective-permute-start.4 = (f32[16,40,128]{2,1,0:T(8,128)S(1)}, f32[16,40,128]{2,1,0:T(8,128)S(1)}, u32[]{:S(2)}, u32[]{:S(2)}) collective-permute-start(f32[16,40,128]{2,1,0:T(8,128)S(1)} %constant_dynamic-update-slice_fusion), channel_id=1, source_target_pairs={{0,96},{16,112},{32,0},{48,16},{64,32},{80,48},{96,64},{112,80},{1... | collective-permute-start | bytes 983048 | tf_op jit(solution)/shard_map/ppermute | solution.py:212
  38.0 8.7 %collective-permute-start.3 = (f32[16,40,128]{2,1,0:T(8,128)S(1)}, f32[16,40,128]{2,1,0:T(8,128)S(1)}, u32[]{:S(2)}, u32[]{:S(2)}) collective-permute-start(f32[16,40,128]{2,1,0:T(8,128)S(1)} %constant_dynamic-update-slice_fusion), channel_id=1, source_target_pairs={{0,64},{16,80},{32,96},{48,112},{64,0},{80,16},{96,32},{112,48},{1... | collective-permute-start | bytes 983048 | tf_op jit(solution)/shard_map/ppermute | solution.py:212
  39.2 17.0 %collective-permute-start.2 = (f32[16,40,128]{2,1,0:T(8,128)S(1)}, f32[16,40,128]{2,1,0:T(8,128)S(1)}, u32[]{:S(2)}, u32[]{:S(2)}) collective-permute-start(f32[16,40,128]{2,1,0:T(8,128)S(1)} %constant_dynamic-update-slice_fusion), channel_id=1, source_target_pairs={{0,32},{16,48},{32,64},{48,80},{64,96},{80,112},{96,0},{112,16},{1... | collective-permute-start | bytes 983048 | tf_op jit(solution)/shard_map/ppermute | solution.py:212
  56.3 3.2 %collective-permute-start.5 = (f32[4,16,40,128]{3,2,1,0:T(8,128)S(1)}, f32[4,16,40,128]{3,2,1,0:T(8,128)S(1)}, u32[]{:S(2)}, u32[]{:S(2)}) collective-permute-start(f32[4,16,40,128]{3,2,1,0:T(8,128)S(1)} %pad_maximum_fusion.own_ref), channel_id=1, source_target_pairs={{0,1},{1,0},{2,3},{3,2},{4,5},{5,4},{6,7},{7,6},{8,9},{9,8},{10,11... | collective-permute-start | bytes 3932168 | tf_op jit(solution)/shard_map/ppermute | solution.py:214

commit v6 on v5

--- a/solution.py
+++ b/solution.py
@@ -26,6 +26,11 @@
 def dot3(a, b):
     dot = functools.partial(jnp.dot, preferred_element_type=jnp.float32)
     return dot(a[0], b[0]) + (dot(a[0], b[1]) + dot(a[1], b[0]))
+
+
+def partner(row, col):
+    bits = 1 if row // 2 == col // 2 else 6
+    return row ^ bits, col ^ bits
 
 
 def prepare(right_hbm, factor_hbm, diag_hbm, message_ref, send_ref, right, factor, diag, scratch, arrived):
@@ -113,12 +118,12 @@
     blocks = turns * 2
     quarter = size // 4
     col, row = lax.axis_index("col"), lax.axis_index("row")
-    turn, low_bit = row // 2, row % 2
+    turn = row // 2
     core = col % 2
 
     def piece(block_row, block_col, half, start, stop):
         slot = (turn - block_row // 2 + turns) % turns
-        at = jnp.bitwise_xor(block_row % 2, low_bit) * blocks + block_col
+        at = block_row % 2 * blocks + block_col
         own, other = own_ref[slot, at, start:stop, :], other_ref[slot, at, start:stop, :]
         return jnp.where(core == half, own, other)
 
@@ -133,7 +138,7 @@
             break
         solved_pair = split(current[j])
         for i in range(j + 1, blocks):
-            places = ((i, j), (blocks - 1 - i, blocks - 1 - j))
+            places = ((i, j), partner(i, j))
             parts = [piece(*at, half, 0, quarter) for half in range(2) for at in places]
             current[i] = current[i] - dot3(solved_pair, split(jnp.concatenate(parts, axis=0)))
     half_rows = solved_ref.shape[0]
@@ -185,27 +190,29 @@
         return row * col_count + col
 
     fold = [
-        (device(row, 2 * j + core), device(row_count - 1 - row, 2 * (blocks - 1 - j) + core))
+        (device(row, 2 * j + core), device(partner(row, j)[0], 2 * partner(row, j)[1] + core))
         for row in range(row_count)
-        for j in range(row)
+        for j in range(blocks)
         for core in range(2)
     ]
     folded = lax.ppermute(send, ("row", "col"), fold)
     copies = pl.pallas_call(
         spread,
-        out_shape=jax.ShapeDtypeStruct((blocks,) + message.shape, jnp.float32),
+        out_shape=jax.ShapeDtypeStruct((2 * blocks,) + message.shape, jnp.float32),
         in_specs=[vmem, vmem],
         out_specs=vmem,
         compiler_params=params,
     )(message, folded)
-    levels = [[2 * j + core for j in range(blocks)] for core in range(2)]
-    plane = lax.all_to_all(copies, "col", 0, 0, axis_index_groups=levels, tiled=True)
+    planes = [
+        [device(2 * turn + low_bit, 2 * j + core) for low_bit in range(2) for j in range(blocks)]
+        for turn in range(turns)
+        for core in range(2)
+    ]
+    plane = lax.all_to_all(copies, ("row", "col"), 0, 0, axis_index_groups=planes, tiled=True)
     tile_count = phase_cov.shape[1] // TILE_ROWS
     cut = jnp.transpose(phase_cov.reshape(col_width, tile_count, TILE_ROWS), (1, 0, 2)).astype(jnp.float32)
     plane, cut = lax.optimization_barrier((plane, cut))
     phase = lax.all_to_all(cut, "col", 0, 0, tiled=True).reshape(col_count * col_width, TILE_ROWS)
-    beside = lax.ppermute(plane, "row", [(row, row ^ 1) for row in range(row_count)])
-    plane = jnp.concatenate([plane, beside], axis=0)
     slots = [plane]
     for step in range(1, turns):
         turn_on = [(2 * turn + bit, 2 * ((turn + step) % turns) + bit) for turn in range(turns) for bit in range(2)]

time: 84.8 us -> 80.8 us (0.953)
  starting transfers between devices: 29.1 us -> 23 us
  waiting for transfers between devices: 27.8 us -> 30 us
    all_to_all x1, starting transfers between devices: 16.7 us -> 9.82 us  [local(): lax.all_to_all(copies, ('row', 'col'), 0, 0, axis_index_groups=planes, ti...]
    ppermute x1, starting transfers between devices: 0.66 us -> 3.64 us  [local(): folded = lax.ppermute(send, ('row', 'col'), fold)]
    ppermute x1 -> x0, starting transfers between devices: 1.61 us -> none  [local(): lax.ppermute(plane, 'row', [(row, row ^ 1) for row in range(row_count)])]
    ppermute x1, waiting for transfers between devices: 0.01 us -> 1.34 us  [local(): folded = lax.ppermute(send, ('row', 'col'), fold)]
  transfers between devices with their start and end apart: 8 -> 7, of which waited for: 6 -> 7; matrix products, arithmetic and copies ran while one was open for 4% -> 4% of each run, Pallas kernels for 2% -> 2%
where the time goes in v6:
time: 80.8 us; the launch traced here: 80.4 us
  waiting for transfers between devices  30 us (37%)
  starting transfers between devices  23 us (28%)
  blocking collectives  12.5 us (15%)
  Pallas kernels  9.93 us (12%)
  local copies, waits for them, and re-layouts  2.97 us (4%)
  other arithmetic  1.45 us (2%)
    ppermute x3, waiting for transfers between devices, local(): slots.append(lax.ppermute(plane, 'row', turn_on))  16.9 us
    all_to_all x1, blocking collectives, local(): return (lax.all_to_all(basis, 'col', 0, 0, tiled=True), solved)  12.5 us
    all_to_all x1, starting transfers between devices, local(): lax.all_to_all(copies, ('row', 'col'), 0, 0, axis_index_groups=planes, ti...  9.82 us
    all_to_all x1, starting transfers between devices, local(): lax.all_to_all(cut, 'col', 0, 0, tiled=True)  6.54 us
    pallas_call x1, Pallas kernels, local(): pl.pallas_call(tile_basis, out_shape=jax.ShapeDtypeStruct((TILE_ROWS, ran...  5.36 us
    all_to_all x1, waiting for transfers between devices, local(): lax.all_to_all(copies, ('row', 'col'), 0, 0, axis_index_groups=planes, ti...  5.05 us
    all_to_all x1, waiting for transfers between devices, local(): lax.all_to_all(cut, 'col', 0, 0, tiled=True)  4.04 us
    ppermute x1, starting transfers between devices, local(): folded = lax.ppermute(send, ('row', 'col'), fold)  3.64 us
  transfers between devices with their start and end apart: 7, of which 7 were waited for; matrix products, arithmetic and copies ran while one was open for 4% of the time, Pallas kernels for 2%

profile of v6, /device:TPU:1, one launch (start us, length us, event | category | flops | bytes accessed | tf_op | source)
XLA Modules:
  0.0 80.4 jit_solution(8450709849375026830)
XLA Ops:
  0.6 1.9 %shard_map.59 = (f32[40,128]{1,0:T(8,128)}, f32[32,128]{1,0:T(8,128)}) custom-call(f32[128,128]{1,0:T(8,128)} %right_hbm.1, f32[64,128]{1,0:T(8,128)} %bitcast.22, f32[128,128]{1,0:T(8,128)} %diag_hbm.1), custom_call_target="tpu_custom_call" | custom-call | tf_op jit(solution)/shard_map/pallas_call | solution.py:171
  2.5 3.6 %collective-permute-start = (f32[32,128]{1,0:T(8,128)}, f32[32,128]{1,0:T(8,128)S(1)}, u32[]{:S(2)}, u32[]{:S(2)}) collective-permute-start(f32[32,128]{1,0:T(8,128)} %get-tuple-element.9), channel_id=1, source_target_pairs={{0,18},{1,19},{2,16},{3,17},{4,104},{5,105},{6,106},{7,107},{8,100... | collective-permute-start | bytes 49160 | tf_op jit(solution)/shard_map/ppermute | solution.py:198
  6.2 1.3 %collective-permute-done.folded_ref = f32[32,128]{1,0:T(8,128)S(1)} collective-permute-done((f32[32,128]{1,0:T(8,128)}, f32[32,128]{1,0:T(8,128)S(1)}, u32[]{:S(2)}, u32[]{:S(2)}) %collective-permute-start) | collective-permute-done | bytes 16416 | tf_op jit(solution)/shard_map/ppermute | solution.py:198
  7.5 0.0 copy-start
  7.5 0.7 copy-done
  8.2 0.7 shard_map.60
  9.0 9.8 %all-to-all-start = ((f32[16,40,128]{2,1,0:T(8,128)}), f32[16,40,128]{2,1,0:T(8,128)S(1)}, u32[]{:S(2)}, u32[]{:S(2)}) async-start(f32[16,40,128]{2,1,0:T(8,128)} %shard_map.60), calls=%async_computation | async-start | bytes 655360 | tf_op jit(solution)/shard_map/all_to_all | solution.py:211
  18.8 1.4 %convert_element_type.13 = f32[64,8192]{1,0:T(8,128)S(1)} convert(bf16[64,8192]{1,0:T(8,128)(2,1)} %param.7) | non-fusion elementwise | flops 524288 | bytes 3145728 | tf_op jit(solution)/shard_map/convert_element_type | solution.py:213
  20.2 1.5 %copy.9 = f32[8,16,8,512]{3,2,0,1:T(8,128)} copy(f32[8,16,8,512]{3,2,1,0:T(8,128)S(1)} %bitcast.17) | data formatting | bytes 4194304 | tf_op jit(solution)/shard_map/convert_element_type | solution.py:213
  21.7 5.0 %all-to-all-done = f32[16,40,128]{2,1,0:T(8,128)S(1)} async-done(((f32[16,40,128]{2,1,0:T(8,128)}), f32[16,40,128]{2,1,0:T(8,128)S(1)}, u32[]{:S(2)}, u32[]{:S(2)}) %all-to-all-start) | async-done | bytes 327712 | tf_op jit(solution)/shard_map/all_to_all | solution.py:211
  26.8 6.5 %all-to-all-start.1 = ((f32[16,64,512]{2,1,0:T(8,128)}), f32[16,64,512]{2,1,0:T(8,128)S(1)}, u32[]{:S(2)}, u32[]{:S(2)}) async-start(f32[16,64,512]{2,1,0:T(8,128)} %bitcast.16), calls=%async_computation.1 | async-start | bytes 4194304 | tf_op jit(solution)/shard_map/all_to_all | solution.py:215
  33.3 1.1 %collective-permute-start.3 = (f32[16,40,128]{2,1,0:T(8,128)S(1)}, f32[16,40,128]{2,1,0:T(8,128)S(1)}, u32[]{:S(2)}, u32[]{:S(2)}) collective-permute-start(f32[16,40,128]{2,1,0:T(8,128)S(1)} %all-to-all-done), channel_id=1, source_target_pairs={{0,96},{16,112},{32,0},{48,16},{64,32},{80,48},{96,64},{112,80},{1... | collective-permute-start | bytes 983048 | tf_op jit(solution)/shard_map/ppermute | solution.py:219
  34.4 0.7 collective-permute-start.2
  35.1 0.6 collective-permute-start.1
  35.7 6.6 %collective-permute-done.3 = f32[16,40,128]{2,1,0:T(8,128)S(1)} collective-permute-done((f32[16,40,128]{2,1,0:T(8,128)S(1)}, f32[16,40,128]{2,1,0:T(8,128)S(1)}, u32[]{:S(2)}, u32[]{:S(2)}) %collective-permute-start.3) | collective-permute-done | bytes 327712 | tf_op jit(solution)/shard_map/ppermute | solution.py:219
  42.3 2.3 %collective-permute-done.2 = f32[16,40,128]{2,1,0:T(8,128)S(1)} collective-permute-done((f32[16,40,128]{2,1,0:T(8,128)S(1)}, f32[16,40,128]{2,1,0:T(8,128)S(1)}, u32[]{:S(2)}, u32[]{:S(2)}) %collective-permute-start.2) | collective-permute-done | bytes 327712 | tf_op jit(solution)/shard_map/ppermute | solution.py:219
  44.7 7.9 %collective-permute-done.1 = f32[16,40,128]{2,1,0:T(8,128)S(1)} collective-permute-done((f32[16,40,128]{2,1,0:T(8,128)S(1)}, f32[16,40,128]{2,1,0:T(8,128)S(1)}, u32[]{:S(2)}, u32[]{:S(2)}) %collective-permute-start.1) | collective-permute-done | bytes 327712 | tf_op jit(solution)/shard_map/ppermute | solution.py:219
  52.6 0.1 pad_maximum_fusion.own_ref
  52.7 0.6 collective-permute-start.4
  53.3 2.7 %collective-permute-done.4.other_ref = f32[4,16,40,128]{3,2,1,0:T(8,128)S(1)} collective-permute-done((f32[4,16,40,128]{3,2,1,0:T(8,128)S(1)}, f32[4,16,40,128]{3,2,1,0:T(8,128)S(1)}, u32[]{:S(2)}, u32[]{:S(2)}) %collective-permute-start.4) | collective-permute-done | bytes 1310752 | tf_op jit(solution)/shard_map/ppermute | solution.py:221
  55.9 1.9 %shard_map.61 = (bf16[128,1024]{1,0:T(8,128)(2,1)S(1)}, f32[64,128]{1,0:T(8,128)}) custom-call(f32[4,16,40,128]{3,2,1,0:T(8,128)S(1)} %pad_maximum_fusion.own_ref, f32[4,16,40,128]{3,2,1,0:T(8,128)S(1)} %collective-permute-done.4.other_ref), custom_call_target="tpu_custom_call" | custom-call | flops 800000000 | bytes 3000000 | tf_op jit(solution)/shard_map/pallas_call | solution.py:222
  57.8 4.0 %all-to-all-done.1 = f32[16,64,512]{2,1,0:T(8,128)S(1)} async-done(((f32[16,64,512]{2,1,0:T(8,128)}), f32[16,64,512]{2,1,0:T(8,128)S(1)}, u32[]{:S(2)}, u32[]{:S(2)}) %all-to-all-start.1) | async-done | bytes 2097184 | tf_op jit(solution)/shard_map/all_to_all | solution.py:215
  61.9 5.4 %shard_map.62 = f32[512,128]{1,0:T(8,128)S(1)} custom-call(bf16[128,1024]{1,0:T(8,128)(2,1)S(1)} %get-tuple-element.11.low_ref, f32[1024,512]{1,0:T(8,128)S(1)} %bitcast.14), custom_call_target="tpu_custom_call" | custom-call | flops 1000000000 | bytes 3000000 | tf_op jit(solution)/shard_map/pallas_call | solution.py:237
  67.2 12.5 %all_to_all.15 = f32[16,32,128]{2,1,0:T(8,128)S(1)} all-to-all(f32[16,32,128]{2,1,0:T(8,128)S(1)} %bitcast.15), channel_id=1, replica_groups=mesh['row'=8,'col'=16] {'col'}, dimensions={0} | all-to-all | bytes 524288 | tf_op jit(solution)/shard_map/all_to_all | solution.py:247
  79.7 0.7 copy.11
Async XLA Ops:
  2.5 5.0 %collective-permute-start = (f32[32,128]{1,0:T(8,128)}, f32[32,128]{1,0:T(8,128)S(1)}, u32[]{:S(2)}, u32[]{:S(2)}) collective-permute-start(f32[32,128]{1,0:T(8,128)} %get-tuple-element.9), channel_id=1, source_target_pairs={{0,18},{1,19},{2,16},{3,17},{4,104},{5,105},{6,106},{7,107},{8,100... | collective-permute-start | bytes 49160 | tf_op jit(solution)/shard_map/ppermute | solution.py:198
  7.5 0.7 copy-start
  9.0 17.8 %all-to-all-start = ((f32[16,40,128]{2,1,0:T(8,128)}), f32[16,40,128]{2,1,0:T(8,128)S(1)}, u32[]{:S(2)}, u32[]{:S(2)}) async-start(f32[16,40,128]{2,1,0:T(8,128)} %shard_map.60), calls=%async_computation | async-start | bytes 655360 | tf_op jit(solution)/shard_map/all_to_all | solution.py:211
  26.8 35.1 %all-to-all-start.1 = ((f32[16,64,512]{2,1,0:T(8,128)}), f32[16,64,512]{2,1,0:T(8,128)S(1)}, u32[]{:S(2)}, u32[]{:S(2)}) async-start(f32[16,64,512]{2,1,0:T(8,128)} %bitcast.16), calls=%async_computation.1 | async-start | bytes 4194304 | tf_op jit(solution)/shard_map/all_to_all | solution.py:215
  33.3 9.0 %collective-permute-start.3 = (f32[16,40,128]{2,1,0:T(8,128)S(1)}, f32[16,40,128]{2,1,0:T(8,128)S(1)}, u32[]{:S(2)}, u32[]{:S(2)}) collective-permute-start(f32[16,40,128]{2,1,0:T(8,128)S(1)} %all-to-all-done), channel_id=1, source_target_pairs={{0,96},{16,112},{32,0},{48,16},{64,32},{80,48},{96,64},{112,80},{1... | collective-permute-start | bytes 983048 | tf_op jit(solution)/shard_map/ppermute | solution.py:219
  34.4 10.2 %collective-permute-start.2 = (f32[16,40,128]{2,1,0:T(8,128)S(1)}, f32[16,40,128]{2,1,0:T(8,128)S(1)}, u32[]{:S(2)}, u32[]{:S(2)}) collective-permute-start(f32[16,40,128]{2,1,0:T(8,128)S(1)} %all-to-all-done), channel_id=1, source_target_pairs={{0,64},{16,80},{32,96},{48,112},{64,0},{80,16},{96,32},{112,48},{1... | collective-permute-start | bytes 983048 | tf_op jit(solution)/shard_map/ppermute | solution.py:219
  35.1 17.5 %collective-permute-start.1 = (f32[16,40,128]{2,1,0:T(8,128)S(1)}, f32[16,40,128]{2,1,0:T(8,128)S(1)}, u32[]{:S(2)}, u32[]{:S(2)}) collective-permute-start(f32[16,40,128]{2,1,0:T(8,128)S(1)} %all-to-all-done), channel_id=1, source_target_pairs={{0,32},{16,48},{32,64},{48,80},{64,96},{80,112},{96,0},{112,16},{1... | collective-permute-start | bytes 983048 | tf_op jit(solution)/shard_map/ppermute | solution.py:219
  52.7 3.2 %collective-permute-start.4 = (f32[4,16,40,128]{3,2,1,0:T(8,128)S(1)}, f32[4,16,40,128]{3,2,1,0:T(8,128)S(1)}, u32[]{:S(2)}, u32[]{:S(2)}) collective-permute-start(f32[4,16,40,128]{3,2,1,0:T(8,128)S(1)} %pad_maximum_fusion.own_ref), channel_id=1, source_target_pairs={{0,1},{1,0},{2,3},{3,2},{4,5},{5,4},{6,7},{7,6},{8,9},{9,8},{10,11... | collective-permute-start | bytes 3932168 | tf_op jit(solution)/shard_map/ppermute | solution.py:221

commit v7 on v4

--- a/solution.py
+++ b/solution.py
@@ -10,6 +10,8 @@
 TILE_ROWS = 512
 PANEL = 32
 SUBLANES = 8
+TURNS = 4
+PLANE_BLOCKS = 7
 HIGHEST = lax.Precision.HIGHEST
 VMEM_BYTES = 48 * 1024 * 1024
 
@@ -28,7 +30,15 @@
     return dot(a[0], b[0]) + (dot(a[0], b[1]) + dot(a[1], b[0]))
 
 
-def prepare(place_ref, right_hbm, factor_hbm, diag_hbm, out_ref, right, factor, diag, scratch, arrived):
+def place_of(block_row, block_col):
+    turn = block_row // 2
+    count = block_col + block_row % 2 * 2 * turn
+    if count < PLANE_BLOCKS:
+        return turn, count
+    return TURNS - 1 - turn, count - PLANE_BLOCKS + 4 * (TURNS - 1 - turn) + 1
+
+
+def prepare(right_hbm, factor_hbm, diag_hbm, copies_ref, right, factor, diag, scratch, arrived):
     sources = ((diag_hbm, diag), (factor_hbm, factor), (right_hbm, right))
     copies = [pltpu.make_async_copy(source, target, arrived.at[i]) for i, (source, target) in enumerate(sources)]
     for copy in copies:
@@ -36,10 +46,39 @@
     for copy in copies:
         copy.wait()
     half = factor.shape[0]
-    chunk = out_ref.shape[0] - half
-    out_ref[:half] = contract(factor[...], diag[...], 1, 1)
+    chunk = copies_ref.shape[1] - half
+    scaled = contract(factor[...], diag[...], 1, 1)
     scratch[...] = contract(right[...], diag[...], 0, 1)
-    out_ref[half:] = scratch[pl.ds(pl.multiple_of(place_ref[0] * chunk, chunk), chunk), :]
+    rows = scratch[pl.ds(pl.multiple_of(lax.axis_index("col") * chunk, chunk), chunk), :]
+    for at in range(copies_ref.shape[0]):
+        copies_ref[at, :half] = scaled
+        copies_ref[at, half:] = rows
+
+
+def plane_index(turn, count, last):
+    return jnp.minimum(jnp.where(count < 2 * turn, count, count + (last + 1) // 2 - 2 * turn), last)
+
+
+def pick_excess(plane_ref, send_ref):
+    turn = lax.axis_index("row") // 2
+    half = send_ref.shape[1]
+    for at in range(send_ref.shape[0]):
+        send_ref[at] = plane_ref[plane_index(turn, at + PLANE_BLOCKS, plane_ref.shape[0] - 1), :half]
+
+
+def even_out(plane_ref, got_ref, out_ref):
+    turn = lax.axis_index("row") // 2
+    places, rows, _ = plane_ref.shape
+    half = got_ref.shape[1]
+    for at in range(PLANE_BLOCKS):
+        held = (turn >= TURNS // 2) | (at <= 4 * turn)
+        other = jnp.clip(at - 4 * turn - 1, 0, got_ref.shape[0] - 1)
+        own = plane_ref[plane_index(turn, at, places - 1), :half]
+        out_ref[at * half : (at + 1) * half] = jnp.where(held, own, got_ref[other])
+    start = PLANE_BLOCKS * half
+    chunk = rows - half
+    for at in range(places):
+        out_ref[start + at * chunk : start + (at + 1) * chunk] = plane_ref[at, half:]
 
 
 def factor_and_invert(work, size):
@@ -96,22 +135,23 @@
     work[...] = jnp.where(lower, work[...], 0.0)
 
 
-def block_solve(place_ref, own_ref, other_ref, low_ref, solved_ref, solved_t, work):
-    turns, planes, rows, size = own_ref.shape
-    blocks = turns * 2
-    quarter = size // 4
-    col, turn = place_ref[0], place_ref[1]
+def block_solve(own_ref, other_ref, low_ref, solved_ref, solved_t, work):
+    turns, _, size = own_ref.shape
+    blocks = solved_t.shape[0]
+    half_rows = size // 2
+    chunk = size // (2 * blocks)
+    col, row = lax.axis_index("col"), lax.axis_index("row")
     core = col % 2
 
-    def piece(block_row, block_col, half, start, stop):
-        slot = (turn - block_row // 2 + turns) % turns
-        at = block_row % 2 * blocks + block_col
-        own, other = own_ref[slot, at, start:stop, :], other_ref[slot, at, start:stop, :]
+    def rows_of(turn, half, start, count):
+        slot = (row // 2 - turn + turns) % turns
+        own, other = own_ref[slot, start : start + count, :], other_ref[slot, start : start + count, :]
         return jnp.where(core == half, own, other)
 
     current = []
     for i in range(blocks):
-        parts = [piece(i, j, half, quarter, rows) for j in range(blocks) for half in range(2)]
+        start = PLANE_BLOCKS * half_rows + i % 2 * blocks * chunk
+        parts = [rows_of(i // 2, half, start + j * chunk, chunk) for j in range(blocks) for half in range(2)]
         current.append(jnp.concatenate(parts, axis=0))
     for j in range(blocks):
         solved_t[j] = current[j]
@@ -120,10 +160,9 @@
             break
         solved_pair = split(current[j])
         for i in range(j + 1, blocks):
-            places = ((i, j), (blocks - 1 - i, blocks - 1 - j))
-            parts = [piece(*at, half, 0, quarter) for half in range(2) for at in places]
+            turn, slot = place_of(i, j)
+            parts = [rows_of(turn, half, slot * half_rows, half_rows) for half in range(2)]
             current[i] = current[i] - dot3(solved_pair, split(jnp.concatenate(parts, axis=0)))
-    half_rows = solved_ref.shape[0]
     work[...] = solved_t[col // 2].T
     solved_ref[...] = work[pl.ds(pl.multiple_of(core * half_rows, half_rows), half_rows), :]
 
@@ -141,8 +180,6 @@
 def local(right_side, factor_window, diag_inverse, phase_cov):
     row_count = lax.axis_size("row")
     col_count = lax.axis_size("col")
-    row_index = lax.axis_index("row")
-    col_index = lax.axis_index("col")
     block_rows = right_side.shape[0]
     rank_width = right_side.shape[1]
     col_width = factor_window.shape[1]
@@ -150,13 +187,12 @@
     turns = row_count // 2
     blocks = col_count // 2
     vmem = pl.BlockSpec(memory_space=pltpu.VMEM)
-    smem = pl.BlockSpec(memory_space=pltpu.SMEM)
     params = pltpu.CompilerParams(vmem_limit_bytes=VMEM_BYTES)
-    place = jnp.stack([col_index, row_index // 2]).astype(jnp.int32)
-    piece = pl.pallas_call(
+    piece_rows = col_width + chunk
+    copies = pl.pallas_call(
         prepare,
-        out_shape=jax.ShapeDtypeStruct((col_width + chunk, block_rows), jnp.float32),
-        in_specs=[smem] + [pl.BlockSpec(memory_space=pltpu.HBM)] * 3,
+        out_shape=jax.ShapeDtypeStruct((2 * blocks, piece_rows, block_rows), jnp.float32),
+        in_specs=[pl.BlockSpec(memory_space=pltpu.HBM)] * 3,
         out_specs=vmem,
         scratch_shapes=[
             pltpu.VMEM(right_side.shape, jnp.float32),
@@ -166,32 +202,36 @@
             pltpu.SemaphoreType.DMA((3,)),
         ],
         compiler_params=pltpu.CompilerParams(vmem_limit_bytes=64 * 1024 * 1024 - 128 * 1024),
-    )(place, right_side, factor_window.T, diag_inverse)
-    quarter = col_width // 2
+    )(right_side, factor_window.T, diag_inverse)
 
     def device(row, col):
         return row * col_count + col
 
-    fold = [
-        (device(row, 2 * j + core), device(row_count - 1 - row, 2 * (blocks - 1 - j) + core))
-        for row in range(row_count)
-        for j in range(row)
-        for core in range(2)
-    ]
-    folded = lax.ppermute(piece[quarter:col_width], ("row", "col"), fold)
-    kept = jnp.where(col_index // 2 < row_index, piece[:quarter], folded)
-    message = jnp.concatenate([kept, piece[col_width:]], axis=0)
     planes = [
         [device(2 * turn + low_bit, 2 * j + core) for low_bit in range(2) for j in range(blocks)]
         for turn in range(turns)
         for core in range(2)
     ]
-    copies = jnp.broadcast_to(message[None], (2 * blocks,) + message.shape)
     plane = lax.all_to_all(copies, ("row", "col"), 0, 0, axis_index_groups=planes, tiled=True)
     tile_count = phase_cov.shape[1] // TILE_ROWS
     cut = jnp.transpose(phase_cov.reshape(col_width, tile_count, TILE_ROWS), (1, 0, 2)).astype(jnp.float32)
-    plane, cut = lax.optimization_barrier((plane, cut))
+    excess = pl.pallas_call(
+        pick_excess,
+        out_shape=jax.ShapeDtypeStruct((PLANE_BLOCKS - 1, col_width, block_rows), jnp.float32),
+        in_specs=[vmem],
+        out_specs=vmem,
+        compiler_params=params,
+    )(plane)
+    excess, cut = lax.optimization_barrier((excess, cut))
     phase = lax.all_to_all(cut, "col", 0, 0, tiled=True).reshape(col_count * col_width, TILE_ROWS)
+    got = lax.ppermute(excess, "row", [(row, 2 * (turns - 1 - row // 2) + row % 2) for row in range(row_count)])
+    plane = pl.pallas_call(
+        even_out,
+        out_shape=jax.ShapeDtypeStruct((PLANE_BLOCKS * col_width + 2 * blocks * chunk, block_rows), jnp.float32),
+        in_specs=[vmem, vmem],
+        out_specs=vmem,
+        compiler_params=params,
+    )(plane, got)
     slots = [plane]
     for step in range(1, turns):
         turn_on = [(2 * turn + bit, 2 * ((turn + step) % turns) + bit) for turn in range(turns) for bit in range(2)]
@@ -204,7 +244,7 @@
             jax.ShapeDtypeStruct((rank_width, row_count * block_rows), jnp.bfloat16),
             jax.ShapeDtypeStruct((col_width, rank_width), jnp.float32),
         ],
-        in_specs=[smem, vmem, vmem],
+        in_specs=[vmem, vmem],
         out_specs=[vmem, vmem],
         scratch_shapes=[
             pltpu.VMEM((row_count, rank_width, block_rows), jnp.float32),
@@ -212,7 +252,7 @@
         ],
         compiler_params=params,
         cost_estimate=pl.CostEstimate(flops=800_000_000, bytes_accessed=3_000_000, transcendentals=0),
-    )(place, own, other)
+    )(own, other)
     basis = pl.pallas_call(
         tile_basis,
         out_shape=jax.ShapeDtypeStruct((TILE_ROWS, rank_width), jnp.float32),

time: 86.7 us -> 79.8 us (0.920)
  starting transfers between devices: 27.1 us -> 23.4 us
  blocking collectives: 12.6 us -> 15.7 us
  local copies, waits for them, and re-layouts: 4.5 us -> 2.25 us
  waiting for transfers between devices: 29.3 us -> 27.8 us
  other arithmetic: 1.55 us -> 0.21 us
  Pallas kernels: 10.4 us -> 9.45 us
    all_to_all x1, starting transfers between devices: 17 us -> 8.75 us  [local(): lax.all_to_all(copies, ('row', 'col'), 0, 0, axis_index_groups=planes, ti...]
    ppermute x1, waiting for transfers between devices: 0.01 us -> 4.93 us  [local(): lax.ppermute(excess, 'row', [(row, 2 * (turns - 1 - row // 2) + row % 2)...]
    ppermute x3, waiting for transfers between devices: 17.2 us -> 12.4 us  [local(): slots.append(lax.ppermute(plane, 'row', turn_on))]
    all_to_all x1, waiting for transfers between devices: 3.12 us -> 0.01 us  [local(): lax.all_to_all(cut, 'col', 0, 0, tiled=True)]
    all_to_all x1, blocking collectives: 12.6 us -> 15.7 us  [local(): return (lax.all_to_all(basis, 'col', 0, 0, tiled=True), solved)]
    ppermute x1, starting transfers between devices: 0.65 us -> 2.48 us  [local(): lax.ppermute(excess, 'row', [(row, 2 * (turns - 1 - row // 2) + row % 2)...]
    all_to_all x1, waiting for transfers between devices: 6.26 us -> 7.99 us  [local(): lax.all_to_all(copies, ('row', 'col'), 0, 0, axis_index_groups=planes, ti...]
    slice x2 -> x0, local copies, waits for them, and re-layouts: 1.5 us -> none  [the longest x1 0.81 us: local(): folded = lax.ppermute(piece[quarter:col_width], ('row', 'col'), fold)]
  transfers between devices with their start and end apart: 7 -> 7, of which waited for: 6 -> 6; matrix products, arithmetic and copies ran while one was open for 3% -> 2% of each run, Pallas kernels for 3% -> 2%
where the time goes in v7:
time: 79.8 us; the launch traced here: 79.5 us
  waiting for transfers between devices  27.8 us (35%)
  starting transfers between devices  23.4 us (29%)
  blocking collectives  15.7 us (20%)
  Pallas kernels  9.45 us (12%)
  local copies, waits for them, and re-layouts  2.25 us (3%)
    all_to_all x1, blocking collectives, local(): return (lax.all_to_all(basis, 'col', 0, 0, tiled=True), solved)  15.7 us
    ppermute x3, waiting for transfers between devices, local(): slots.append(lax.ppermute(plane, 'row', turn_on))  12.4 us
    all_to_all x1, starting transfers between devices, local(): lax.all_to_all(copies, ('row', 'col'), 0, 0, axis_index_groups=planes, ti...  8.75 us
    all_to_all x1, waiting for transfers between devices, local(): lax.all_to_all(copies, ('row', 'col'), 0, 0, axis_index_groups=planes, ti...  7.99 us
    all_to_all x1, starting transfers between devices, local(): lax.all_to_all(cut, 'col', 0, 0, tiled=True)  6.47 us
    pallas_call x1, Pallas kernels, local(): pl.pallas_call(tile_basis, out_shape=jax.ShapeDtypeStruct((TILE_ROWS, ran...  5.35 us
    ppermute x1, waiting for transfers between devices, local(): lax.ppermute(excess, 'row', [(row, 2 * (turns - 1 - row // 2) + row % 2)...  4.93 us
    ppermute x3, starting transfers between devices, local(): slots.append(lax.ppermute(plane, 'row', turn_on))  3.73 us
  transfers between devices with their start and end apart: 7, of which 6 were waited for; matrix products, arithmetic and copies ran while one was open for 2% of the time, Pallas kernels for 2%

profile of v7, /device:TPU:1, one launch (start us, length us, event | category | flops | bytes accessed | tf_op | source)
XLA Modules:
  0.0 79.5 jit_solution(5880462864718136888)
XLA Ops:
  0.6 2.1 %shard_map.59 = f32[16,72,128]{2,1,0:T(8,128)} custom-call(f32[128,128]{1,0:T(8,128)} %right_hbm.1, f32[64,128]{1,0:T(8,128)} %bitcast.22, f32[128,128]{1,0:T(8,128)} %diag_hbm.1), custom_call_target="tpu_custom_call" | custom-call | tf_op jit(solution)/shard_map/pallas_call | solution.py:192
  2.8 0.0 copy-start
  2.8 8.7 %all-to-all-start = ((f32[16,72,128]{2,1,0:T(8,128)}), f32[16,72,128]{2,1,0:T(8,128)S(1)}, u32[]{:S(2)}, u32[]{:S(2)}) async-start(f32[16,72,128]{2,1,0:T(8,128)} %shard_map.59), calls=%async_computation | async-start | bytes 1179648 | tf_op jit(solution)/shard_map/all_to_all | solution.py:215
  11.5 0.0 copy-done
  11.5 0.1 convert_element_type.13
  11.7 1.5 %copy.9 = f32[8,16,8,512]{3,2,0,1:T(8,128)} copy(f32[8,16,8,512]{3,2,1,0:T(8,128)S(1)} %bitcast.18) | data formatting | bytes 4194304 | tf_op jit(solution)/shard_map/convert_element_type | solution.py:217
  13.2 8.0 %all-to-all-done.plane_ref = f32[16,72,128]{2,1,0:T(8,128)S(1)} async-done(((f32[16,72,128]{2,1,0:T(8,128)}), f32[16,72,128]{2,1,0:T(8,128)S(1)}, u32[]{:S(2)}, u32[]{:S(2)}) %all-to-all-start) | async-done | bytes 589856 | tf_op jit(solution)/shard_map/all_to_all | solution.py:215
  21.2 6.5 %all-to-all-start.1 = ((f32[16,64,512]{2,1,0:T(8,128)}), f32[16,64,512]{2,1,0:T(8,128)S(1)}, u32[]{:S(2)}, u32[]{:S(2)}) async-start(f32[16,64,512]{2,1,0:T(8,128)} %bitcast.17), calls=%async_computation.1 | async-start | bytes 4194304 | tf_op jit(solution)/shard_map/all_to_all | solution.py:226
  27.7 2.5 %collective-permute-start = (f32[6,64,128]{2,1,0:T(8,128)S(1)}, f32[6,64,128]{2,1,0:T(8,128)S(1)}, u32[]{:S(2)}, u32[]{:S(2)}) collective-permute-start(f32[6,64,128]{2,1,0:T(8,128)S(1)} %shard_map.60), channel_id=1, source_target_pairs={{0,96},{16,112},{32,64},{48,80},{64,32},{80,48},{96,0},{112,16},{1... | collective-permute-start | bytes 589832 | tf_op jit(solution)/shard_map/ppermute | solution.py:227
  30.2 4.9 %collective-permute-done.got_ref = f32[6,64,128]{2,1,0:T(8,128)S(1)} collective-permute-done((f32[6,64,128]{2,1,0:T(8,128)S(1)}, f32[6,64,128]{2,1,0:T(8,128)S(1)}, u32[]{:S(2)}, u32[]{:S(2)}) %collective-permute-start) | collective-permute-done | bytes 196640 | tf_op jit(solution)/shard_map/ppermute | solution.py:227
  35.2 0.1 collective-permute-start.1
  35.2 3.6 %collective-permute-start.2 = (f32[576,128]{1,0:T(8,128)S(1)}, f32[576,128]{1,0:T(8,128)S(1)}, u32[]{:S(2)}, u32[]{:S(2)}) collective-permute-start(f32[576,128]{1,0:T(8,128)S(1)} %shard_map.61), channel_id=1, source_target_pairs={{0,64},{16,80},{32,96},{48,112},{64,0},{80,16},{96,32},{112,48},{1... | collective-permute-start | bytes 884744 | tf_op jit(solution)/shard_map/ppermute | solution.py:238
  38.9 0.0 collective-permute-start.3
  38.9 4.9 %collective-permute-done.1 = f32[576,128]{1,0:T(8,128)S(1)} collective-permute-done((f32[576,128]{1,0:T(8,128)S(1)}, f32[576,128]{1,0:T(8,128)S(1)}, u32[]{:S(2)}, u32[]{:S(2)}) %collective-permute-start.1) | collective-permute-done | bytes 294944 | tf_op jit(solution)/shard_map/ppermute | solution.py:238
  43.8 7.3 %collective-permute-done.2 = f32[576,128]{1,0:T(8,128)S(1)} collective-permute-done((f32[576,128]{1,0:T(8,128)S(1)}, f32[576,128]{1,0:T(8,128)S(1)}, u32[]{:S(2)}, u32[]{:S(2)}) %collective-permute-start.2) | collective-permute-done | bytes 294944 | tf_op jit(solution)/shard_map/ppermute | solution.py:238
  51.1 0.1 collective-permute-done.3
  51.2 0.1 pad_maximum_fusion.own_ref
  51.3 2.0 %collective-permute-start.4 = (f32[4,576,128]{2,1,0:T(8,128)S(1)}, f32[4,576,128]{2,1,0:T(8,128)S(1)}, u32[]{:S(2)}, u32[]{:S(2)}) collective-permute-start(f32[4,576,128]{2,1,0:T(8,128)S(1)} %pad_maximum_fusion.own_ref), channel_id=1, source_target_pairs={{0,1},{1,0},{2,3},{3,2},{4,5},{5,4},{6,7},{7,6},{8,9},{9,8},{10,11... | collective-permute-start | bytes 3538952 | tf_op jit(solution)/shard_map/ppermute | solution.py:240
  53.3 2.5 %collective-permute-done.4.other_ref = f32[4,576,128]{2,1,0:T(8,128)S(1)} collective-permute-done((f32[4,576,128]{2,1,0:T(8,128)S(1)}, f32[4,576,128]{2,1,0:T(8,128)S(1)}, u32[]{:S(2)}, u32[]{:S(2)}) %collective-permute-start.4) | collective-permute-done | bytes 1179680 | tf_op jit(solution)/shard_map/ppermute | solution.py:240
  55.8 1.9 %shard_map.62 = (bf16[128,1024]{1,0:T(8,128)(2,1)S(1)}, f32[64,128]{1,0:T(8,128)}) custom-call(f32[4,576,128]{2,1,0:T(8,128)S(1)} %pad_maximum_fusion.own_ref, f32[4,576,128]{2,1,0:T(8,128)S(1)} %collective-permute-done.4.other_ref), custom_call_target="tpu_custom_call" | custom-call | flops 800000000 | bytes 3000000 | tf_op jit(solution)/shard_map/pallas_call | solution.py:241
  57.7 0.0 all-to-all-done.1
  57.7 5.4 %shard_map.63 = f32[512,128]{1,0:T(8,128)S(1)} custom-call(bf16[128,1024]{1,0:T(8,128)(2,1)S(1)} %get-tuple-element.7.low_ref, f32[1024,512]{1,0:T(8,128)S(1)} %bitcast.14), custom_call_target="tpu_custom_call" | custom-call | flops 1000000000 | bytes 3000000 | tf_op jit(solution)/shard_map/pallas_call | solution.py:256
  63.1 15.7 %all_to_all.15 = f32[16,32,128]{2,1,0:T(8,128)S(1)} all-to-all(f32[16,32,128]{2,1,0:T(8,128)S(1)} %bitcast.16), channel_id=1, replica_groups=mesh['row'=8,'col'=16] {'col'}, dimensions={0} | all-to-all | bytes 524288 | tf_op jit(solution)/shard_map/all_to_all | solution.py:266
  78.8 0.7 copy.11
  (2 shorter events, 0.1 us)
Async XLA Ops:
  2.8 8.8 %copy-start = (bf16[64,8192]{1,0:T(8,128)(2,1)S(1)}, bf16[64,8192]{1,0:T(8,128)(2,1)}, u32[]{:S(2)}) copy-start(bf16[64,8192]{1,0:T(8,128)(2,1)} %param.7) | copy-start | bytes 3145732
  2.8 18.4 %all-to-all-start = ((f32[16,72,128]{2,1,0:T(8,128)}), f32[16,72,128]{2,1,0:T(8,128)S(1)}, u32[]{:S(2)}, u32[]{:S(2)}) async-start(f32[16,72,128]{2,1,0:T(8,128)} %shard_map.59), calls=%async_computation | async-start | bytes 1179648 | tf_op jit(solution)/shard_map/all_to_all | solution.py:215
  21.2 36.5 %all-to-all-start.1 = ((f32[16,64,512]{2,1,0:T(8,128)}), f32[16,64,512]{2,1,0:T(8,128)S(1)}, u32[]{:S(2)}, u32[]{:S(2)}) async-start(f32[16,64,512]{2,1,0:T(8,128)} %bitcast.17), calls=%async_computation.1 | async-start | bytes 4194304 | tf_op jit(solution)/shard_map/all_to_all | solution.py:226
  27.7 7.4 %collective-permute-start = (f32[6,64,128]{2,1,0:T(8,128)S(1)}, f32[6,64,128]{2,1,0:T(8,128)S(1)}, u32[]{:S(2)}, u32[]{:S(2)}) collective-permute-start(f32[6,64,128]{2,1,0:T(8,128)S(1)} %shard_map.60), channel_id=1, source_target_pairs={{0,96},{16,112},{32,64},{48,80},{64,32},{80,48},{96,0},{112,16},{1... | collective-permute-start | bytes 589832 | tf_op jit(solution)/shard_map/ppermute | solution.py:227
  35.2 8.7 %collective-permute-start.1 = (f32[576,128]{1,0:T(8,128)S(1)}, f32[576,128]{1,0:T(8,128)S(1)}, u32[]{:S(2)}, u32[]{:S(2)}) collective-permute-start(f32[576,128]{1,0:T(8,128)S(1)} %shard_map.61), channel_id=1, source_target_pairs={{0,32},{16,48},{32,64},{48,80},{64,96},{80,112},{96,0},{112,16},{1... | collective-permute-start | bytes 884744 | tf_op jit(solution)/shard_map/ppermute | solution.py:238
  35.2 15.9 %collective-permute-start.2 = (f32[576,128]{1,0:T(8,128)S(1)}, f32[576,128]{1,0:T(8,128)S(1)}, u32[]{:S(2)}, u32[]{:S(2)}) collective-permute-start(f32[576,128]{1,0:T(8,128)S(1)} %shard_map.61), channel_id=1, source_target_pairs={{0,64},{16,80},{32,96},{48,112},{64,0},{80,16},{96,32},{112,48},{1... | collective-permute-start | bytes 884744 | tf_op jit(solution)/shard_map/ppermute | solution.py:238
  38.9 12.4 %collective-permute-start.3 = (f32[576,128]{1,0:T(8,128)S(1)}, f32[576,128]{1,0:T(8,128)S(1)}, u32[]{:S(2)}, u32[]{:S(2)}) collective-permute-start(f32[576,128]{1,0:T(8,128)S(1)} %shard_map.61), channel_id=1, source_target_pairs={{0,96},{16,112},{32,0},{48,16},{64,32},{80,48},{96,64},{112,80},{1... | collective-permute-start | bytes 884744 | tf_op jit(solution)/shard_map/ppermute | solution.py:238
  51.3 4.5 %collective-permute-start.4 = (f32[4,576,128]{2,1,0:T(8,128)S(1)}, f32[4,576,128]{2,1,0:T(8,128)S(1)}, u32[]{:S(2)}, u32[]{:S(2)}) collective-permute-start(f32[4,576,128]{2,1,0:T(8,128)S(1)} %pad_maximum_fusion.own_ref), channel_id=1, source_target_pairs={{0,1},{1,0},{2,3},{3,2},{4,5},{5,4},{6,7},{7,6},{8,9},{9,8},{10,11... | collective-permute-start | bytes 3538952 | tf_op jit(solution)/shard_map/ppermute | solution.py:240

commit v8 on v7

--- a/solution.py
+++ b/solution.py
@@ -251,7 +251,7 @@
             pltpu.VMEM((rank_width, block_rows), jnp.float32),
         ],
         compiler_params=params,
-        cost_estimate=pl.CostEstimate(flops=800_000_000, bytes_accessed=3_000_000, transcendentals=0),
+        cost_estimate=pl.CostEstimate(flops=2_400_000_000, bytes_accessed=3_000_000, transcendentals=0),
     )(own, other)
     basis = pl.pallas_call(
         tile_basis,

time: 79.8 us -> 78 us (0.977)
  blocking collectives: 15.7 us -> 12.5 us
  waiting for transfers between devices: 27.8 us -> 29.9 us
  starting transfers between devices: 23.4 us -> 22.6 us
    all_to_all x1, waiting for transfers between devices: 0.01 us -> 6.27 us  [local(): lax.all_to_all(cut, 'col', 0, 0, tiled=True)]
    ppermute x1, waiting for transfers between devices: 4.93 us -> 0.01 us  [local(): lax.ppermute(excess, 'row', [(row, 2 * (turns - 1 - row // 2) + row % 2)...]
    all_to_all x1, blocking collectives: 15.7 us -> 12.5 us  [local(): return (lax.all_to_all(basis, 'col', 0, 0, tiled=True), solved)]
    ppermute x3, starting transfers between devices: 3.73 us -> 2.74 us  [local(): slots.append(lax.ppermute(plane, 'row', turn_on))]
    ppermute x3, waiting for transfers between devices: 12.4 us -> 13.2 us  [local(): slots.append(lax.ppermute(plane, 'row', turn_on))]
  transfers between devices with their start and end apart: 7 -> 7, of which waited for: 6 -> 5; matrix products, arithmetic and copies ran while one was open for 2% -> 2% of each run, Pallas kernels for 2% -> 3%
where the time goes in v8:
time: 78 us; the launch traced here: 77.6 us
  waiting for transfers between devices  29.9 us (38%)
  starting transfers between devices  22.6 us (29%)
  blocking collectives  12.5 us (16%)
  Pallas kernels  9.47 us (12%)
  local copies, waits for them, and re-layouts  2.25 us (3%)
    ppermute x3, waiting for transfers between devices, local(): slots.append(lax.ppermute(plane, 'row', turn_on))  13.2 us
    all_to_all x1, blocking collectives, local(): return (lax.all_to_all(basis, 'col', 0, 0, tiled=True), solved)  12.5 us
    all_to_all x1, starting transfers between devices, local(): lax.all_to_all(copies, ('row', 'col'), 0, 0, axis_index_groups=planes, ti...  8.75 us
    all_to_all x1, waiting for transfers between devices, local(): lax.all_to_all(copies, ('row', 'col'), 0, 0, axis_index_groups=planes, ti...  7.99 us
    all_to_all x1, starting transfers between devices, local(): lax.all_to_all(cut, 'col', 0, 0, tiled=True)  6.74 us
    all_to_all x1, waiting for transfers between devices, local(): lax.all_to_all(cut, 'col', 0, 0, tiled=True)  6.27 us
    pallas_call x1, Pallas kernels, local(): pl.pallas_call(tile_basis, out_shape=jax.ShapeDtypeStruct((TILE_ROWS, ran...  5.35 us
    ppermute x3, starting transfers between devices, local(): slots.append(lax.ppermute(plane, 'row', turn_on))  2.74 us
  transfers between devices with their start and end apart: 7, of which 5 were waited for; matrix products, arithmetic and copies ran while one was open for 2% of the time, Pallas kernels for 3%

profile of v8, /device:TPU:1, one launch (start us, length us, event | category | flops | bytes accessed | tf_op | source)
XLA Modules:
  0.0 77.6 jit_solution(14406297114688668006)
XLA Ops:
  0.6 2.1 %shard_map.59 = f32[16,72,128]{2,1,0:T(8,128)} custom-call(f32[128,128]{1,0:T(8,128)} %right_hbm.1, f32[64,128]{1,0:T(8,128)} %bitcast.22, f32[128,128]{1,0:T(8,128)} %diag_hbm.1), custom_call_target="tpu_custom_call" | custom-call | tf_op jit(solution)/shard_map/pallas_call | solution.py:192
  2.8 0.0 copy-start
  2.8 8.7 %all-to-all-start = ((f32[16,72,128]{2,1,0:T(8,128)}), f32[16,72,128]{2,1,0:T(8,128)S(1)}, u32[]{:S(2)}, u32[]{:S(2)}) async-start(f32[16,72,128]{2,1,0:T(8,128)} %shard_map.59), calls=%async_computation | async-start | bytes 1179648 | tf_op jit(solution)/shard_map/all_to_all | solution.py:215
  11.5 0.0 copy-done
  11.5 0.1 convert_element_type.13
  11.7 1.5 %copy.9 = f32[8,16,8,512]{3,2,0,1:T(8,128)} copy(f32[8,16,8,512]{3,2,1,0:T(8,128)S(1)} %bitcast.18) | data formatting | bytes 4194304 | tf_op jit(solution)/shard_map/convert_element_type | solution.py:217
  13.2 8.0 %all-to-all-done.plane_ref = f32[16,72,128]{2,1,0:T(8,128)S(1)} async-done(((f32[16,72,128]{2,1,0:T(8,128)}), f32[16,72,128]{2,1,0:T(8,128)S(1)}, u32[]{:S(2)}, u32[]{:S(2)}) %all-to-all-start) | async-done | bytes 589856 | tf_op jit(solution)/shard_map/all_to_all | solution.py:215
  21.2 2.6 %collective-permute-start = (f32[6,64,128]{2,1,0:T(8,128)S(1)}, f32[6,64,128]{2,1,0:T(8,128)S(1)}, u32[]{:S(2)}, u32[]{:S(2)}) collective-permute-start(f32[6,64,128]{2,1,0:T(8,128)S(1)} %shard_map.60), channel_id=1, source_target_pairs={{0,96},{16,112},{32,64},{48,80},{64,32},{80,48},{96,0},{112,16},{1... | collective-permute-start | bytes 589832 | tf_op jit(solution)/shard_map/ppermute | solution.py:227
  23.8 6.7 %all-to-all-start.1 = ((f32[16,64,512]{2,1,0:T(8,128)}), f32[16,64,512]{2,1,0:T(8,128)S(1)}, u32[]{:S(2)}, u32[]{:S(2)}) async-start(f32[16,64,512]{2,1,0:T(8,128)} %bitcast.17), calls=%async_computation.1 | async-start | bytes 4194304 | tf_op jit(solution)/shard_map/all_to_all | solution.py:226
  30.5 0.0 collective-permute-done.got_ref
  30.5 0.1 shard_map.61
  30.6 0.1 collective-permute-start.1
  30.7 1.4 %collective-permute-start.2 = (f32[576,128]{1,0:T(8,128)S(1)}, f32[576,128]{1,0:T(8,128)S(1)}, u32[]{:S(2)}, u32[]{:S(2)}) collective-permute-start(f32[576,128]{1,0:T(8,128)S(1)} %shard_map.61), channel_id=1, source_target_pairs={{0,64},{16,80},{32,96},{48,112},{64,0},{80,16},{96,32},{112,48},{1... | collective-permute-start | bytes 884744 | tf_op jit(solution)/shard_map/ppermute | solution.py:238
  32.1 1.3 %collective-permute-start.3 = (f32[576,128]{1,0:T(8,128)S(1)}, f32[576,128]{1,0:T(8,128)S(1)}, u32[]{:S(2)}, u32[]{:S(2)}) collective-permute-start(f32[576,128]{1,0:T(8,128)S(1)} %shard_map.61), channel_id=1, source_target_pairs={{0,96},{16,112},{32,0},{48,16},{64,32},{80,48},{96,64},{112,80},{1... | collective-permute-start | bytes 884744 | tf_op jit(solution)/shard_map/ppermute | solution.py:238
  33.3 12.8 %collective-permute-done.1 = f32[576,128]{1,0:T(8,128)S(1)} collective-permute-done((f32[576,128]{1,0:T(8,128)S(1)}, f32[576,128]{1,0:T(8,128)S(1)}, u32[]{:S(2)}, u32[]{:S(2)}) %collective-permute-start.1) | collective-permute-done | bytes 294944 | tf_op jit(solution)/shard_map/ppermute | solution.py:238
  46.2 0.0 collective-permute-done.2
  46.2 0.3 collective-permute-done.3
  46.5 0.1 pad_maximum_fusion.own_ref
  46.6 1.8 %collective-permute-start.4 = (f32[4,576,128]{2,1,0:T(8,128)S(1)}, f32[4,576,128]{2,1,0:T(8,128)S(1)}, u32[]{:S(2)}, u32[]{:S(2)}) collective-permute-start(f32[4,576,128]{2,1,0:T(8,128)S(1)} %pad_maximum_fusion.own_ref), channel_id=1, source_target_pairs={{0,1},{1,0},{2,3},{3,2},{4,5},{5,4},{6,7},{7,6},{8,9},{9,8},{10,11... | collective-permute-start | bytes 3538952 | tf_op jit(solution)/shard_map/ppermute | solution.py:240
  48.4 2.5 %collective-permute-done.4.other_ref = f32[4,576,128]{2,1,0:T(8,128)S(1)} collective-permute-done((f32[4,576,128]{2,1,0:T(8,128)S(1)}, f32[4,576,128]{2,1,0:T(8,128)S(1)}, u32[]{:S(2)}, u32[]{:S(2)}) %collective-permute-start.4) | collective-permute-done | bytes 1179680 | tf_op jit(solution)/shard_map/ppermute | solution.py:240
  50.9 1.9 %shard_map.62 = (bf16[128,1024]{1,0:T(8,128)(2,1)S(1)}, f32[64,128]{1,0:T(8,128)}) custom-call(f32[4,576,128]{2,1,0:T(8,128)S(1)} %pad_maximum_fusion.own_ref, f32[4,576,128]{2,1,0:T(8,128)S(1)} %collective-permute-done.4.other_ref), custom_call_target="tpu_custom_call" | custom-call | flops 2400000000 | bytes 3000000 | tf_op jit(solution)/shard_map/pallas_call | solution.py:241
  52.8 6.3 %all-to-all-done.1 = f32[16,64,512]{2,1,0:T(8,128)S(1)} async-done(((f32[16,64,512]{2,1,0:T(8,128)}), f32[16,64,512]{2,1,0:T(8,128)S(1)}, u32[]{:S(2)}, u32[]{:S(2)}) %all-to-all-start.1) | async-done | bytes 2097184 | tf_op jit(solution)/shard_map/all_to_all | solution.py:226
  59.1 5.4 %shard_map.63 = f32[512,128]{1,0:T(8,128)S(1)} custom-call(bf16[128,1024]{1,0:T(8,128)(2,1)S(1)} %get-tuple-element.7.low_ref, f32[1024,512]{1,0:T(8,128)S(1)} %bitcast.14), custom_call_target="tpu_custom_call" | custom-call | flops 1000000000 | bytes 3000000 | tf_op jit(solution)/shard_map/pallas_call | solution.py:256
  64.4 12.5 %all_to_all.15 = f32[16,32,128]{2,1,0:T(8,128)S(1)} all-to-all(f32[16,32,128]{2,1,0:T(8,128)S(1)} %bitcast.16), channel_id=1, replica_groups=mesh['row'=8,'col'=16] {'col'}, dimensions={0} | all-to-all | bytes 524288 | tf_op jit(solution)/shard_map/all_to_all | solution.py:266
  76.9 0.7 copy.11
  (1 shorter events, 0.0 us)
Async XLA Ops:
  2.8 8.8 %copy-start = (bf16[64,8192]{1,0:T(8,128)(2,1)S(1)}, bf16[64,8192]{1,0:T(8,128)(2,1)}, u32[]{:S(2)}) copy-start(bf16[64,8192]{1,0:T(8,128)(2,1)} %param.7) | copy-start | bytes 3145732
  2.8 18.4 %all-to-all-start = ((f32[16,72,128]{2,1,0:T(8,128)}), f32[16,72,128]{2,1,0:T(8,128)S(1)}, u32[]{:S(2)}, u32[]{:S(2)}) async-start(f32[16,72,128]{2,1,0:T(8,128)} %shard_map.59), calls=%async_computation | async-start | bytes 1179648 | tf_op jit(solution)/shard_map/all_to_all | solution.py:215
  21.2 9.3 %collective-permute-start = (f32[6,64,128]{2,1,0:T(8,128)S(1)}, f32[6,64,128]{2,1,0:T(8,128)S(1)}, u32[]{:S(2)}, u32[]{:S(2)}) collective-permute-start(f32[6,64,128]{2,1,0:T(8,128)S(1)} %shard_map.60), channel_id=1, source_target_pairs={{0,96},{16,112},{32,64},{48,80},{64,32},{80,48},{96,0},{112,16},{1... | collective-permute-start | bytes 589832 | tf_op jit(solution)/shard_map/ppermute | solution.py:227
  23.8 35.3 %all-to-all-start.1 = ((f32[16,64,512]{2,1,0:T(8,128)}), f32[16,64,512]{2,1,0:T(8,128)S(1)}, u32[]{:S(2)}, u32[]{:S(2)}) async-start(f32[16,64,512]{2,1,0:T(8,128)} %bitcast.17), calls=%async_computation.1 | async-start | bytes 4194304 | tf_op jit(solution)/shard_map/all_to_all | solution.py:226
  30.6 15.6 %collective-permute-start.1 = (f32[576,128]{1,0:T(8,128)S(1)}, f32[576,128]{1,0:T(8,128)S(1)}, u32[]{:S(2)}, u32[]{:S(2)}) collective-permute-start(f32[576,128]{1,0:T(8,128)S(1)} %shard_map.61), channel_id=1, source_target_pairs={{0,32},{16,48},{32,64},{48,80},{64,96},{80,112},{96,0},{112,16},{1... | collective-permute-start | bytes 884744 | tf_op jit(solution)/shard_map/ppermute | solution.py:238
  30.7 15.5 %collective-permute-start.2 = (f32[576,128]{1,0:T(8,128)S(1)}, f32[576,128]{1,0:T(8,128)S(1)}, u32[]{:S(2)}, u32[]{:S(2)}) collective-permute-start(f32[576,128]{1,0:T(8,128)S(1)} %shard_map.61), channel_id=1, source_target_pairs={{0,64},{16,80},{32,96},{48,112},{64,0},{80,16},{96,32},{112,48},{1... | collective-permute-start | bytes 884744 | tf_op jit(solution)/shard_map/ppermute | solution.py:238
  32.1 14.5 %collective-permute-start.3 = (f32[576,128]{1,0:T(8,128)S(1)}, f32[576,128]{1,0:T(8,128)S(1)}, u32[]{:S(2)}, u32[]{:S(2)}) collective-permute-start(f32[576,128]{1,0:T(8,128)S(1)} %shard_map.61), channel_id=1, source_target_pairs={{0,96},{16,112},{32,0},{48,16},{64,32},{80,48},{96,64},{112,80},{1... | collective-permute-start | bytes 884744 | tf_op jit(solution)/shard_map/ppermute | solution.py:238
  46.6 4.3 %collective-permute-start.4 = (f32[4,576,128]{2,1,0:T(8,128)S(1)}, f32[4,576,128]{2,1,0:T(8,128)S(1)}, u32[]{:S(2)}, u32[]{:S(2)}) collective-permute-start(f32[4,576,128]{2,1,0:T(8,128)S(1)} %pad_maximum_fusion.own_ref), channel_id=1, source_target_pairs={{0,1},{1,0},{2,3},{3,2},{4,5},{5,4},{6,7},{7,6},{8,9},{9,8},{10,11... | collective-permute-start | bytes 3538952 | tf_op jit(solution)/shard_map/ppermute | solution.py:240

commit v9 on v8

--- a/solution.py
+++ b/solution.py
@@ -135,6 +135,27 @@
     work[...] = jnp.where(lower, work[...], 0.0)
 
 
+def cut_tiles(cov_ref, keep_ref, *give_refs):
+    count, _, width = keep_ref.shape
+    core = lax.axis_index("col") % 2
+    for at in range(count):
+        part = give_refs[0].shape[0]
+        for out_ref, place, there in ((keep_ref, at, core), (give_refs[at // part], at % part, 1 - core)):
+            tile = 2 * at + there
+            out_ref[place] = cov_ref[:, pl.ds(pl.multiple_of(tile * width, width), width)].astype(jnp.float32)
+
+
+def pair_rows(keep_ref, *refs):
+    rows = keep_ref.shape[1]
+    first = lax.axis_index("col") % 2 == 0
+    got_refs, out_ref = refs[:-1], refs[-1]
+    part = got_refs[0].shape[0]
+    for at in range(keep_ref.shape[0]):
+        keep, got = keep_ref[at], got_refs[at // part][at % part]
+        out_ref[at, :rows] = jnp.where(first, keep, got)
+        out_ref[at, rows:] = jnp.where(first, got, keep)
+
+
 def block_solve(own_ref, other_ref, low_ref, solved_ref, solved_t, work):
     turns, _, size = own_ref.shape
     blocks = solved_t.shape[0]
@@ -212,9 +233,25 @@
         for turn in range(turns)
         for core in range(2)
     ]
+    copies, cov = lax.optimization_barrier((copies, phase_cov))
     plane = lax.all_to_all(copies, ("row", "col"), 0, 0, axis_index_groups=planes, tiled=True)
-    tile_count = phase_cov.shape[1] // TILE_ROWS
-    cut = jnp.transpose(phase_cov.reshape(col_width, tile_count, TILE_ROWS), (1, 0, 2)).astype(jnp.float32)
+    cores = [(col, col ^ 1) for col in range(col_count)]
+    cut_shapes = [jax.ShapeDtypeStruct((blocks // part, col_width, TILE_ROWS), jnp.float32) for part in (1,) + (2,) * 2]
+    keep, *gives = pl.pallas_call(
+        cut_tiles,
+        out_shape=cut_shapes,
+        in_specs=[vmem],
+        out_specs=[vmem] * len(cut_shapes),
+        compiler_params=params,
+    )(cov)
+    cut = pl.pallas_call(
+        pair_rows,
+        out_shape=jax.ShapeDtypeStruct((blocks, 2 * col_width, TILE_ROWS), jnp.float32),
+        in_specs=[vmem] * len(cut_shapes),
+        out_specs=vmem,
+        compiler_params=params,
+    )(keep, *[lax.ppermute(give, "col", cores) for give in gives])
+    plane, cut = lax.optimization_barrier((plane, cut))
     excess = pl.pallas_call(
         pick_excess,
         out_shape=jax.ShapeDtypeStruct((PLANE_BLOCKS - 1, col_width, block_rows), jnp.float32),
@@ -223,7 +260,8 @@
         compiler_params=params,
     )(plane)
     excess, cut = lax.optimization_barrier((excess, cut))
-    phase = lax.all_to_all(cut, "col", 0, 0, tiled=True).reshape(col_count * col_width, TILE_ROWS)
+    groups = [[2 * j + core for j in range(blocks)] for core in range(2)]
+    phase = lax.all_to_all(cut, "col", 0, 0, axis_index_groups=groups, tiled=True).reshape(col_count * col_width, TILE_ROWS)
     got = lax.ppermute(excess, "row", [(row, 2 * (turns - 1 - row // 2) + row % 2) for row in range(row_count)])
     plane = pl.pallas_call(
         even_out,
@@ -237,7 +275,7 @@
         turn_on = [(2 * turn + bit, 2 * ((turn + step) % turns) + bit) for turn in range(turns) for bit in range(2)]
         slots.append(lax.ppermute(plane, "row", turn_on))
     own = jnp.stack(slots)
-    other = lax.ppermute(own, "col", [(col, col ^ 1) for col in range(col_count)])
+    other = lax.ppermute(own, "col", cores)
     low, solved = pl.pallas_call(
         block_solve,
         out_shape=[
@@ -251,7 +289,7 @@
             pltpu.VMEM((rank_width, block_rows), jnp.float32),
         ],
         compiler_params=params,
-        cost_estimate=pl.CostEstimate(flops=2_400_000_000, bytes_accessed=3_000_000, transcendentals=0),
+        cost_estimate=pl.CostEstimate(flops=1_600_000_000, bytes_accessed=3_000_000, transcendentals=0),
     )(own, other)
     basis = pl.pallas_call(
         tile_basis,

time: 78 us -> 75.6 us (0.969)
  waiting for transfers between devices: 29.9 us -> 27.6 us
  Pallas kernels: 9.47 us -> 11.1 us
  starting transfers between devices: 22.6 us -> 21 us
  blocking collectives: 12.5 us -> 14.1 us
  local copies, waits for them, and re-layouts: 2.25 us -> 0.71 us
    all_to_all x1, waiting for transfers between devices: 7.99 us -> 4.72 us  [local(): lax.all_to_all(copies, ('row', 'col'), 0, 0, axis_index_groups=planes, ti...]
    all_to_all x1, waiting for transfers between devices: 6.27 us -> 3.62 us  [local(): lax.all_to_all(cut, 'col', 0, 0, axis_index_groups=groups, tiled=True)]
    ppermute x1 -> x3, waiting for transfers between devices: 2.47 us -> 4.67 us  [the longest x1 2.47 us: local(): other = lax.ppermute(own, 'col', cores)]
    all_to_all x1, starting transfers between devices: 6.74 us -> 4.79 us  [local(): lax.all_to_all(cut, 'col', 0, 0, axis_index_groups=groups, tiled=True)]
    all_to_all x1, blocking collectives: 12.5 us -> 14.1 us  [local(): return (lax.all_to_all(basis, 'col', 0, 0, tiled=True), solved)]
    pallas_call x0 -> x2, Pallas kernels: none -> 1.63 us  [the longest x1 1.48 us: local(): pl.pallas_call(pair_rows, out_shape=jax.ShapeDtypeStruct((blocks, 2 * col...]
    convert_element_type x1 -> x0, local copies, waits for them, and re-layouts: 1.55 us -> none  [local(): jnp.transpose(phase_cov.reshape(col_width, tile_count, TILE_ROWS), (1, 0,...]
    ppermute x3, waiting for transfers between devices: 13.2 us -> 14.6 us  [local(): slots.append(lax.ppermute(plane, 'row', turn_on))]
  transfers between devices with their start and end apart: 7 -> 9, of which waited for: 5 -> 8; matrix products, arithmetic and copies ran while one was open for 2% -> 0% of each run, Pallas kernels for 3% -> 5%
where the time goes in v9:
time: 75.6 us; the launch traced here: 75.3 us
  waiting for transfers between devices  27.6 us (37%)
  starting transfers between devices  21 us (28%)
  blocking collectives  14.1 us (19%)
  Pallas kernels  11.1 us (15%)
    ppermute x3, waiting for transfers between devices, local(): slots.append(lax.ppermute(plane, 'row', turn_on))  14.6 us
    all_to_all x1, blocking collectives, local(): return (lax.all_to_all(basis, 'col', 0, 0, tiled=True), solved)  14.1 us
    all_to_all x1, starting transfers between devices, local(): lax.all_to_all(copies, ('row', 'col'), 0, 0, axis_index_groups=planes, ti...  8.75 us
    pallas_call x1, Pallas kernels, local(): pl.pallas_call(tile_basis, out_shape=jax.ShapeDtypeStruct((TILE_ROWS, ran...  5.35 us
    all_to_all x1, starting transfers between devices, local(): lax.all_to_all(cut, 'col', 0, 0, axis_index_groups=groups, tiled=True)  4.79 us
    all_to_all x1, waiting for transfers between devices, local(): lax.all_to_all(copies, ('row', 'col'), 0, 0, axis_index_groups=planes, ti...  4.72 us
    all_to_all x1, waiting for transfers between devices, local(): lax.all_to_all(cut, 'col', 0, 0, axis_index_groups=groups, tiled=True)  3.62 us
    ppermute x1, starting transfers between devices, local(): lax.ppermute(excess, 'row', [(row, 2 * (turns - 1 - row // 2) + row % 2)...  2.56 us
  transfers between devices with their start and end apart: 9, of which 8 were waited for; matrix products, arithmetic and copies ran while one was open for 0% of the time, Pallas kernels for 5%

profile of v9, /device:TPU:1, one launch (start us, length us, event | category | flops | bytes accessed | tf_op | source)
XLA Modules:
  0.0 75.3 jit_solution(1283817529191627239)
XLA Ops:
  0.6 2.1 %shard_map.59 = f32[16,72,128]{2,1,0:T(8,128)} custom-call(f32[128,128]{1,0:T(8,128)} %right_hbm.1, f32[64,128]{1,0:T(8,128)} %bitcast.13, f32[128,128]{1,0:T(8,128)} %diag_hbm.1), custom_call_target="tpu_custom_call" | custom-call | tf_op jit(solution)/shard_map/pallas_call | solution.py:213
  2.8 0.0 copy-start
  2.8 8.7 %all-to-all-start = ((f32[16,72,128]{2,1,0:T(8,128)}), f32[16,72,128]{2,1,0:T(8,128)S(1)}, u32[]{:S(2)}, u32[]{:S(2)}) async-start(f32[16,72,128]{2,1,0:T(8,128)} %shard_map.59), calls=%async_computation | async-start | bytes 1179648 | tf_op jit(solution)/shard_map/all_to_all | solution.py:237
  11.5 0.0 copy-done
  11.5 0.2 shard_map.60
  11.7 1.0 %collective-permute-start = (f32[4,64,512]{2,1,0:T(8,128)S(1)}, f32[4,64,512]{2,1,0:T(8,128)S(1)}, u32[]{:S(2)}, u32[]{:S(2)}) collective-permute-start(f32[4,64,512]{2,1,0:T(8,128)S(1)} %get-tuple-element.16), channel_id=1, source_target_pairs={{0,1},{1,0},{2,3},{3,2},{4,5},{5,4},{6,7},{7,6},{8,9},{9,8},{10,11... | collective-permute-start | bytes 1572872 | tf_op jit(solution)/shard_map/ppermute | solution.py:253
  12.7 0.1 collective-permute-start.1
  12.8 1.4 %collective-permute-done.refs_0_ = f32[4,64,512]{2,1,0:T(8,128)S(1)} collective-permute-done((f32[4,64,512]{2,1,0:T(8,128)S(1)}, f32[4,64,512]{2,1,0:T(8,128)S(1)}, u32[]{:S(2)}, u32[]{:S(2)}) %collective-permute-start) | collective-permute-done | bytes 524320 | tf_op jit(solution)/shard_map/ppermute | solution.py:253
  14.3 0.7 collective-permute-done.1.refs_1_
  15.0 1.5 %shard_map.61 = f32[8,128,512]{2,1,0:T(8,128)} custom-call(f32[8,64,512]{2,1,0:T(8,128)S(1)} %get-tuple-element.15.keep_ref, f32[4,64,512]{2,1,0:T(8,128)S(1)} %collective-permute-done.refs_0_, f32[4,64,512]{2,1,0:T(8,128)S(1)} %collective-permute-done.1.refs_1_), custom_call_target="tpu_custom_call" | custom-call | tf_op jit(solution)/shard_map/pallas_call | solution.py:247
  16.5 4.7 %all-to-all-done.plane_ref = f32[16,72,128]{2,1,0:T(8,128)S(1)} async-done(((f32[16,72,128]{2,1,0:T(8,128)}), f32[16,72,128]{2,1,0:T(8,128)S(1)}, u32[]{:S(2)}, u32[]{:S(2)}) %all-to-all-start) | async-done | bytes 589856 | tf_op jit(solution)/shard_map/all_to_all | solution.py:237
  21.2 2.6 %collective-permute-start.2 = (f32[6,64,128]{2,1,0:T(8,128)S(1)}, f32[6,64,128]{2,1,0:T(8,128)S(1)}, u32[]{:S(2)}, u32[]{:S(2)}) collective-permute-start(f32[6,64,128]{2,1,0:T(8,128)S(1)} %shard_map.62), channel_id=1, source_target_pairs={{0,96},{16,112},{32,64},{48,80},{64,32},{80,48},{96,0},{112,16},{1... | collective-permute-start | bytes 589832 | tf_op jit(solution)/shard_map/ppermute | solution.py:265
  23.8 4.8 %all-to-all-start.1 = ((f32[8,128,512]{2,1,0:T(8,128)}), f32[8,128,512]{2,1,0:T(8,128)S(1)}, u32[]{:S(2)}, u32[]{:S(2)}) async-start(f32[8,128,512]{2,1,0:T(8,128)} %shard_map.61), calls=%async_computation.1 | async-start | bytes 4194304 | tf_op jit(solution)/shard_map/all_to_all | solution.py:264
  28.6 0.0 collective-permute-done.2.got_ref
  28.6 0.1 shard_map.63
  28.7 1.0 %collective-permute-start.5 = (f32[576,128]{1,0:T(8,128)S(1)}, f32[576,128]{1,0:T(8,128)S(1)}, u32[]{:S(2)}, u32[]{:S(2)}) collective-permute-start(f32[576,128]{1,0:T(8,128)S(1)} %shard_map.63), channel_id=1, source_target_pairs={{0,96},{16,112},{32,0},{48,16},{64,32},{80,48},{96,64},{112,80},{1... | collective-permute-start | bytes 884744 | tf_op jit(solution)/shard_map/ppermute | solution.py:276
  29.7 0.8 %collective-permute-start.4 = (f32[576,128]{1,0:T(8,128)S(1)}, f32[576,128]{1,0:T(8,128)S(1)}, u32[]{:S(2)}, u32[]{:S(2)}) collective-permute-start(f32[576,128]{1,0:T(8,128)S(1)} %shard_map.63), channel_id=1, source_target_pairs={{0,64},{16,80},{32,96},{48,112},{64,0},{80,16},{96,32},{112,48},{1... | collective-permute-start | bytes 884744 | tf_op jit(solution)/shard_map/ppermute | solution.py:276
  30.5 0.0 collective-permute-start.3
  30.5 4.2 %collective-permute-done.5 = f32[576,128]{1,0:T(8,128)S(1)} collective-permute-done((f32[576,128]{1,0:T(8,128)S(1)}, f32[576,128]{1,0:T(8,128)S(1)}, u32[]{:S(2)}, u32[]{:S(2)}) %collective-permute-start.5) | collective-permute-done | bytes 294944 | tf_op jit(solution)/shard_map/ppermute | solution.py:276
  34.7 2.4 %collective-permute-done.4 = f32[576,128]{1,0:T(8,128)S(1)} collective-permute-done((f32[576,128]{1,0:T(8,128)S(1)}, f32[576,128]{1,0:T(8,128)S(1)}, u32[]{:S(2)}, u32[]{:S(2)}) %collective-permute-start.4) | collective-permute-done | bytes 294944 | tf_op jit(solution)/shard_map/ppermute | solution.py:276
  37.1 8.0 %collective-permute-done.3 = f32[576,128]{1,0:T(8,128)S(1)} collective-permute-done((f32[576,128]{1,0:T(8,128)S(1)}, f32[576,128]{1,0:T(8,128)S(1)}, u32[]{:S(2)}, u32[]{:S(2)}) %collective-permute-start.3) | collective-permute-done | bytes 294944 | tf_op jit(solution)/shard_map/ppermute | solution.py:276
  45.0 0.1 pad_maximum_fusion.own_ref
  45.1 1.9 %collective-permute-start.6 = (f32[4,576,128]{2,1,0:T(8,128)S(1)}, f32[4,576,128]{2,1,0:T(8,128)S(1)}, u32[]{:S(2)}, u32[]{:S(2)}) collective-permute-start(f32[4,576,128]{2,1,0:T(8,128)S(1)} %pad_maximum_fusion.own_ref), channel_id=1, source_target_pairs={{0,1},{1,0},{2,3},{3,2},{4,5},{5,4},{6,7},{7,6},{8,9},{9,8},{10,11... | collective-permute-start | bytes 3538952 | tf_op jit(solution)/shard_map/ppermute | solution.py:278
  47.1 2.5 %collective-permute-done.6.other_ref = f32[4,576,128]{2,1,0:T(8,128)S(1)} collective-permute-done((f32[4,576,128]{2,1,0:T(8,128)S(1)}, f32[4,576,128]{2,1,0:T(8,128)S(1)}, u32[]{:S(2)}, u32[]{:S(2)}) %collective-permute-start.6) | collective-permute-done | bytes 1179680 | tf_op jit(solution)/shard_map/ppermute | solution.py:278
  49.5 1.9 %shard_map.64 = (bf16[128,1024]{1,0:T(8,128)(2,1)S(1)}, f32[64,128]{1,0:T(8,128)}) custom-call(f32[4,576,128]{2,1,0:T(8,128)S(1)} %pad_maximum_fusion.own_ref, f32[4,576,128]{2,1,0:T(8,128)S(1)} %collective-permute-done.6.other_ref), custom_call_target="tpu_custom_call" | custom-call | flops 1600000000 | bytes 3000000 | tf_op jit(solution)/shard_map/pallas_call | solution.py:279
  51.5 3.6 %all-to-all-done.1 = f32[8,128,512]{2,1,0:T(8,128)S(1)} async-done(((f32[8,128,512]{2,1,0:T(8,128)}), f32[8,128,512]{2,1,0:T(8,128)S(1)}, u32[]{:S(2)}, u32[]{:S(2)}) %all-to-all-start.1) | async-done | bytes 2097184 | tf_op jit(solution)/shard_map/all_to_all | solution.py:264
  55.1 5.4 %shard_map.65 = f32[512,128]{1,0:T(8,128)S(1)} custom-call(bf16[128,1024]{1,0:T(8,128)(2,1)S(1)} %get-tuple-element.21.low_ref, f32[1024,512]{1,0:T(8,128)S(1)} %bitcast.7), custom_call_target="tpu_custom_call" | custom-call | flops 1000000000 | bytes 3000000 | tf_op jit(solution)/shard_map/pallas_call | solution.py:294
  60.4 14.1 %all_to_all.15 = f32[16,32,128]{2,1,0:T(8,128)S(1)} all-to-all(f32[16,32,128]{2,1,0:T(8,128)S(1)} %bitcast.9), channel_id=1, replica_groups=mesh['row'=8,'col'=16] {'col'}, dimensions={0} | all-to-all | bytes 524288 | tf_op jit(solution)/shard_map/all_to_all | solution.py:304
  74.6 0.7 copy.7
  (1 shorter events, 0.0 us)
Async XLA Ops:
  2.8 8.8 %copy-start = (bf16[64,8192]{1,0:T(8,128)(2,1)S(1)}, bf16[64,8192]{1,0:T(8,128)(2,1)}, u32[]{:S(2)}) copy-start(bf16[64,8192]{1,0:T(8,128)(2,1)} %cov_ref) | copy-start | bytes 3145732
  2.8 18.4 %all-to-all-start = ((f32[16,72,128]{2,1,0:T(8,128)}), f32[16,72,128]{2,1,0:T(8,128)S(1)}, u32[]{:S(2)}, u32[]{:S(2)}) async-start(f32[16,72,128]{2,1,0:T(8,128)} %shard_map.59), calls=%async_computation | async-start | bytes 1179648 | tf_op jit(solution)/shard_map/all_to_all | solution.py:237
  11.7 2.6 %collective-permute-start = (f32[4,64,512]{2,1,0:T(8,128)S(1)}, f32[4,64,512]{2,1,0:T(8,128)S(1)}, u32[]{:S(2)}, u32[]{:S(2)}) collective-permute-start(f32[4,64,512]{2,1,0:T(8,128)S(1)} %get-tuple-element.16), channel_id=1, source_target_pairs={{0,1},{1,0},{2,3},{3,2},{4,5},{5,4},{6,7},{7,6},{8,9},{9,8},{10,11... | collective-permute-start | bytes 1572872 | tf_op jit(solution)/shard_map/ppermute | solution.py:253
  12.7 2.3 %collective-permute-start.1 = (f32[4,64,512]{2,1,0:T(8,128)S(1)}, f32[4,64,512]{2,1,0:T(8,128)S(1)}, u32[]{:S(2)}, u32[]{:S(2)}) collective-permute-start(f32[4,64,512]{2,1,0:T(8,128)S(1)} %get-tuple-element.17), channel_id=1, source_target_pairs={{0,1},{1,0},{2,3},{3,2},{4,5},{5,4},{6,7},{7,6},{8,9},{9,8},{10,11... | collective-permute-start | bytes 1572872 | tf_op jit(solution)/shard_map/ppermute | solution.py:253
  21.2 7.4 %collective-permute-start.2 = (f32[6,64,128]{2,1,0:T(8,128)S(1)}, f32[6,64,128]{2,1,0:T(8,128)S(1)}, u32[]{:S(2)}, u32[]{:S(2)}) collective-permute-start(f32[6,64,128]{2,1,0:T(8,128)S(1)} %shard_map.62), channel_id=1, source_target_pairs={{0,96},{16,112},{32,64},{48,80},{64,32},{80,48},{96,0},{112,16},{1... | collective-permute-start | bytes 589832 | tf_op jit(solution)/shard_map/ppermute | solution.py:265
  23.8 31.3 %all-to-all-start.1 = ((f32[8,128,512]{2,1,0:T(8,128)}), f32[8,128,512]{2,1,0:T(8,128)S(1)}, u32[]{:S(2)}, u32[]{:S(2)}) async-start(f32[8,128,512]{2,1,0:T(8,128)} %shard_map.61), calls=%async_computation.1 | async-start | bytes 4194304 | tf_op jit(solution)/shard_map/all_to_all | solution.py:264
  28.7 6.0 %collective-permute-start.5 = (f32[576,128]{1,0:T(8,128)S(1)}, f32[576,128]{1,0:T(8,128)S(1)}, u32[]{:S(2)}, u32[]{:S(2)}) collective-permute-start(f32[576,128]{1,0:T(8,128)S(1)} %shard_map.63), channel_id=1, source_target_pairs={{0,96},{16,112},{32,0},{48,16},{64,32},{80,48},{96,64},{112,80},{1... | collective-permute-start | bytes 884744 | tf_op jit(solution)/shard_map/ppermute | solution.py:276
  29.7 7.4 %collective-permute-start.4 = (f32[576,128]{1,0:T(8,128)S(1)}, f32[576,128]{1,0:T(8,128)S(1)}, u32[]{:S(2)}, u32[]{:S(2)}) collective-permute-start(f32[576,128]{1,0:T(8,128)S(1)} %shard_map.63), channel_id=1, source_target_pairs={{0,64},{16,80},{32,96},{48,112},{64,0},{80,16},{96,32},{112,48},{1... | collective-permute-start | bytes 884744 | tf_op jit(solution)/shard_map/ppermute | solution.py:276
  30.5 14.6 %collective-permute-start.3 = (f32[576,128]{1,0:T(8,128)S(1)}, f32[576,128]{1,0:T(8,128)S(1)}, u32[]{:S(2)}, u32[]{:S(2)}) collective-permute-start(f32[576,128]{1,0:T(8,128)S(1)} %shard_map.63), channel_id=1, source_target_pairs={{0,32},{16,48},{32,64},{48,80},{64,96},{80,112},{96,0},{112,16},{1... | collective-permute-start | bytes 884744 | tf_op jit(solution)/shard_map/ppermute | solution.py:276
  45.1 4.4 %collective-permute-start.6 = (f32[4,576,128]{2,1,0:T(8,128)S(1)}, f32[4,576,128]{2,1,0:T(8,128)S(1)}, u32[]{:S(2)}, u32[]{:S(2)}) collective-permute-start(f32[4,576,128]{2,1,0:T(8,128)S(1)} %pad_maximum_fusion.own_ref), channel_id=1, source_target_pairs={{0,1},{1,0},{2,3},{3,2},{4,5},{5,4},{6,7},{7,6},{8,9},{9,8},{10,11... | collective-permute-start | bytes 3538952 | tf_op jit(solution)/shard_map/ppermute | solution.py:278

commit v10 on v9

--- a/solution.py
+++ b/solution.py
@@ -38,21 +38,19 @@
     return TURNS - 1 - turn, count - PLANE_BLOCKS + 4 * (TURNS - 1 - turn) + 1
 
 
-def prepare(right_hbm, factor_hbm, diag_hbm, copies_ref, right, factor, diag, scratch, arrived):
+def prepare(right_hbm, factor_hbm, diag_hbm, copies_ref, side_ref, right, factor, diag, scratch, arrived):
     sources = ((diag_hbm, diag), (factor_hbm, factor), (right_hbm, right))
     copies = [pltpu.make_async_copy(source, target, arrived.at[i]) for i, (source, target) in enumerate(sources)]
     for copy in copies:
         copy.start()
     for copy in copies:
         copy.wait()
-    half = factor.shape[0]
-    chunk = copies_ref.shape[1] - half
     scaled = contract(factor[...], diag[...], 1, 1)
+    for at in range(copies_ref.shape[0]):
+        copies_ref[at] = scaled
     scratch[...] = contract(right[...], diag[...], 0, 1)
-    rows = scratch[pl.ds(pl.multiple_of(lax.axis_index("col") * chunk, chunk), chunk), :]
-    for at in range(copies_ref.shape[0]):
-        copies_ref[at, :half] = scaled
-        copies_ref[at, half:] = rows
+    half = side_ref.shape[0]
+    side_ref[...] = scratch[pl.ds(pl.multiple_of(lax.axis_index("col") % 2 * half, half), half), :]
 
 
 def plane_index(turn, count, last):
@@ -61,24 +59,22 @@
 
 def pick_excess(plane_ref, send_ref):
     turn = lax.axis_index("row") // 2
-    half = send_ref.shape[1]
     for at in range(send_ref.shape[0]):
-        send_ref[at] = plane_ref[plane_index(turn, at + PLANE_BLOCKS, plane_ref.shape[0] - 1), :half]
-
-
-def even_out(plane_ref, got_ref, out_ref):
-    turn = lax.axis_index("row") // 2
-    places, rows, _ = plane_ref.shape
-    half = got_ref.shape[1]
+        send_ref[at] = plane_ref[plane_index(turn, at + PLANE_BLOCKS, plane_ref.shape[0] - 1)]
+
+
+def even_out(plane_ref, got_ref, side_ref, beside_ref, out_ref):
+    row = lax.axis_index("row")
+    turn = row // 2
+    places, half, _ = plane_ref.shape
     for at in range(PLANE_BLOCKS):
         held = (turn >= TURNS // 2) | (at <= 4 * turn)
         other = jnp.clip(at - 4 * turn - 1, 0, got_ref.shape[0] - 1)
-        own = plane_ref[plane_index(turn, at, places - 1), :half]
+        own = plane_ref[plane_index(turn, at, places - 1)]
         out_ref[at * half : (at + 1) * half] = jnp.where(held, own, got_ref[other])
-    start = PLANE_BLOCKS * half
-    chunk = rows - half
-    for at in range(places):
-        out_ref[start + at * chunk : start + (at + 1) * chunk] = plane_ref[at, half:]
+    for low_bit in range(2):
+        start = (PLANE_BLOCKS + low_bit) * half
+        out_ref[start : start + half] = jnp.where(row % 2 == low_bit, side_ref[...], beside_ref[...])
 
 
 def factor_and_invert(work, size):
@@ -160,7 +156,6 @@
     turns, _, size = own_ref.shape
     blocks = solved_t.shape[0]
     half_rows = size // 2
-    chunk = size // (2 * blocks)
     col, row = lax.axis_index("col"), lax.axis_index("row")
     core = col % 2
 
@@ -171,8 +166,8 @@
 
     current = []
     for i in range(blocks):
-        start = PLANE_BLOCKS * half_rows + i % 2 * blocks * chunk
-        parts = [rows_of(i // 2, half, start + j * chunk, chunk) for j in range(blocks) for half in range(2)]
+        start = (PLANE_BLOCKS + i % 2) * half_rows
+        parts = [rows_of(i // 2, half, start, half_rows) for half in range(2)]
         current.append(jnp.concatenate(parts, axis=0))
     for j in range(blocks):
         solved_t[j] = current[j]
@@ -204,17 +199,19 @@
     block_rows = right_side.shape[0]
     rank_width = right_side.shape[1]
     col_width = factor_window.shape[1]
-    chunk = rank_width // col_count
     turns = row_count // 2
     blocks = col_count // 2
     vmem = pl.BlockSpec(memory_space=pltpu.VMEM)
     params = pltpu.CompilerParams(vmem_limit_bytes=VMEM_BYTES)
-    piece_rows = col_width + chunk
-    copies = pl.pallas_call(
+    half_rank = rank_width // 2
+    copies, side = pl.pallas_call(
         prepare,
-        out_shape=jax.ShapeDtypeStruct((2 * blocks, piece_rows, block_rows), jnp.float32),
+        out_shape=[
+            jax.ShapeDtypeStruct((2 * blocks, col_width, block_rows), jnp.float32),
+            jax.ShapeDtypeStruct((half_rank, block_rows), jnp.float32),
+        ],
         in_specs=[pl.BlockSpec(memory_space=pltpu.HBM)] * 3,
-        out_specs=vmem,
+        out_specs=[vmem, vmem],
         scratch_shapes=[
             pltpu.VMEM(right_side.shape, jnp.float32),
             pltpu.VMEM((col_width, block_rows), jnp.float32),
@@ -236,7 +233,7 @@
     copies, cov = lax.optimization_barrier((copies, phase_cov))
     plane = lax.all_to_all(copies, ("row", "col"), 0, 0, axis_index_groups=planes, tiled=True)
     cores = [(col, col ^ 1) for col in range(col_count)]
-    cut_shapes = [jax.ShapeDtypeStruct((blocks // part, col_width, TILE_ROWS), jnp.float32) for part in (1,) + (2,) * 2]
+    cut_shapes = [jax.ShapeDtypeStruct((blocks // part, col_width, TILE_ROWS), jnp.float32) for part in (1,) + (4,) * 4]
     keep, *gives = pl.pallas_call(
         cut_tiles,
         out_shape=cut_shapes,
@@ -251,7 +248,8 @@
         out_specs=vmem,
         compiler_params=params,
     )(keep, *[lax.ppermute(give, "col", cores) for give in gives])
-    plane, cut = lax.optimization_barrier((plane, cut))
+    beside = lax.ppermute(side, "row", [(row, row ^ 1) for row in range(row_count)])
+    plane, cut, beside = lax.optimization_barrier((plane, cut, beside))
     excess = pl.pallas_call(
         pick_excess,
         out_shape=jax.ShapeDtypeStruct((PLANE_BLOCKS - 1, col_width, block_rows), jnp.float32),
@@ -265,11 +263,11 @@
     got = lax.ppermute(excess, "row", [(row, 2 * (turns - 1 - row // 2) + row % 2) for row in range(row_count)])
     plane = pl.pallas_call(
         even_out,
-        out_shape=jax.ShapeDtypeStruct((PLANE_BLOCKS * col_width + 2 * blocks * chunk, block_rows), jnp.float32),
-        in_specs=[vmem, vmem],
+        out_shape=jax.ShapeDtypeStruct(((PLANE_BLOCKS + 2) * col_width, block_rows), jnp.float32),
+        in_specs=[vmem] * 4,
         out_specs=vmem,
         compiler_params=params,
-    )(plane, got)
+    )(plane, got, side, beside)
     slots = [plane]
     for step in range(1, turns):
         turn_on = [(2 * turn + bit, 2 * ((turn + step) % turns) + bit) for turn in range(turns) for bit in range(2)]

time: 75.6 us -> 74.9 us (level)
  waiting for transfers between devices: 27.6 us -> 21.3 us
  starting transfers between devices: 21 us -> 25.7 us
  blocking collectives: 14.1 us -> 14.9 us
    ppermute x3, waiting for transfers between devices: 14.6 us -> 11.2 us  [local(): slots.append(lax.ppermute(plane, 'row', turn_on))]
    all_to_all x1, waiting for transfers between devices: 4.72 us -> 1.51 us  [local(): lax.all_to_all(copies, ('row', 'col'), 0, 0, axis_index_groups=planes, ti...]
    ppermute x0 -> x1, waiting for transfers between devices: none -> 2.68 us  [local(): lax.ppermute(side, 'row', [(row, row ^ 1) for row in range(row_count)])]
    ppermute x2 -> x4, waiting for transfers between devices: 2.19 us -> 0.03 us  [local(): lax.ppermute(give, 'col', cores)]
    ppermute x1, starting transfers between devices: 1.93 us -> 3.79 us  [local(): other = lax.ppermute(own, 'col', cores)]
    ppermute x0 -> x1, starting transfers between devices: none -> 1.64 us  [local(): lax.ppermute(side, 'row', [(row, row ^ 1) for row in range(row_count)])]
    ppermute x3, starting transfers between devices: 1.8 us -> 2.74 us  [local(): slots.append(lax.ppermute(plane, 'row', turn_on))]
    all_to_all x1, blocking collectives: 14.1 us -> 14.9 us  [local(): return (lax.all_to_all(basis, 'col', 0, 0, tiled=True), solved)]
  transfers between devices with their start and end apart: 9 -> 12, of which waited for: 8 -> 7; matrix products, arithmetic and copies ran while one was open for 0% -> 0% of each run, Pallas kernels for 5% -> 5%
where the time goes in v10:
time: 74.9 us; the launch traced here: 74.5 us
  starting transfers between devices  25.7 us (34%)
  waiting for transfers between devices  21.3 us (28%)
  blocking collectives  14.9 us (20%)
  Pallas kernels  11.1 us (15%)
    all_to_all x1, blocking collectives, local(): return (lax.all_to_all(basis, 'col', 0, 0, tiled=True), solved)  14.9 us
    ppermute x3, waiting for transfers between devices, local(): slots.append(lax.ppermute(plane, 'row', turn_on))  11.2 us
    all_to_all x1, starting transfers between devices, local(): lax.all_to_all(copies, ('row', 'col'), 0, 0, axis_index_groups=planes, ti...  8.74 us
    pallas_call x1, Pallas kernels, local(): pl.pallas_call(tile_basis, out_shape=jax.ShapeDtypeStruct((TILE_ROWS, ran...  5.35 us
    all_to_all x1, starting transfers between devices, local(): lax.all_to_all(cut, 'col', 0, 0, axis_index_groups=groups, tiled=True)  4.57 us
    ppermute x1, starting transfers between devices, local(): other = lax.ppermute(own, 'col', cores)  3.79 us
    all_to_all x1, waiting for transfers between devices, local(): lax.all_to_all(cut, 'col', 0, 0, axis_index_groups=groups, tiled=True)  3.42 us
    ppermute x3, starting transfers between devices, local(): slots.append(lax.ppermute(plane, 'row', turn_on))  2.74 us
  transfers between devices with their start and end apart: 12, of which 7 were waited for; matrix products, arithmetic and copies ran while one was open for 0% of the time, Pallas kernels for 5%

profile of v10, /device:TPU:1, one launch (start us, length us, event | category | flops | bytes accessed | tf_op | source)
XLA Modules:
  0.0 74.5 jit_solution(10117322473989147218)
XLA Ops:
  0.6 2.1 %shard_map.59 = (f32[16,64,128]{2,1,0:T(8,128)}, f32[64,128]{1,0:T(8,128)}) custom-call(f32[128,128]{1,0:T(8,128)} %right_hbm.1, f32[64,128]{1,0:T(8,128)} %bitcast.13, f32[128,128]{1,0:T(8,128)} %diag_hbm.1), custom_call_target="tpu_custom_call" | custom-call | tf_op jit(solution)/shard_map/pallas_call | solution.py:207
  2.7 0.0 copy-start
  2.7 0.0 copy-start.1
  2.8 8.7 %all-to-all-start = ((f32[16,64,128]{2,1,0:T(8,128)}), f32[16,64,128]{2,1,0:T(8,128)S(1)}, u32[]{:S(2)}, u32[]{:S(2)}) async-start(f32[16,64,128]{2,1,0:T(8,128)} %get-tuple-element.19), calls=%async_computation | async-start | bytes 1048576 | tf_op jit(solution)/shard_map/all_to_all | solution.py:234
  11.5 0.0 copy-done
  11.5 0.2 shard_map.60
  11.7 1.0 %collective-permute-start = (f32[2,64,512]{2,1,0:T(8,128)S(1)}, f32[2,64,512]{2,1,0:T(8,128)S(1)}, u32[]{:S(2)}, u32[]{:S(2)}) collective-permute-start(f32[2,64,512]{2,1,0:T(8,128)S(1)} %get-tuple-element.22), channel_id=1, source_target_pairs={{0,1},{1,0},{2,3},{3,2},{4,5},{5,4},{6,7},{7,6},{8,9},{9,8},{10,11... | collective-permute-start | bytes 786440 | tf_op jit(solution)/shard_map/ppermute | solution.py:250
  12.7 0.1 collective-permute-start.1
  12.8 0.4 collective-permute-start.2
  13.2 0.1 collective-permute-start.3
  13.3 0.0 copy-done.1
  13.3 1.6 %collective-permute-start.4 = (f32[64,128]{1,0:T(8,128)S(1)}, f32[64,128]{1,0:T(8,128)S(1)}, u32[]{:S(2)}, u32[]{:S(2)}) collective-permute-start(f32[64,128]{1,0:T(8,128)S(1)} %copy-done.1), channel_id=1, source_target_pairs={{0,16},{16,0},{32,48},{48,32},{64,80},{80,64},{96,112},{112,96},{1... | collective-permute-start | bytes 98312 | tf_op jit(solution)/shard_map/ppermute | solution.py:251
  15.0 0.0 collective-permute-done.refs_0_
  15.0 0.0 collective-permute-done.1.refs_1_
  15.0 0.0 collective-permute-done.2.refs_2_
  15.0 0.0 collective-permute-done.3.refs_3_
  15.0 1.5 %shard_map.61 = f32[8,128,512]{2,1,0:T(8,128)} custom-call(f32[8,64,512]{2,1,0:T(8,128)S(1)} %get-tuple-element.21.keep_ref, f32[2,64,512]{2,1,0:T(8,128)S(1)} %collective-permute-done.refs_0_, f32[2,64,512]{2,1,0:T(8,128)S(1)} %collective-permute-done.1.refs_1_, f32[2,64,512]{2,1,0:T(8,128)S(1)} %collective-permute-done.2.refs_2_, ...), custom_call_target="tpu_custom_call" | custom-call | tf_op jit(solution)/shard_map/pallas_call | solution.py:244
  16.5 2.7 %collective-permute-done.4.beside_ref = f32[64,128]{1,0:T(8,128)S(1)} collective-permute-done((f32[64,128]{1,0:T(8,128)S(1)}, f32[64,128]{1,0:T(8,128)S(1)}, u32[]{:S(2)}, u32[]{:S(2)}) %collective-permute-start.4) | collective-permute-done | bytes 32800 | tf_op jit(solution)/shard_map/ppermute | solution.py:251
  19.2 1.5 %all-to-all-done.plane_ref = f32[16,64,128]{2,1,0:T(8,128)S(1)} async-done(((f32[16,64,128]{2,1,0:T(8,128)}), f32[16,64,128]{2,1,0:T(8,128)S(1)}, u32[]{:S(2)}, u32[]{:S(2)}) %all-to-all-start) | async-done | bytes 524320 | tf_op jit(solution)/shard_map/all_to_all | solution.py:234
  20.7 2.6 %collective-permute-start.5 = (f32[6,64,128]{2,1,0:T(8,128)S(1)}, f32[6,64,128]{2,1,0:T(8,128)S(1)}, u32[]{:S(2)}, u32[]{:S(2)}) collective-permute-start(f32[6,64,128]{2,1,0:T(8,128)S(1)} %shard_map.62), channel_id=1, source_target_pairs={{0,96},{16,112},{32,64},{48,80},{64,32},{80,48},{96,0},{112,16},{1... | collective-permute-start | bytes 589832 | tf_op jit(solution)/shard_map/ppermute | solution.py:263
  23.3 4.6 %all-to-all-start.1 = ((f32[8,128,512]{2,1,0:T(8,128)}), f32[8,128,512]{2,1,0:T(8,128)S(1)}, u32[]{:S(2)}, u32[]{:S(2)}) async-start(f32[8,128,512]{2,1,0:T(8,128)} %shard_map.61), calls=%async_computation.1 | async-start | bytes 4194304 | tf_op jit(solution)/shard_map/all_to_all | solution.py:262
  27.8 0.0 collective-permute-done.5.got_ref
  27.8 0.1 shard_map.63
  27.9 0.1 collective-permute-start.6
  28.0 2.3 %collective-permute-start.7 = (f32[576,128]{1,0:T(8,128)S(1)}, f32[576,128]{1,0:T(8,128)S(1)}, u32[]{:S(2)}, u32[]{:S(2)}) collective-permute-start(f32[576,128]{1,0:T(8,128)S(1)} %shard_map.63), channel_id=1, source_target_pairs={{0,64},{16,80},{32,96},{48,112},{64,0},{80,16},{96,32},{112,48},{1... | collective-permute-start | bytes 884744 | tf_op jit(solution)/shard_map/ppermute | solution.py:274
  30.3 0.4 collective-permute-start.8
  30.6 6.8 %collective-permute-done.6 = f32[576,128]{1,0:T(8,128)S(1)} collective-permute-done((f32[576,128]{1,0:T(8,128)S(1)}, f32[576,128]{1,0:T(8,128)S(1)}, u32[]{:S(2)}, u32[]{:S(2)}) %collective-permute-start.6) | collective-permute-done | bytes 294944 | tf_op jit(solution)/shard_map/ppermute | solution.py:274
  37.4 1.9 %collective-permute-done.7 = f32[576,128]{1,0:T(8,128)S(1)} collective-permute-done((f32[576,128]{1,0:T(8,128)S(1)}, f32[576,128]{1,0:T(8,128)S(1)}, u32[]{:S(2)}, u32[]{:S(2)}) %collective-permute-start.7) | collective-permute-done | bytes 294944 | tf_op jit(solution)/shard_map/ppermute | solution.py:274
  39.4 2.5 %collective-permute-done.8 = f32[576,128]{1,0:T(8,128)S(1)} collective-permute-done((f32[576,128]{1,0:T(8,128)S(1)}, f32[576,128]{1,0:T(8,128)S(1)}, u32[]{:S(2)}, u32[]{:S(2)}) %collective-permute-start.8) | collective-permute-done | bytes 294944 | tf_op jit(solution)/shard_map/ppermute | solution.py:274
  41.8 0.1 pad_maximum_fusion.own_ref
  41.9 3.8 %collective-permute-start.9 = (f32[4,576,128]{2,1,0:T(8,128)S(1)}, f32[4,576,128]{2,1,0:T(8,128)S(1)}, u32[]{:S(2)}, u32[]{:S(2)}) collective-permute-start(f32[4,576,128]{2,1,0:T(8,128)S(1)} %pad_maximum_fusion.own_ref), channel_id=1, source_target_pairs={{0,1},{1,0},{2,3},{3,2},{4,5},{5,4},{6,7},{7,6},{8,9},{9,8},{10,11... | collective-permute-start | bytes 3538952 | tf_op jit(solution)/shard_map/ppermute | solution.py:276
  45.7 2.5 %collective-permute-done.9.other_ref = f32[4,576,128]{2,1,0:T(8,128)S(1)} collective-permute-done((f32[4,576,128]{2,1,0:T(8,128)S(1)}, f32[4,576,128]{2,1,0:T(8,128)S(1)}, u32[]{:S(2)}, u32[]{:S(2)}) %collective-permute-start.9) | collective-permute-done | bytes 1179680 | tf_op jit(solution)/shard_map/ppermute | solution.py:276
  48.2 1.9 %shard_map.64 = (bf16[128,1024]{1,0:T(8,128)(2,1)S(1)}, f32[64,128]{1,0:T(8,128)}) custom-call(f32[4,576,128]{2,1,0:T(8,128)S(1)} %pad_maximum_fusion.own_ref, f32[4,576,128]{2,1,0:T(8,128)S(1)} %collective-permute-done.9.other_ref), custom_call_target="tpu_custom_call" | custom-call | flops 1600000000 | bytes 3000000 | tf_op jit(solution)/shard_map/pallas_call | solution.py:277
  50.1 3.4 %all-to-all-done.1 = f32[8,128,512]{2,1,0:T(8,128)S(1)} async-done(((f32[8,128,512]{2,1,0:T(8,128)}), f32[8,128,512]{2,1,0:T(8,128)S(1)}, u32[]{:S(2)}, u32[]{:S(2)}) %all-to-all-start.1) | async-done | bytes 2097184 | tf_op jit(solution)/shard_map/all_to_all | solution.py:262
  53.5 5.4 %shard_map.65 = f32[512,128]{1,0:T(8,128)S(1)} custom-call(bf16[128,1024]{1,0:T(8,128)(2,1)S(1)} %get-tuple-element.31.low_ref, f32[1024,512]{1,0:T(8,128)S(1)} %bitcast.7), custom_call_target="tpu_custom_call" | custom-call | flops 1000000000 | bytes 3000000 | tf_op jit(solution)/shard_map/pallas_call | solution.py:292
  58.9 14.9 %all_to_all.15 = f32[16,32,128]{2,1,0:T(8,128)S(1)} all-to-all(f32[16,32,128]{2,1,0:T(8,128)S(1)} %bitcast.9), channel_id=1, replica_groups=mesh['row'=8,'col'=16] {'col'}, dimensions={0} | all-to-all | bytes 524288 | tf_op jit(solution)/shard_map/all_to_all | solution.py:302
  73.8 0.7 copy.7
  (1 shorter events, 0.0 us)
Async XLA Ops:
  2.7 8.8 %copy-start = (bf16[64,8192]{1,0:T(8,128)(2,1)S(1)}, bf16[64,8192]{1,0:T(8,128)(2,1)}, u32[]{:S(2)}) copy-start(bf16[64,8192]{1,0:T(8,128)(2,1)} %cov_ref) | copy-start | bytes 3145732
  2.7 10.6 %copy-start.1 = (f32[64,128]{1,0:T(8,128)S(1)}, f32[64,128]{1,0:T(8,128)}, u32[]{:S(2)}) copy-start(f32[64,128]{1,0:T(8,128)} %get-tuple-element.26.side_ref) | copy-start | bytes 98308
  2.8 17.9 %all-to-all-start = ((f32[16,64,128]{2,1,0:T(8,128)}), f32[16,64,128]{2,1,0:T(8,128)S(1)}, u32[]{:S(2)}, u32[]{:S(2)}) async-start(f32[16,64,128]{2,1,0:T(8,128)} %get-tuple-element.19), calls=%async_computation | async-start | bytes 1048576 | tf_op jit(solution)/shard_map/all_to_all | solution.py:234
  11.7 3.3 %collective-permute-start = (f32[2,64,512]{2,1,0:T(8,128)S(1)}, f32[2,64,512]{2,1,0:T(8,128)S(1)}, u32[]{:S(2)}, u32[]{:S(2)}) collective-permute-start(f32[2,64,512]{2,1,0:T(8,128)S(1)} %get-tuple-element.22), channel_id=1, source_target_pairs={{0,1},{1,0},{2,3},{3,2},{4,5},{5,4},{6,7},{7,6},{8,9},{9,8},{10,11... | collective-permute-start | bytes 786440 | tf_op jit(solution)/shard_map/ppermute | solution.py:250
  12.7 2.3 %collective-permute-start.1 = (f32[2,64,512]{2,1,0:T(8,128)S(1)}, f32[2,64,512]{2,1,0:T(8,128)S(1)}, u32[]{:S(2)}, u32[]{:S(2)}) collective-permute-start(f32[2,64,512]{2,1,0:T(8,128)S(1)} %get-tuple-element.23), channel_id=1, source_target_pairs={{0,1},{1,0},{2,3},{3,2},{4,5},{5,4},{6,7},{7,6},{8,9},{9,8},{10,11... | collective-permute-start | bytes 786440 | tf_op jit(solution)/shard_map/ppermute | solution.py:250
  12.8 2.2 %collective-permute-start.2 = (f32[2,64,512]{2,1,0:T(8,128)S(1)}, f32[2,64,512]{2,1,0:T(8,128)S(1)}, u32[]{:S(2)}, u32[]{:S(2)}) collective-permute-start(f32[2,64,512]{2,1,0:T(8,128)S(1)} %get-tuple-element.24), channel_id=1, source_target_pairs={{0,1},{1,0},{2,3},{3,2},{4,5},{5,4},{6,7},{7,6},{8,9},{9,8},{10,11... | collective-permute-start | bytes 786440 | tf_op jit(solution)/shard_map/ppermute | solution.py:250
  13.2 1.8 %collective-permute-start.3 = (f32[2,64,512]{2,1,0:T(8,128)S(1)}, f32[2,64,512]{2,1,0:T(8,128)S(1)}, u32[]{:S(2)}, u32[]{:S(2)}) collective-permute-start(f32[2,64,512]{2,1,0:T(8,128)S(1)} %get-tuple-element.25), channel_id=1, source_target_pairs={{0,1},{1,0},{2,3},{3,2},{4,5},{5,4},{6,7},{7,6},{8,9},{9,8},{10,11... | collective-permute-start | bytes 786440 | tf_op jit(solution)/shard_map/ppermute | solution.py:250
  13.3 5.9 %collective-permute-start.4 = (f32[64,128]{1,0:T(8,128)S(1)}, f32[64,128]{1,0:T(8,128)S(1)}, u32[]{:S(2)}, u32[]{:S(2)}) collective-permute-start(f32[64,128]{1,0:T(8,128)S(1)} %copy-done.1), channel_id=1, source_target_pairs={{0,16},{16,0},{32,48},{48,32},{64,80},{80,64},{96,112},{112,96},{1... | collective-permute-start | bytes 98312 | tf_op jit(solution)/shard_map/ppermute | solution.py:251
  20.7 7.1 %collective-permute-start.5 = (f32[6,64,128]{2,1,0:T(8,128)S(1)}, f32[6,64,128]{2,1,0:T(8,128)S(1)}, u32[]{:S(2)}, u32[]{:S(2)}) collective-permute-start(f32[6,64,128]{2,1,0:T(8,128)S(1)} %shard_map.62), channel_id=1, source_target_pairs={{0,96},{16,112},{32,64},{48,80},{64,32},{80,48},{96,0},{112,16},{1... | collective-permute-start | bytes 589832 | tf_op jit(solution)/shard_map/ppermute | solution.py:263
  23.3 30.3 %all-to-all-start.1 = ((f32[8,128,512]{2,1,0:T(8,128)}), f32[8,128,512]{2,1,0:T(8,128)S(1)}, u32[]{:S(2)}, u32[]{:S(2)}) async-start(f32[8,128,512]{2,1,0:T(8,128)} %shard_map.61), calls=%async_computation.1 | async-start | bytes 4194304 | tf_op jit(solution)/shard_map/all_to_all | solution.py:262
  27.9 9.5 %collective-permute-start.6 = (f32[576,128]{1,0:T(8,128)S(1)}, f32[576,128]{1,0:T(8,128)S(1)}, u32[]{:S(2)}, u32[]{:S(2)}) collective-permute-start(f32[576,128]{1,0:T(8,128)S(1)} %shard_map.63), channel_id=1, source_target_pairs={{0,32},{16,48},{32,64},{48,80},{64,96},{80,112},{96,0},{112,16},{1... | collective-permute-start | bytes 884744 | tf_op jit(solution)/shard_map/ppermute | solution.py:274
  28.0 11.4 %collective-permute-start.7 = (f32[576,128]{1,0:T(8,128)S(1)}, f32[576,128]{1,0:T(8,128)S(1)}, u32[]{:S(2)}, u32[]{:S(2)}) collective-permute-start(f32[576,128]{1,0:T(8,128)S(1)} %shard_map.63), channel_id=1, source_target_pairs={{0,64},{16,80},{32,96},{48,112},{64,0},{80,16},{96,32},{112,48},{1... | collective-permute-start | bytes 884744 | tf_op jit(solution)/shard_map/ppermute | solution.py:274
  30.3 11.6 %collective-permute-start.8 = (f32[576,128]{1,0:T(8,128)S(1)}, f32[576,128]{1,0:T(8,128)S(1)}, u32[]{:S(2)}, u32[]{:S(2)}) collective-permute-start(f32[576,128]{1,0:T(8,128)S(1)} %shard_map.63), channel_id=1, source_target_pairs={{0,96},{16,112},{32,0},{48,16},{64,32},{80,48},{96,64},{112,80},{1... | collective-permute-start | bytes 884744 | tf_op jit(solution)/shard_map/ppermute | solution.py:274
  41.9 6.3 %collective-permute-start.9 = (f32[4,576,128]{2,1,0:T(8,128)S(1)}, f32[4,576,128]{2,1,0:T(8,128)S(1)}, u32[]{:S(2)}, u32[]{:S(2)}) collective-permute-start(f32[4,576,128]{2,1,0:T(8,128)S(1)} %pad_maximum_fusion.own_ref), channel_id=1, source_target_pairs={{0,1},{1,0},{2,3},{3,2},{4,5},{5,4},{6,7},{7,6},{8,9},{9,8},{10,11... | collective-permute-start | bytes 3538952 | tf_op jit(solution)/shard_map/ppermute | solution.py:276

commit v11 on v10

--- a/solution.py
+++ b/solution.py
@@ -8,10 +8,11 @@
 from jax.sharding import PartitionSpec as P
 
 TILE_ROWS = 512
-PANEL = 32
+PANEL = 64
 SUBLANES = 8
 TURNS = 4
 PLANE_BLOCKS = 7
+CORE_PARTS = (3, 3, 2)
 HIGHEST = lax.Precision.HIGHEST
 VMEM_BYTES = 48 * 1024 * 1024
 
@@ -233,7 +234,7 @@
     copies, cov = lax.optimization_barrier((copies, phase_cov))
     plane = lax.all_to_all(copies, ("row", "col"), 0, 0, axis_index_groups=planes, tiled=True)
     cores = [(col, col ^ 1) for col in range(col_count)]
-    cut_shapes = [jax.ShapeDtypeStruct((blocks // part, col_width, TILE_ROWS), jnp.float32) for part in (1,) + (4,) * 4]
+    cut_shapes = [jax.ShapeDtypeStruct((count, col_width, TILE_ROWS), jnp.float32) for count in (blocks, *CORE_PARTS)]
     keep, *gives = pl.pallas_call(
         cut_tiles,
         out_shape=cut_shapes,

time: 74.9 us -> 74.8 us (level)
    ppermute x4 -> x3, starting transfers between devices: 1.64 us -> 1.54 us  [local(): lax.ppermute(give, 'col', cores)]
  transfers between devices with their start and end apart: 12 -> 11, of which waited for: 7 -> 8; matrix products, arithmetic and copies ran while one was open for 0% -> 0% of each run, Pallas kernels for 5% -> 5%
where the time goes in v11:
time: 74.8 us; the launch traced here: 74.4 us
  starting transfers between devices  25.6 us (34%)
  waiting for transfers between devices  21.4 us (29%)
  blocking collectives  14.9 us (20%)
  Pallas kernels  11.1 us (15%)
    all_to_all x1, blocking collectives, local(): return (lax.all_to_all(basis, 'col', 0, 0, tiled=True), solved)  14.9 us
    ppermute x3, waiting for transfers between devices, local(): slots.append(lax.ppermute(plane, 'row', turn_on))  11.2 us
    all_to_all x1, starting transfers between devices, local(): lax.all_to_all(copies, ('row', 'col'), 0, 0, axis_index_groups=planes, ti...  8.74 us
    pallas_call x1, Pallas kernels, local(): pl.pallas_call(tile_basis, out_shape=jax.ShapeDtypeStruct((TILE_ROWS, ran...  5.29 us
    all_to_all x1, starting transfers between devices, local(): lax.all_to_all(cut, 'col', 0, 0, axis_index_groups=groups, tiled=True)  4.57 us
    ppermute x1, starting transfers between devices, local(): other = lax.ppermute(own, 'col', cores)  3.79 us
    all_to_all x1, waiting for transfers between devices, local(): lax.all_to_all(cut, 'col', 0, 0, axis_index_groups=groups, tiled=True)  3.42 us
    ppermute x3, starting transfers between devices, local(): slots.append(lax.ppermute(plane, 'row', turn_on))  2.74 us
  transfers between devices with their start and end apart: 11, of which 8 were waited for; matrix products, arithmetic and copies ran while one was open for 0% of the time, Pallas kernels for 5%

profile of v11, /device:TPU:1, one launch (start us, length us, event | category | flops | bytes accessed | tf_op | source)
XLA Modules:
  0.0 74.4 jit_solution(16784026107456516397)
XLA Ops:
  0.6 2.1 %shard_map.59 = (f32[16,64,128]{2,1,0:T(8,128)}, f32[64,128]{1,0:T(8,128)}) custom-call(f32[128,128]{1,0:T(8,128)} %right_hbm.1, f32[64,128]{1,0:T(8,128)} %bitcast.13, f32[128,128]{1,0:T(8,128)} %diag_hbm.1), custom_call_target="tpu_custom_call" | custom-call | tf_op jit(solution)/shard_map/pallas_call | solution.py:208
  2.7 0.0 copy-start
  2.8 0.0 copy-start.1
  2.8 8.7 %all-to-all-start = ((f32[16,64,128]{2,1,0:T(8,128)}), f32[16,64,128]{2,1,0:T(8,128)S(1)}, u32[]{:S(2)}, u32[]{:S(2)}) async-start(f32[16,64,128]{2,1,0:T(8,128)} %get-tuple-element.18), calls=%async_computation | async-start | bytes 1048576 | tf_op jit(solution)/shard_map/all_to_all | solution.py:235
  11.5 0.0 copy-done
  11.5 0.2 shard_map.60
  11.7 1.0 %collective-permute-start = (f32[3,64,512]{2,1,0:T(8,128)S(1)}, f32[3,64,512]{2,1,0:T(8,128)S(1)}, u32[]{:S(2)}, u32[]{:S(2)}) collective-permute-start(f32[3,64,512]{2,1,0:T(8,128)S(1)} %get-tuple-element.21), channel_id=1, source_target_pairs={{0,1},{1,0},{2,3},{3,2},{4,5},{5,4},{6,7},{7,6},{8,9},{9,8},{10,11... | collective-permute-start | bytes 1179656 | tf_op jit(solution)/shard_map/ppermute | solution.py:251
  12.7 0.1 collective-permute-start.1
  12.8 0.4 collective-permute-start.2
  13.2 0.0 copy-done.1
  13.2 1.7 %collective-permute-start.3 = (f32[64,128]{1,0:T(8,128)S(1)}, f32[64,128]{1,0:T(8,128)S(1)}, u32[]{:S(2)}, u32[]{:S(2)}) collective-permute-start(f32[64,128]{1,0:T(8,128)S(1)} %copy-done.1), channel_id=1, source_target_pairs={{0,16},{16,0},{32,48},{48,32},{64,80},{80,64},{96,112},{112,96},{1... | collective-permute-start | bytes 98312 | tf_op jit(solution)/shard_map/ppermute | solution.py:252
  14.9 0.1 collective-permute-done.2.refs_2_
  15.0 0.0 collective-permute-done.refs_0_
  15.0 0.0 collective-permute-done.1.refs_1_
  15.0 1.5 %shard_map.61 = f32[8,128,512]{2,1,0:T(8,128)} custom-call(f32[8,64,512]{2,1,0:T(8,128)S(1)} %get-tuple-element.20.keep_ref, f32[3,64,512]{2,1,0:T(8,128)S(1)} %collective-permute-done.refs_0_, f32[3,64,512]{2,1,0:T(8,128)S(1)} %collective-permute-done.1.refs_1_, f32[2,64,512]{2,1,0:T(8,128)S(1)} %collective-permute-done.2.refs_2_), custom_call_target="tpu_custom_call" | custom-call | tf_op jit(solution)/shard_map/pallas_call | solution.py:245
  16.5 2.7 %collective-permute-done.3.beside_ref = f32[64,128]{1,0:T(8,128)S(1)} collective-permute-done((f32[64,128]{1,0:T(8,128)S(1)}, f32[64,128]{1,0:T(8,128)S(1)}, u32[]{:S(2)}, u32[]{:S(2)}) %collective-permute-start.3) | collective-permute-done | bytes 32800 | tf_op jit(solution)/shard_map/ppermute | solution.py:252
  19.2 1.5 %all-to-all-done.plane_ref = f32[16,64,128]{2,1,0:T(8,128)S(1)} async-done(((f32[16,64,128]{2,1,0:T(8,128)}), f32[16,64,128]{2,1,0:T(8,128)S(1)}, u32[]{:S(2)}, u32[]{:S(2)}) %all-to-all-start) | async-done | bytes 524320 | tf_op jit(solution)/shard_map/all_to_all | solution.py:235
  20.7 2.6 %collective-permute-start.4 = (f32[6,64,128]{2,1,0:T(8,128)S(1)}, f32[6,64,128]{2,1,0:T(8,128)S(1)}, u32[]{:S(2)}, u32[]{:S(2)}) collective-permute-start(f32[6,64,128]{2,1,0:T(8,128)S(1)} %shard_map.62), channel_id=1, source_target_pairs={{0,96},{16,112},{32,64},{48,80},{64,32},{80,48},{96,0},{112,16},{1... | collective-permute-start | bytes 589832 | tf_op jit(solution)/shard_map/ppermute | solution.py:264
  23.3 4.6 %all-to-all-start.1 = ((f32[8,128,512]{2,1,0:T(8,128)}), f32[8,128,512]{2,1,0:T(8,128)S(1)}, u32[]{:S(2)}, u32[]{:S(2)}) async-start(f32[8,128,512]{2,1,0:T(8,128)} %shard_map.61), calls=%async_computation.1 | async-start | bytes 4194304 | tf_op jit(solution)/shard_map/all_to_all | solution.py:263
  27.8 0.0 collective-permute-done.4.got_ref
  27.8 0.1 shard_map.63
  27.9 0.1 collective-permute-start.5
  28.0 2.3 %collective-permute-start.6 = (f32[576,128]{1,0:T(8,128)S(1)}, f32[576,128]{1,0:T(8,128)S(1)}, u32[]{:S(2)}, u32[]{:S(2)}) collective-permute-start(f32[576,128]{1,0:T(8,128)S(1)} %shard_map.63), channel_id=1, source_target_pairs={{0,64},{16,80},{32,96},{48,112},{64,0},{80,16},{96,32},{112,48},{1... | collective-permute-start | bytes 884744 | tf_op jit(solution)/shard_map/ppermute | solution.py:275
  30.3 0.4 collective-permute-start.7
  30.7 6.8 %collective-permute-done.5 = f32[576,128]{1,0:T(8,128)S(1)} collective-permute-done((f32[576,128]{1,0:T(8,128)S(1)}, f32[576,128]{1,0:T(8,128)S(1)}, u32[]{:S(2)}, u32[]{:S(2)}) %collective-permute-start.5) | collective-permute-done | bytes 294944 | tf_op jit(solution)/shard_map/ppermute | solution.py:275
  37.4 1.9 %collective-permute-done.6 = f32[576,128]{1,0:T(8,128)S(1)} collective-permute-done((f32[576,128]{1,0:T(8,128)S(1)}, f32[576,128]{1,0:T(8,128)S(1)}, u32[]{:S(2)}, u32[]{:S(2)}) %collective-permute-start.6) | collective-permute-done | bytes 294944 | tf_op jit(solution)/shard_map/ppermute | solution.py:275
  39.4 2.5 %collective-permute-done.7 = f32[576,128]{1,0:T(8,128)S(1)} collective-permute-done((f32[576,128]{1,0:T(8,128)S(1)}, f32[576,128]{1,0:T(8,128)S(1)}, u32[]{:S(2)}, u32[]{:S(2)}) %collective-permute-start.7) | collective-permute-done | bytes 294944 | tf_op jit(solution)/shard_map/ppermute | solution.py:275
  41.9 0.1 pad_maximum_fusion.own_ref
  41.9 3.8 %collective-permute-start.8 = (f32[4,576,128]{2,1,0:T(8,128)S(1)}, f32[4,576,128]{2,1,0:T(8,128)S(1)}, u32[]{:S(2)}, u32[]{:S(2)}) collective-permute-start(f32[4,576,128]{2,1,0:T(8,128)S(1)} %pad_maximum_fusion.own_ref), channel_id=1, source_target_pairs={{0,1},{1,0},{2,3},{3,2},{4,5},{5,4},{6,7},{7,6},{8,9},{9,8},{10,11... | collective-permute-start | bytes 3538952 | tf_op jit(solution)/shard_map/ppermute | solution.py:277
  45.7 2.5 %collective-permute-done.8.other_ref = f32[4,576,128]{2,1,0:T(8,128)S(1)} collective-permute-done((f32[4,576,128]{2,1,0:T(8,128)S(1)}, f32[4,576,128]{2,1,0:T(8,128)S(1)}, u32[]{:S(2)}, u32[]{:S(2)}) %collective-permute-start.8) | collective-permute-done | bytes 1179680 | tf_op jit(solution)/shard_map/ppermute | solution.py:277
  48.2 1.9 %shard_map.64 = (bf16[128,1024]{1,0:T(8,128)(2,1)S(1)}, f32[64,128]{1,0:T(8,128)}) custom-call(f32[4,576,128]{2,1,0:T(8,128)S(1)} %pad_maximum_fusion.own_ref, f32[4,576,128]{2,1,0:T(8,128)S(1)} %collective-permute-done.8.other_ref), custom_call_target="tpu_custom_call" | custom-call | flops 1600000000 | bytes 3000000 | tf_op jit(solution)/shard_map/pallas_call | solution.py:278
  50.1 3.4 %all-to-all-done.1 = f32[8,128,512]{2,1,0:T(8,128)S(1)} async-done(((f32[8,128,512]{2,1,0:T(8,128)}), f32[8,128,512]{2,1,0:T(8,128)S(1)}, u32[]{:S(2)}, u32[]{:S(2)}) %all-to-all-start.1) | async-done | bytes 2097184 | tf_op jit(solution)/shard_map/all_to_all | solution.py:263
  53.5 5.3 %shard_map.65 = f32[512,128]{1,0:T(8,128)S(1)} custom-call(bf16[128,1024]{1,0:T(8,128)(2,1)S(1)} %get-tuple-element.29.low_ref, f32[1024,512]{1,0:T(8,128)S(1)} %bitcast.7), custom_call_target="tpu_custom_call" | custom-call | flops 1000000000 | bytes 3000000 | tf_op jit(solution)/shard_map/pallas_call | solution.py:293
  58.8 14.9 %all_to_all.15 = f32[16,32,128]{2,1,0:T(8,128)S(1)} all-to-all(f32[16,32,128]{2,1,0:T(8,128)S(1)} %bitcast.9), channel_id=1, replica_groups=mesh['row'=8,'col'=16] {'col'}, dimensions={0} | all-to-all | bytes 524288 | tf_op jit(solution)/shard_map/all_to_all | solution.py:303
  73.7 0.7 copy.7
  (1 shorter events, 0.0 us)
Async XLA Ops:
  2.7 8.8 %copy-start = (bf16[64,8192]{1,0:T(8,128)(2,1)S(1)}, bf16[64,8192]{1,0:T(8,128)(2,1)}, u32[]{:S(2)}) copy-start(bf16[64,8192]{1,0:T(8,128)(2,1)} %cov_ref) | copy-start | bytes 3145732
  2.8 10.5 %copy-start.1 = (f32[64,128]{1,0:T(8,128)S(1)}, f32[64,128]{1,0:T(8,128)}, u32[]{:S(2)}) copy-start(f32[64,128]{1,0:T(8,128)} %get-tuple-element.24.side_ref) | copy-start | bytes 98308
  2.8 17.9 %all-to-all-start = ((f32[16,64,128]{2,1,0:T(8,128)}), f32[16,64,128]{2,1,0:T(8,128)S(1)}, u32[]{:S(2)}, u32[]{:S(2)}) async-start(f32[16,64,128]{2,1,0:T(8,128)} %get-tuple-element.18), calls=%async_computation | async-start | bytes 1048576 | tf_op jit(solution)/shard_map/all_to_all | solution.py:235
  11.7 3.3 %collective-permute-start = (f32[3,64,512]{2,1,0:T(8,128)S(1)}, f32[3,64,512]{2,1,0:T(8,128)S(1)}, u32[]{:S(2)}, u32[]{:S(2)}) collective-permute-start(f32[3,64,512]{2,1,0:T(8,128)S(1)} %get-tuple-element.21), channel_id=1, source_target_pairs={{0,1},{1,0},{2,3},{3,2},{4,5},{5,4},{6,7},{7,6},{8,9},{9,8},{10,11... | collective-permute-start | bytes 1179656 | tf_op jit(solution)/shard_map/ppermute | solution.py:251
  12.7 2.3 %collective-permute-start.1 = (f32[3,64,512]{2,1,0:T(8,128)S(1)}, f32[3,64,512]{2,1,0:T(8,128)S(1)}, u32[]{:S(2)}, u32[]{:S(2)}) collective-permute-start(f32[3,64,512]{2,1,0:T(8,128)S(1)} %get-tuple-element.22), channel_id=1, source_target_pairs={{0,1},{1,0},{2,3},{3,2},{4,5},{5,4},{6,7},{7,6},{8,9},{9,8},{10,11... | collective-permute-start | bytes 1179656 | tf_op jit(solution)/shard_map/ppermute | solution.py:251
  12.8 2.2 %collective-permute-start.2 = (f32[2,64,512]{2,1,0:T(8,128)S(1)}, f32[2,64,512]{2,1,0:T(8,128)S(1)}, u32[]{:S(2)}, u32[]{:S(2)}) collective-permute-start(f32[2,64,512]{2,1,0:T(8,128)S(1)} %get-tuple-element.23), channel_id=1, source_target_pairs={{0,1},{1,0},{2,3},{3,2},{4,5},{5,4},{6,7},{7,6},{8,9},{9,8},{10,11... | collective-permute-start | bytes 786440 | tf_op jit(solution)/shard_map/ppermute | solution.py:251
  13.2 5.9 %collective-permute-start.3 = (f32[64,128]{1,0:T(8,128)S(1)}, f32[64,128]{1,0:T(8,128)S(1)}, u32[]{:S(2)}, u32[]{:S(2)}) collective-permute-start(f32[64,128]{1,0:T(8,128)S(1)} %copy-done.1), channel_id=1, source_target_pairs={{0,16},{16,0},{32,48},{48,32},{64,80},{80,64},{96,112},{112,96},{1... | collective-permute-start | bytes 98312 | tf_op jit(solution)/shard_map/ppermute | solution.py:252
  20.7 7.1 %collective-permute-start.4 = (f32[6,64,128]{2,1,0:T(8,128)S(1)}, f32[6,64,128]{2,1,0:T(8,128)S(1)}, u32[]{:S(2)}, u32[]{:S(2)}) collective-permute-start(f32[6,64,128]{2,1,0:T(8,128)S(1)} %shard_map.62), channel_id=1, source_target_pairs={{0,96},{16,112},{32,64},{48,80},{64,32},{80,48},{96,0},{112,16},{1... | collective-permute-start | bytes 589832 | tf_op jit(solution)/shard_map/ppermute | solution.py:264
  23.3 30.3 %all-to-all-start.1 = ((f32[8,128,512]{2,1,0:T(8,128)}), f32[8,128,512]{2,1,0:T(8,128)S(1)}, u32[]{:S(2)}, u32[]{:S(2)}) async-start(f32[8,128,512]{2,1,0:T(8,128)} %shard_map.61), calls=%async_computation.1 | async-start | bytes 4194304 | tf_op jit(solution)/shard_map/all_to_all | solution.py:263
  27.9 9.5 %collective-permute-start.5 = (f32[576,128]{1,0:T(8,128)S(1)}, f32[576,128]{1,0:T(8,128)S(1)}, u32[]{:S(2)}, u32[]{:S(2)}) collective-permute-start(f32[576,128]{1,0:T(8,128)S(1)} %shard_map.63), channel_id=1, source_target_pairs={{0,32},{16,48},{32,64},{48,80},{64,96},{80,112},{96,0},{112,16},{1... | collective-permute-start | bytes 884744 | tf_op jit(solution)/shard_map/ppermute | solution.py:275
  28.0 11.4 %collective-permute-start.6 = (f32[576,128]{1,0:T(8,128)S(1)}, f32[576,128]{1,0:T(8,128)S(1)}, u32[]{:S(2)}, u32[]{:S(2)}) collective-permute-start(f32[576,128]{1,0:T(8,128)S(1)} %shard_map.63), channel_id=1, source_target_pairs={{0,64},{16,80},{32,96},{48,112},{64,0},{80,16},{96,32},{112,48},{1... | collective-permute-start | bytes 884744 | tf_op jit(solution)/shard_map/ppermute | solution.py:275
  30.3 11.6 %collective-permute-start.7 = (f32[576,128]{1,0:T(8,128)S(1)}, f32[576,128]{1,0:T(8,128)S(1)}, u32[]{:S(2)}, u32[]{:S(2)}) collective-permute-start(f32[576,128]{1,0:T(8,128)S(1)} %shard_map.63), channel_id=1, source_target_pairs={{0,96},{16,112},{32,0},{48,16},{64,32},{80,48},{96,64},{112,80},{1... | collective-permute-start | bytes 884744 | tf_op jit(solution)/shard_map/ppermute | solution.py:275
  41.9 6.3 %collective-permute-start.8 = (f32[4,576,128]{2,1,0:T(8,128)S(1)}, f32[4,576,128]{2,1,0:T(8,128)S(1)}, u32[]{:S(2)}, u32[]{:S(2)}) collective-permute-start(f32[4,576,128]{2,1,0:T(8,128)S(1)} %pad_maximum_fusion.own_ref), channel_id=1, source_target_pairs={{0,1},{1,0},{2,3},{3,2},{4,5},{5,4},{6,7},{7,6},{8,9},{9,8},{10,11... | collective-permute-start | bytes 3538952 | tf_op jit(solution)/shard_map/ppermute | solution.py:277

commit v12 on v11

--- a/solution.py
+++ b/solution.py
@@ -161,7 +161,7 @@
     core = col % 2
 
     def rows_of(turn, half, start, count):
-        slot = (row // 2 - turn + turns) % turns
+        slot = jnp.bitwise_xor(row // 2, turn)
         own, other = own_ref[slot, start : start + count, :], other_ref[slot, start : start + count, :]
         return jnp.where(core == half, own, other)
 
@@ -271,8 +271,7 @@
     )(plane, got, side, beside)
     slots = [plane]
     for step in range(1, turns):
-        turn_on = [(2 * turn + bit, 2 * ((turn + step) % turns) + bit) for turn in range(turns) for bit in range(2)]
-        slots.append(lax.ppermute(plane, "row", turn_on))
+        slots.append(lax.ppermute(plane, "row", [(row, row ^ 2 * step) for row in range(row_count)]))
     own = jnp.stack(slots)
     other = lax.ppermute(own, "col", cores)
     low, solved = pl.pallas_call(

time: 74.8 us -> 74.8 us (level)
    all_to_all x1, waiting for transfers between devices: 3.42 us -> 1.72 us  [local(): lax.all_to_all(cut, 'col', 0, 0, axis_index_groups=groups, tiled=True)]
    ppermute x3, waiting for transfers between devices: 11.2 us -> 12.7 us  [local(): lax.ppermute(plane, 'row', [(row, row ^ 2 * step) for row in range(row_co...]
    ppermute x3, starting transfers between devices: 2.74 us -> 3.93 us  [local(): lax.ppermute(plane, 'row', [(row, row ^ 2 * step) for row in range(row_co...]
    ppermute x1, starting transfers between devices: 3.79 us -> 2.76 us  [local(): other = lax.ppermute(own, 'col', cores)]
where the time goes in v12:
time: 74.8 us; the launch traced here: 74.4 us
  starting transfers between devices  25.8 us (34%)
  waiting for transfers between devices  21.2 us (28%)
  blocking collectives  14.9 us (20%)
  Pallas kernels  11.1 us (15%)
    all_to_all x1, blocking collectives, local(): return (lax.all_to_all(basis, 'col', 0, 0, tiled=True), solved)  14.9 us
    ppermute x3, waiting for transfers between devices, local(): lax.ppermute(plane, 'row', [(row, row ^ 2 * step) for row in range(row_co...  12.7 us
    all_to_all x1, starting transfers between devices, local(): lax.all_to_all(copies, ('row', 'col'), 0, 0, axis_index_groups=planes, ti...  8.74 us
    pallas_call x1, Pallas kernels, local(): pl.pallas_call(tile_basis, out_shape=jax.ShapeDtypeStruct((TILE_ROWS, ran...  5.29 us
    all_to_all x1, starting transfers between devices, local(): lax.all_to_all(cut, 'col', 0, 0, axis_index_groups=groups, tiled=True)  4.57 us
    ppermute x3, starting transfers between devices, local(): lax.ppermute(plane, 'row', [(row, row ^ 2 * step) for row in range(row_co...  3.93 us
    ppermute x1, starting transfers between devices, local(): other = lax.ppermute(own, 'col', cores)  2.76 us
    ppermute x1, waiting for transfers between devices, local(): lax.ppermute(side, 'row', [(row, row ^ 1) for row in range(row_count)])  2.66 us
  transfers between devices with their start and end apart: 11, of which 8 were waited for; matrix products, arithmetic and copies ran while one was open for 0% of the time, Pallas kernels for 5%

profile of v12, /device:TPU:1, one launch (start us, length us, event | category | flops | bytes accessed | tf_op | source)
XLA Modules:
  0.0 74.4 jit_solution(9442510806395303521)
XLA Ops:
  0.6 2.1 %shard_map.59 = (f32[16,64,128]{2,1,0:T(8,128)}, f32[64,128]{1,0:T(8,128)}) custom-call(f32[128,128]{1,0:T(8,128)} %right_hbm.1, f32[64,128]{1,0:T(8,128)} %bitcast.13, f32[128,128]{1,0:T(8,128)} %diag_hbm.1), custom_call_target="tpu_custom_call" | custom-call | tf_op jit(solution)/shard_map/pallas_call | solution.py:208
  2.7 0.0 copy-start
  2.8 0.0 copy-start.1
  2.8 8.7 %all-to-all-start = ((f32[16,64,128]{2,1,0:T(8,128)}), f32[16,64,128]{2,1,0:T(8,128)S(1)}, u32[]{:S(2)}, u32[]{:S(2)}) async-start(f32[16,64,128]{2,1,0:T(8,128)} %get-tuple-element.18), calls=%async_computation | async-start | bytes 1048576 | tf_op jit(solution)/shard_map/all_to_all | solution.py:235
  11.5 0.0 copy-done
  11.5 0.2 shard_map.60
  11.7 1.0 %collective-permute-start = (f32[3,64,512]{2,1,0:T(8,128)S(1)}, f32[3,64,512]{2,1,0:T(8,128)S(1)}, u32[]{:S(2)}, u32[]{:S(2)}) collective-permute-start(f32[3,64,512]{2,1,0:T(8,128)S(1)} %get-tuple-element.21), channel_id=1, source_target_pairs={{0,1},{1,0},{2,3},{3,2},{4,5},{5,4},{6,7},{7,6},{8,9},{9,8},{10,11... | collective-permute-start | bytes 1179656 | tf_op jit(solution)/shard_map/ppermute | solution.py:251
  12.7 0.1 collective-permute-start.1
  12.8 0.4 collective-permute-start.2
  13.2 0.0 copy-done.1
  13.2 1.7 %collective-permute-start.3 = (f32[64,128]{1,0:T(8,128)S(1)}, f32[64,128]{1,0:T(8,128)S(1)}, u32[]{:S(2)}, u32[]{:S(2)}) collective-permute-start(f32[64,128]{1,0:T(8,128)S(1)} %copy-done.1), channel_id=1, source_target_pairs={{0,16},{16,0},{32,48},{48,32},{64,80},{80,64},{96,112},{112,96},{1... | collective-permute-start | bytes 98312 | tf_op jit(solution)/shard_map/ppermute | solution.py:252
  14.9 0.1 collective-permute-done.2.refs_2_
  15.0 0.0 collective-permute-done.refs_0_
  15.0 0.0 collective-permute-done.1.refs_1_
  15.0 1.5 %shard_map.61 = f32[8,128,512]{2,1,0:T(8,128)} custom-call(f32[8,64,512]{2,1,0:T(8,128)S(1)} %get-tuple-element.20.keep_ref, f32[3,64,512]{2,1,0:T(8,128)S(1)} %collective-permute-done.refs_0_, f32[3,64,512]{2,1,0:T(8,128)S(1)} %collective-permute-done.1.refs_1_, f32[2,64,512]{2,1,0:T(8,128)S(1)} %collective-permute-done.2.refs_2_), custom_call_target="tpu_custom_call" | custom-call | tf_op jit(solution)/shard_map/pallas_call | solution.py:245
  16.5 2.7 %collective-permute-done.3.beside_ref = f32[64,128]{1,0:T(8,128)S(1)} collective-permute-done((f32[64,128]{1,0:T(8,128)S(1)}, f32[64,128]{1,0:T(8,128)S(1)}, u32[]{:S(2)}, u32[]{:S(2)}) %collective-permute-start.3) | collective-permute-done | bytes 32800 | tf_op jit(solution)/shard_map/ppermute | solution.py:252
  19.2 1.5 %all-to-all-done.plane_ref = f32[16,64,128]{2,1,0:T(8,128)S(1)} async-done(((f32[16,64,128]{2,1,0:T(8,128)}), f32[16,64,128]{2,1,0:T(8,128)S(1)}, u32[]{:S(2)}, u32[]{:S(2)}) %all-to-all-start) | async-done | bytes 524320 | tf_op jit(solution)/shard_map/all_to_all | solution.py:235
  20.7 2.6 %collective-permute-start.4 = (f32[6,64,128]{2,1,0:T(8,128)S(1)}, f32[6,64,128]{2,1,0:T(8,128)S(1)}, u32[]{:S(2)}, u32[]{:S(2)}) collective-permute-start(f32[6,64,128]{2,1,0:T(8,128)S(1)} %shard_map.62), channel_id=1, source_target_pairs={{0,96},{16,112},{32,64},{48,80},{64,32},{80,48},{96,0},{112,16},{1... | collective-permute-start | bytes 589832 | tf_op jit(solution)/shard_map/ppermute | solution.py:264
  23.3 4.6 %all-to-all-start.1 = ((f32[8,128,512]{2,1,0:T(8,128)}), f32[8,128,512]{2,1,0:T(8,128)S(1)}, u32[]{:S(2)}, u32[]{:S(2)}) async-start(f32[8,128,512]{2,1,0:T(8,128)} %shard_map.61), calls=%async_computation.1 | async-start | bytes 4194304 | tf_op jit(solution)/shard_map/all_to_all | solution.py:263
  27.8 0.0 collective-permute-done.4.got_ref
  27.8 0.1 shard_map.63
  27.9 0.1 collective-permute-start.5
  28.0 2.3 %collective-permute-start.6 = (f32[576,128]{1,0:T(8,128)S(1)}, f32[576,128]{1,0:T(8,128)S(1)}, u32[]{:S(2)}, u32[]{:S(2)}) collective-permute-start(f32[576,128]{1,0:T(8,128)S(1)} %shard_map.63), channel_id=1, source_target_pairs={{0,64},{16,80},{32,96},{48,112},{64,0},{80,16},{96,32},{112,48},{1... | collective-permute-start | bytes 884744 | tf_op jit(solution)/shard_map/ppermute | solution.py:274
  30.3 1.5 %collective-permute-start.7 = (f32[576,128]{1,0:T(8,128)S(1)}, f32[576,128]{1,0:T(8,128)S(1)}, u32[]{:S(2)}, u32[]{:S(2)}) collective-permute-start(f32[576,128]{1,0:T(8,128)S(1)} %shard_map.63), channel_id=1, source_target_pairs={{0,96},{16,112},{32,64},{48,80},{64,32},{80,48},{96,0},{112,16},{1... | collective-permute-start | bytes 884744 | tf_op jit(solution)/shard_map/ppermute | solution.py:274
  31.9 2.0 %collective-permute-done.5 = f32[576,128]{1,0:T(8,128)S(1)} collective-permute-done((f32[576,128]{1,0:T(8,128)S(1)}, f32[576,128]{1,0:T(8,128)S(1)}, u32[]{:S(2)}, u32[]{:S(2)}) %collective-permute-start.5) | collective-permute-done | bytes 294944 | tf_op jit(solution)/shard_map/ppermute | solution.py:274
  33.9 5.5 %collective-permute-done.6 = f32[576,128]{1,0:T(8,128)S(1)} collective-permute-done((f32[576,128]{1,0:T(8,128)S(1)}, f32[576,128]{1,0:T(8,128)S(1)}, u32[]{:S(2)}, u32[]{:S(2)}) %collective-permute-start.6) | collective-permute-done | bytes 294944 | tf_op jit(solution)/shard_map/ppermute | solution.py:274
  39.4 5.2 %collective-permute-done.7 = f32[576,128]{1,0:T(8,128)S(1)} collective-permute-done((f32[576,128]{1,0:T(8,128)S(1)}, f32[576,128]{1,0:T(8,128)S(1)}, u32[]{:S(2)}, u32[]{:S(2)}) %collective-permute-start.7) | collective-permute-done | bytes 294944 | tf_op jit(solution)/shard_map/ppermute | solution.py:274
  44.6 0.1 pad_maximum_fusion.own_ref
  44.7 2.8 %collective-permute-start.8 = (f32[4,576,128]{2,1,0:T(8,128)S(1)}, f32[4,576,128]{2,1,0:T(8,128)S(1)}, u32[]{:S(2)}, u32[]{:S(2)}) collective-permute-start(f32[4,576,128]{2,1,0:T(8,128)S(1)} %pad_maximum_fusion.own_ref), channel_id=1, source_target_pairs={{0,1},{1,0},{2,3},{3,2},{4,5},{5,4},{6,7},{7,6},{8,9},{9,8},{10,11... | collective-permute-start | bytes 3538952 | tf_op jit(solution)/shard_map/ppermute | solution.py:276
  47.4 2.5 %collective-permute-done.8.other_ref = f32[4,576,128]{2,1,0:T(8,128)S(1)} collective-permute-done((f32[4,576,128]{2,1,0:T(8,128)S(1)}, f32[4,576,128]{2,1,0:T(8,128)S(1)}, u32[]{:S(2)}, u32[]{:S(2)}) %collective-permute-start.8) | collective-permute-done | bytes 1179680 | tf_op jit(solution)/shard_map/ppermute | solution.py:276
  49.9 1.9 %shard_map.64 = (bf16[128,1024]{1,0:T(8,128)(2,1)S(1)}, f32[64,128]{1,0:T(8,128)}) custom-call(f32[4,576,128]{2,1,0:T(8,128)S(1)} %pad_maximum_fusion.own_ref, f32[4,576,128]{2,1,0:T(8,128)S(1)} %collective-permute-done.8.other_ref), custom_call_target="tpu_custom_call" | custom-call | flops 1600000000 | bytes 3000000 | tf_op jit(solution)/shard_map/pallas_call | solution.py:277
  51.8 1.7 %all-to-all-done.1 = f32[8,128,512]{2,1,0:T(8,128)S(1)} async-done(((f32[8,128,512]{2,1,0:T(8,128)}), f32[8,128,512]{2,1,0:T(8,128)S(1)}, u32[]{:S(2)}, u32[]{:S(2)}) %all-to-all-start.1) | async-done | bytes 2097184 | tf_op jit(solution)/shard_map/all_to_all | solution.py:263
  53.5 5.3 %shard_map.65 = f32[512,128]{1,0:T(8,128)S(1)} custom-call(bf16[128,1024]{1,0:T(8,128)(2,1)S(1)} %get-tuple-element.29.low_ref, f32[1024,512]{1,0:T(8,128)S(1)} %bitcast.7), custom_call_target="tpu_custom_call" | custom-call | flops 1000000000 | bytes 3000000 | tf_op jit(solution)/shard_map/pallas_call | solution.py:292
  58.8 14.9 %all_to_all.15 = f32[16,32,128]{2,1,0:T(8,128)S(1)} all-to-all(f32[16,32,128]{2,1,0:T(8,128)S(1)} %bitcast.9), channel_id=1, replica_groups=mesh['row'=8,'col'=16] {'col'}, dimensions={0} | all-to-all | bytes 524288 | tf_op jit(solution)/shard_map/all_to_all | solution.py:302
  73.7 0.7 copy.7
  (1 shorter events, 0.0 us)
Async XLA Ops:
  2.7 8.8 %copy-start = (bf16[64,8192]{1,0:T(8,128)(2,1)S(1)}, bf16[64,8192]{1,0:T(8,128)(2,1)}, u32[]{:S(2)}) copy-start(bf16[64,8192]{1,0:T(8,128)(2,1)} %cov_ref) | copy-start | bytes 3145732
  2.8 10.5 %copy-start.1 = (f32[64,128]{1,0:T(8,128)S(1)}, f32[64,128]{1,0:T(8,128)}, u32[]{:S(2)}) copy-start(f32[64,128]{1,0:T(8,128)} %get-tuple-element.24.side_ref) | copy-start | bytes 98308
  2.8 17.9 %all-to-all-start = ((f32[16,64,128]{2,1,0:T(8,128)}), f32[16,64,128]{2,1,0:T(8,128)S(1)}, u32[]{:S(2)}, u32[]{:S(2)}) async-start(f32[16,64,128]{2,1,0:T(8,128)} %get-tuple-element.18), calls=%async_computation | async-start | bytes 1048576 | tf_op jit(solution)/shard_map/all_to_all | solution.py:235
  11.7 3.3 %collective-permute-start = (f32[3,64,512]{2,1,0:T(8,128)S(1)}, f32[3,64,512]{2,1,0:T(8,128)S(1)}, u32[]{:S(2)}, u32[]{:S(2)}) collective-permute-start(f32[3,64,512]{2,1,0:T(8,128)S(1)} %get-tuple-element.21), channel_id=1, source_target_pairs={{0,1},{1,0},{2,3},{3,2},{4,5},{5,4},{6,7},{7,6},{8,9},{9,8},{10,11... | collective-permute-start | bytes 1179656 | tf_op jit(solution)/shard_map/ppermute | solution.py:251
  12.7 2.3 %collective-permute-start.1 = (f32[3,64,512]{2,1,0:T(8,128)S(1)}, f32[3,64,512]{2,1,0:T(8,128)S(1)}, u32[]{:S(2)}, u32[]{:S(2)}) collective-permute-start(f32[3,64,512]{2,1,0:T(8,128)S(1)} %get-tuple-element.22), channel_id=1, source_target_pairs={{0,1},{1,0},{2,3},{3,2},{4,5},{5,4},{6,7},{7,6},{8,9},{9,8},{10,11... | collective-permute-start | bytes 1179656 | tf_op jit(solution)/shard_map/ppermute | solution.py:251
  12.8 2.2 %collective-permute-start.2 = (f32[2,64,512]{2,1,0:T(8,128)S(1)}, f32[2,64,512]{2,1,0:T(8,128)S(1)}, u32[]{:S(2)}, u32[]{:S(2)}) collective-permute-start(f32[2,64,512]{2,1,0:T(8,128)S(1)} %get-tuple-element.23), channel_id=1, source_target_pairs={{0,1},{1,0},{2,3},{3,2},{4,5},{5,4},{6,7},{7,6},{8,9},{9,8},{10,11... | collective-permute-start | bytes 786440 | tf_op jit(solution)/shard_map/ppermute | solution.py:251
  13.2 5.9 %collective-permute-start.3 = (f32[64,128]{1,0:T(8,128)S(1)}, f32[64,128]{1,0:T(8,128)S(1)}, u32[]{:S(2)}, u32[]{:S(2)}) collective-permute-start(f32[64,128]{1,0:T(8,128)S(1)} %copy-done.1), channel_id=1, source_target_pairs={{0,16},{16,0},{32,48},{48,32},{64,80},{80,64},{96,112},{112,96},{1... | collective-permute-start | bytes 98312 | tf_op jit(solution)/shard_map/ppermute | solution.py:252
  20.7 7.1 %collective-permute-start.4 = (f32[6,64,128]{2,1,0:T(8,128)S(1)}, f32[6,64,128]{2,1,0:T(8,128)S(1)}, u32[]{:S(2)}, u32[]{:S(2)}) collective-permute-start(f32[6,64,128]{2,1,0:T(8,128)S(1)} %shard_map.62), channel_id=1, source_target_pairs={{0,96},{16,112},{32,64},{48,80},{64,32},{80,48},{96,0},{112,16},{1... | collective-permute-start | bytes 589832 | tf_op jit(solution)/shard_map/ppermute | solution.py:264
  23.3 30.3 %all-to-all-start.1 = ((f32[8,128,512]{2,1,0:T(8,128)}), f32[8,128,512]{2,1,0:T(8,128)S(1)}, u32[]{:S(2)}, u32[]{:S(2)}) async-start(f32[8,128,512]{2,1,0:T(8,128)} %shard_map.61), calls=%async_computation.1 | async-start | bytes 4194304 | tf_op jit(solution)/shard_map/all_to_all | solution.py:263
  27.9 5.9 %collective-permute-start.5 = (f32[576,128]{1,0:T(8,128)S(1)}, f32[576,128]{1,0:T(8,128)S(1)}, u32[]{:S(2)}, u32[]{:S(2)}) collective-permute-start(f32[576,128]{1,0:T(8,128)S(1)} %shard_map.63), channel_id=1, source_target_pairs={{0,32},{16,48},{32,0},{48,16},{64,96},{80,112},{96,64},{112,80},{1... | collective-permute-start | bytes 884744 | tf_op jit(solution)/shard_map/ppermute | solution.py:274
  28.0 11.4 %collective-permute-start.6 = (f32[576,128]{1,0:T(8,128)S(1)}, f32[576,128]{1,0:T(8,128)S(1)}, u32[]{:S(2)}, u32[]{:S(2)}) collective-permute-start(f32[576,128]{1,0:T(8,128)S(1)} %shard_map.63), channel_id=1, source_target_pairs={{0,64},{16,80},{32,96},{48,112},{64,0},{80,16},{96,32},{112,48},{1... | collective-permute-start | bytes 884744 | tf_op jit(solution)/shard_map/ppermute | solution.py:274
  30.3 14.3 %collective-permute-start.7 = (f32[576,128]{1,0:T(8,128)S(1)}, f32[576,128]{1,0:T(8,128)S(1)}, u32[]{:S(2)}, u32[]{:S(2)}) collective-permute-start(f32[576,128]{1,0:T(8,128)S(1)} %shard_map.63), channel_id=1, source_target_pairs={{0,96},{16,112},{32,64},{48,80},{64,32},{80,48},{96,0},{112,16},{1... | collective-permute-start | bytes 884744 | tf_op jit(solution)/shard_map/ppermute | solution.py:274
  44.7 5.2 %collective-permute-start.8 = (f32[4,576,128]{2,1,0:T(8,128)S(1)}, f32[4,576,128]{2,1,0:T(8,128)S(1)}, u32[]{:S(2)}, u32[]{:S(2)}) collective-permute-start(f32[4,576,128]{2,1,0:T(8,128)S(1)} %pad_maximum_fusion.own_ref), channel_id=1, source_target_pairs={{0,1},{1,0},{2,3},{3,2},{4,5},{5,4},{6,7},{7,6},{8,9},{9,8},{10,11... | collective-permute-start | bytes 3538952 | tf_op jit(solution)/shard_map/ppermute | solution.py:276
